TPU v7x, 32 devices: a whole 2x2x4 slice. The times are simulated.
32 devices in a mesh: dp: 16 (over z, y, core), mp: 2 (over x).
Axes of the slice: x: 2, y: 2, z: 4, core: 2. Of those that a mesh axis runs over, the one named last changes fastest.
Arguments:
- inputs: bfloat16 [128, 1152, 256], P('dp', 'mp'), may hold values from -6 to 6
- condition: bfloat16 [128, 1152], P('dp', 'mp'), may hold values from -6 to 6
- cotangent: bfloat16 [128, 1152, 256], P('dp', 'mp'), may hold values from -6 to 6
- kept_rows: int32 [128, 192], P('dp'), may hold values from 0 to 255, as said below
- kept_counts: int32 [128], P('dp'), may hold values from 64 to 192, as said below
- group_tokens: int32 [128], P('dp'), may hold values from 64 to 285, as said below
- w_qkv: bfloat16 [1152, 3, 1152], P('dp', None, 'mp'), may hold values from -0.1875 to 0.1875
- b_qv: bfloat16 [2, 1152], P(None, 'mp'), may hold values from -3 to 3
- w_out: bfloat16 [1152, 1152], P('mp', 'dp'), may hold values from -0.75 to 0.75
- b_out: bfloat16 [1152], P('mp'), may hold values from -3 to 3
- w_one: bfloat16 [1152, 4608], P('dp', 'mp'), may hold values from -0.1875 to 0.1875
- b_one: bfloat16 [4608], P('mp'), may hold values from -3 to 3
- w_two: bfloat16 [4608, 1152], P('mp', 'dp'), may hold values from -0.09375 to 0.09375
- b_two: bfloat16 [1152], P('mp'), may hold values from -3 to 3
- w_ada: bfloat16 [1152, 6, 1152], P('dp', None, 'mp'), may hold values from -0.1875 to 0.1875
- b_ada: bfloat16 [6, 1152], P(None, 'mp'), may hold values from -3 to 3
Outputs:
- output: bfloat16 [128, 1152, 256], P('dp', 'mp')
- input_grad: float32 [128, 1152, 256], P('dp', 'mp')
- cond_grad: float32 [128, 1152], P('dp', 'mp')
- grad_w_qkv: float32 [1152, 3, 1152], P('dp', None, 'mp')
- gradient_query_value_bias: float32 [2, 1152], P(None, 'mp')
- grad_w_out: float32 [1152, 1152], P('mp', 'dp')
- grad_b_out: float32 [1152], P('mp')
- grad_w_one: float32 [1152, 4608], P('dp', 'mp')
- grad_b_one: float32 [4608], P('mp')
- grad_w_two: float32 [4608, 1152], P('mp', 'dp')
- grad_b_two: float32 [1152], P('mp')
- gradient_adaptive_weight: float32 [1152, 6, 1152], P('dp', None, 'mp')
- grad_b_ada: float32 [6, 1152], P(None, 'mp')
Inputs may be any that keep to these rules, and one draw needn't show every extreme that they name: `kept_rows`: for latent l the first kept_counts[l] entries are the kept rows in increasing order; all entries of a latent are distinct. `kept_counts`: some latent keeps 192 tokens and some keeps 192 // 3. `group_tokens`: positive counts.
All inputs are finite; a program needn't handle non-finite values.
Results may differ from a plain program's by a relative error of at most 0.012.
The roundings to bfloat16 on the way count: a program that leaves them out, or rounds other values in their place, can miss the bound.
Values may be sent and summed in bfloat16 or wider, within the bound.
No kernel may reach another device: no remote copies, remote signals or barrier semaphores. Data moves between devices by JAX's collectives and lax.ppermute only.
A program may use at most 320 MiB of HBM per device.

v0:
```python
from functools import partial
import math

import jax
import jax.numpy as jnp
from jax import lax
from jax.sharding import PartitionSpec as P

HD = 72


EPS = 1e-06


def features(values):
    return lax.all_gather(values, "mp", axis=1, tiled=True)


def partials(values):
    return lax.psum_scatter(values, "mp", scatter_dimension=1, tiled=True)


def row_pair(first_term, second_term):
    return lax.psum((first_term, second_term), "mp")


def normalize(values, full_width):
    totals, squares = row_pair(jnp.sum(values, axis=1), jnp.sum(values * values, axis=1))
    center = totals / full_width
    spread = squares / full_width - center * center
    scaled = lax.rsqrt(spread + EPS)
    return ((values - center[:, None]) * scaled[:, None], scaled)


def norm_back(grad_normed, normed, scaled, full_width):
    first_mean, second_mean = row_pair(
        jnp.sum(grad_normed, axis=1), jnp.sum(grad_normed * normed, axis=1)
    )
    return (
        grad_normed
        - first_mean[:, None] / full_width
        - normed * (second_mean[:, None] / full_width)
    ) * scaled[:, None]


def pick_rows(source, places):
    return jax.vmap(lambda table_rows, slot_rows: table_rows[slot_rows])(source, places)


def put_rows(source, places, fresh_rows):
    return jax.vmap(lambda table_rows, slot_rows, new_rows: table_rows.at[slot_rows].set(new_rows))(
        source, places, fresh_rows
    )


def local(
    inputs,
    condition,
    cotangent,
    kept_rows,
    kept_counts,
    group_tokens,
    w_qkv,
    b_qv,
    w_out,
    b_out,
    w_one,
    b_one,
    w_two,
    b_two,
    w_ada,
    b_ada,
):
    token_rows = jnp.swapaxes(inputs, 1, 2)
    lat_dev, seq_len, own_width = token_rows.shape
    keep_slots = kept_rows.shape[1]
    full_width = own_width * lax.axis_size("mp")
    heads_dev = own_width // HD
    rows_dev = lat_dev * keep_slots
    inv_root = 1.0 / math.sqrt(HD)
    gelu_tanh = partial(jax.nn.gelu, approximate=True)

    def flatten(values):
        return values.reshape(rows_dev, -1)

    def cubes(values):
        return values.reshape(lat_dev, keep_slots, -1)

    token_total = lax.psum(jnp.sum(group_tokens.astype(jnp.float32)), "dp")
    row_scale = lat_dev * lax.axis_size("dp") * group_tokens.astype(jnp.float32) / token_total
    full_qkv, full_out, full_one, full_two, full_adaptive_output = (
        lax.all_gather(w_qkv, "dp", axis=0, tiled=True),
        lax.all_gather(w_out, "dp", axis=1, tiled=True),
        lax.all_gather(w_one, "dp", axis=0, tiled=True),
        lax.all_gather(w_two, "dp", axis=1, tiled=True),
        lax.all_gather(w_ada, "dp", axis=0, tiled=True),
    )
    cond_full = features(condition)
    silu_reduced_precision = jax.nn.silu(cond_full.astype(jnp.float32)).astype(jnp.bfloat16)
    modulation = jnp.einsum(
        "ro,olg->rlg",
        silu_reduced_precision,
        full_adaptive_output,
        preferred_element_type=jnp.float32,
    ) + b_ada.astype(jnp.float32)
    shift_one, scale_one, first_gate_value, shift_two, scale_two, gate_two = [
        modulation[:, position, None, :] for position in range(6)
    ]
    kept_slot = pick_rows(token_rows, kept_rows).astype(jnp.float32)
    is_valid = jnp.arange(keep_slots)[None, :] < kept_counts[:, None]
    normed_one, scaled_one = normalize(flatten(kept_slot), full_width)
    first_low = flatten((cubes(normed_one) * (1.0 + scale_one) + shift_one).astype(jnp.bfloat16))
    first_full = features(first_low)
    projected = jnp.dot(
        first_full, full_qkv.reshape(full_width, 3 * own_width), preferred_element_type=jnp.float32
    )
    projected = projected.reshape(lat_dev, keep_slots, 3, heads_dev, HD)
    b_float = b_qv.astype(jnp.float32).reshape(2, heads_dev, HD)
    queries = (projected[:, :, 0] + b_float[0]).astype(jnp.bfloat16)
    key_rows = projected[:, :, 1].astype(jnp.bfloat16)
    value_rows = (projected[:, :, 2] + b_float[1]).astype(jnp.bfloat16)

    def masked_scores():
        scores = (
            jnp.einsum("gqhe,gkhe->ghqk", queries, key_rows, preferred_element_type=jnp.float32)
            * inv_root
        )
        return jnp.where(is_valid[:, None, None, :], scores, -1e30)

    scores = masked_scores()
    upper_row_bound = jnp.max(scores, axis=-1, keepdims=True)
    exponent = jnp.exp(scores - upper_row_bound)
    denominator = jnp.sum(exponent, axis=-1, keepdims=True)
    probability = exponent / denominator
    log_total = upper_row_bound + jnp.log(denominator)
    mixture = jnp.einsum(
        "ghqk,gkhe->gqhe",
        probability.astype(jnp.bfloat16),
        value_rows,
        preferred_element_type=jnp.float32,
    )
    mixture_low = mixture.astype(jnp.bfloat16).reshape(rows_dev, own_width)
    attended = cubes(
        partials(jnp.dot(mixture_low, full_out, preferred_element_type=jnp.float32))
        + b_out.astype(jnp.float32)
    )
    residual = kept_slot + first_gate_value * attended
    normed_two, scaled_two = normalize(flatten(residual), full_width)
    second_low = flatten((cubes(normed_two) * (1.0 + scale_two) + shift_two).astype(jnp.bfloat16))
    second_full = features(second_low)
    hidden = jnp.dot(second_full, full_one, preferred_element_type=jnp.float32) + b_one.astype(
        jnp.float32
    )
    activated, gelu_back = jax.vjp(gelu_tanh, hidden)
    activated_low = activated.astype(jnp.bfloat16)
    branch = cubes(
        partials(jnp.dot(activated_low, full_two, preferred_element_type=jnp.float32))
        + b_two.astype(jnp.float32)
    )
    result = residual + gate_two * branch
    fresh_rows = jnp.where(is_valid[:, :, None], result, kept_slot).astype(jnp.bfloat16)
    output = jnp.swapaxes(put_rows(token_rows, kept_rows, fresh_rows), 1, 2)
    full_qkv, full_out, full_one, full_two, full_adaptive_output = (
        lax.all_gather(w_qkv, "dp", axis=0, tiled=True),
        lax.all_gather(w_out, "dp", axis=1, tiled=True),
        lax.all_gather(w_one, "dp", axis=0, tiled=True),
        lax.all_gather(w_two, "dp", axis=1, tiled=True),
        lax.all_gather(w_ada, "dp", axis=0, tiled=True),
    )
    cot_scaled = jnp.swapaxes(cotangent, 1, 2).astype(jnp.float32) * row_scale[:, None, None]
    cot_rows = pick_rows(cot_scaled, kept_rows)
    grad_result = jnp.where(is_valid[:, :, None], cot_rows, 0.0)
    grad_gate_two = jnp.sum(grad_result * branch, axis=1)
    grad_branch = flatten((gate_two * grad_result).astype(jnp.bfloat16))
    grad_b_two = jnp.sum(grad_branch.astype(jnp.float32), axis=0)
    grad_branch_full = features(grad_branch)
    grad_w_two = jnp.einsum(
        "rf,rd->fd", activated_low, grad_branch_full, preferred_element_type=jnp.float32
    )
    grad_act = jnp.einsum(
        "rd,fd->rf", grad_branch_full, full_two, preferred_element_type=jnp.float32
    )
    grad_hidden = gelu_back(grad_act)[0].astype(jnp.bfloat16)
    grad_b_one = jnp.sum(grad_hidden.astype(jnp.float32), axis=0)
    grad_w_one = jnp.einsum(
        "rd,rf->df", second_full, grad_hidden, preferred_element_type=jnp.float32
    )
    grad_second = cubes(
        partials(jnp.einsum("rf,df->rd", grad_hidden, full_one, preferred_element_type=jnp.float32))
    )
    grad_shift_two = jnp.sum(grad_second, axis=1)
    grad_scale_two = jnp.sum(grad_second * cubes(normed_two), axis=1)
    grad_residual = grad_result + cubes(
        norm_back(flatten(grad_second * (1.0 + scale_two)), normed_two, scaled_two, full_width)
    )
    grad_gate_one = jnp.sum(grad_residual * attended, axis=1)
    grad_attended = flatten((first_gate_value * grad_residual).astype(jnp.bfloat16))
    grad_b_out = jnp.sum(grad_attended.astype(jnp.float32), axis=0)
    grad_attended_full = features(grad_attended)
    grad_w_out = jnp.einsum(
        "rh,rd->hd", mixture_low, grad_attended_full, preferred_element_type=jnp.float32
    )
    grad_mixture = jnp.einsum(
        "rd,hd->rh", grad_attended_full, full_out, preferred_element_type=jnp.float32
    )
    grad_mixture = grad_mixture.astype(jnp.bfloat16).reshape(lat_dev, keep_slots, heads_dev, HD)
    repeat_probability = jnp.exp(masked_scores() - log_total)
    grad_values = jnp.einsum(
        "ghqk,gqhe->gkhe",
        repeat_probability.astype(jnp.bfloat16),
        grad_mixture,
        preferred_element_type=jnp.float32,
    )
    grad_prob = jnp.einsum(
        "gqhe,gkhe->ghqk", grad_mixture, value_rows, preferred_element_type=jnp.float32
    )
    row_delta = jnp.sum(grad_prob * repeat_probability, axis=-1, keepdims=True)
    grad_scores = (repeat_probability * (grad_prob - row_delta)).astype(jnp.bfloat16)
    grad_queries = (
        jnp.einsum("ghqk,gkhe->gqhe", grad_scores, key_rows, preferred_element_type=jnp.float32)
        * inv_root
    )
    grad_keys = (
        jnp.einsum("ghqk,gqhe->gkhe", grad_scores, queries, preferred_element_type=jnp.float32)
        * inv_root
    )
    grad_proj = jnp.stack([grad_queries, grad_keys, grad_values], axis=2).astype(jnp.bfloat16)
    grad_proj = grad_proj.reshape(rows_dev, 3 * own_width)
    grad_proj_float = grad_proj.astype(jnp.float32).reshape(rows_dev, 3, own_width)
    gradient_query_value_bias = jnp.stack(
        [jnp.sum(grad_proj_float[:, 0], axis=0), jnp.sum(grad_proj_float[:, 2], axis=0)], axis=0
    )
    grad_w_qkv = jnp.einsum(
        "rd,rc->dc", first_full, grad_proj, preferred_element_type=jnp.float32
    ).reshape(full_width, 3, own_width)
    grad_first = cubes(
        partials(
            jnp.einsum(
                "rc,dc->rd",
                grad_proj,
                full_qkv.reshape(full_width, 3 * own_width),
                preferred_element_type=jnp.float32,
            )
        )
    )
    grad_shift_one = jnp.sum(grad_first, axis=1)
    grad_scale_one = jnp.sum(grad_first * cubes(normed_one), axis=1)
    grad_kept = grad_residual + cubes(
        norm_back(flatten(grad_first * (1.0 + scale_one)), normed_one, scaled_one, full_width)
    )
    input_grad = jnp.swapaxes(
        put_rows(cot_scaled, kept_rows, jnp.where(is_valid[:, :, None], grad_kept, cot_rows)), 1, 2
    )
    modulation_gradient = jnp.stack(
        [
            grad_shift_one,
            grad_scale_one,
            grad_gate_one,
            grad_shift_two,
            grad_scale_two,
            grad_gate_two,
        ],
        axis=1,
    ).astype(jnp.bfloat16)
    grad_b_ada = jnp.sum(modulation_gradient.astype(jnp.float32), axis=0)
    gradient_adaptive_weight = jnp.einsum(
        "nb,nov->bov",
        silu_reduced_precision,
        modulation_gradient,
        preferred_element_type=jnp.float32,
    )
    grad_silu = partials(
        jnp.einsum(
            "jma,nma->jn",
            modulation_gradient,
            full_adaptive_output,
            preferred_element_type=jnp.float32,
        )
    )
    silu_value, silu_back = jax.vjp(jax.nn.silu, condition.astype(jnp.float32))
    cond_grad = silu_back(grad_silu)[0]
    summed_qkv, summed_out, summed_one, summed_two, summed_ada = (
        lax.psum_scatter(grad_w_qkv, "dp", scatter_dimension=0, tiled=True),
        lax.psum_scatter(grad_w_out, "dp", scatter_dimension=1, tiled=True),
        lax.psum_scatter(grad_w_one, "dp", scatter_dimension=0, tiled=True),
        lax.psum_scatter(grad_w_two, "dp", scatter_dimension=1, tiled=True),
        lax.psum_scatter(gradient_adaptive_weight, "dp", scatter_dimension=0, tiled=True),
    )
    bias_qv, bias_out, bias_one, bias_two, bias_ada = lax.psum(
        (gradient_query_value_bias, grad_b_out, grad_b_one, grad_b_two, grad_b_ada), "dp"
    )
    return (
        output,
        input_grad,
        cond_grad,
        summed_qkv,
        bias_qv,
        summed_out,
        bias_out,
        summed_one,
        bias_one,
        summed_two,
        bias_two,
        summed_ada,
        bias_ada,
    )


def solution(mesh):
    placed = (
        P("dp", "mp", None),
        P("dp", "mp"),
        P("dp", "mp", None),
        P("dp", None),
        P("dp"),
        P("dp"),
        P("dp", None, "mp"),
        P(None, "mp"),
        P("mp", "dp"),
        P("mp"),
        P("dp", "mp"),
        P("mp"),
        P("mp", "dp"),
        P("mp"),
        P("dp", None, "mp"),
        P(None, "mp"),
    )
    return jax.shard_map(
        local,
        mesh=mesh,
        in_specs=placed,
        out_specs=(
            P("dp", "mp", None),
            P("dp", "mp", None),
            P("dp", "mp"),
            P("dp", None, "mp"),
            P(None, "mp"),
            P("mp", "dp"),
            P("mp"),
            P("dp", "mp"),
            P("mp"),
            P("mp", "dp"),
            P("mp"),
            P("dp", None, "mp"),
            P(None, "mp"),
        ),
        check_vma=False,
    )
```

profile of v0, /device:TPU:0, one launch (start us, length us, event | category | flops | bytes accessed | tf_op | source)
XLA Modules:
  0.0 1632.0 jit_solution(2201142404431557612)
XLA Ops:
  17.4 19.2 %gather_fusion = bf16[1536,576]{1,0:T(8,128)(2,1)} fusion(bf16[8,256,576]{2,1,0:T(8,128)(2,1)S(1)} %bitcast.213, s32[1536]{0:T(1024)S(1)} %reshape.231), kind=kCustom, calls=%fused_computation | custom fusion | bytes 3551232 | tf_op jit(solution)/shard_map/vmap()/gather | solution.py:47
  56.3 34.5 %all-gather.11.cloned.1.call-done = bf16[1152,6,576]{2,0,1:T(8,128)(2,1)} async-done(((bf16[72,6,576]{2,0,1:T(8,128)(2,1)}), bf16[1152,6,576]{2,0,1:T(8,128)(2,1)}) %all-gather.11.cloned.1.call-update) | async-done | bytes 7962640 | tf_op jit(solution)/shard_map/all_gather | solution.py:96
  117.9 25.0 %all-gather.15.cloned.1.call-done = bf16[1152,3,576]{2,0,1:T(8,128)(2,1)} async-done(((bf16[72,3,576]{2,0,1:T(8,128)(2,1)}), bf16[1152,3,576]{2,0,1:T(8,128)(2,1)}) %all-gather.15.cloned.1.call-update) | async-done | bytes 3981328 | tf_op jit(solution)/shard_map/all_gather | solution.py:92
  149.5 43.4 %all-gather.13.cloned.1.call-done = bf16[1536,1152]{0,1:T(8,128)(2,1)} async-done(((bf16[1536,576]{0,1:T(8,128)(2,1)}), bf16[1536,1152]{0,1:T(8,128)(2,1)}) %all-gather.13.cloned.1.call-update) | async-done | bytes 3538960 | tf_op jit(solution)/shard_map/all_gather | solution.py:16
  198.7 15.1 fusion.60
  239.2 16.7 %fusion.66 = f32[1536,1152]{0,1:T(8,128)} fusion(bf16[576,1152]{0,1:T(8,128)(2,1)} %all-gather.17.cloned.1.call-done, bf16[1536,576]{0,1:T(8,128)(2,1)S(1)} %reshape.213), kind=kOutput, calls=%fused_computation.154 | convolution fusion | flops 2038431744 | bytes 10174464 | tf_op jit(solution)/shard_map/dot_general | solution.py:144
  257.2 33.8 %psum.102 = f32[]{:T(128)} all-reduce(f32[]{:T(128)} %convert_reduce_fusion.7), channel_id=1, replica_groups=mesh['dp'=16,'mp'=2] {'dp'}, use_global_device_ids=true, to_apply=%region_14.15 | all-reduce | flops 1 | bytes 8 | tf_op jit(solution)/shard_map/psum | solution.py:89
  301.8 27.6 %gather_fusion.1 = f32[1536,576]{1,0:T(8,128)} fusion(f32[8,256,576]{2,1,0:T(8,128)} %copy.215, s32[1536]{0:T(1024)S(1)} %reshape.231), kind=kCustom, calls=%fused_computation.1 | custom fusion | bytes 7090176 | tf_op jit(solution)/shard_map/vmap()/gather | solution.py:47
  400.3 50.2 %all-gather.25.cloned.1.call-done = bf16[1536,1152]{0,1:T(8,128)(2,1)} async-done(((bf16[1536,576]{0,1:T(8,128)(2,1)}), bf16[1536,1152]{0,1:T(8,128)(2,1)}) %all-gather.25.cloned.1.call-update) | async-done | bytes 3538960 | tf_op jit(solution)/shard_map/all_gather | solution.py:16
  450.5 15.6 fusion.61
  466.1 43.2 %all-gather.21.cloned.1.call-done = bf16[1152,2304]{1,0:T(8,128)(2,1)} async-done(((bf16[72,2304]{1,0:T(8,128)(2,1)}), bf16[1152,2304]{1,0:T(8,128)(2,1)}) %all-gather.21.cloned.1.call-update) | async-done | bytes 5308432 | tf_op jit(solution)/shard_map/all_gather | solution.py:94
  509.3 49.6 %all-gather.19.cloned.1.call-done = bf16[1536,1152]{0,1:T(8,128)(2,1)} async-done(((bf16[1536,576]{0,1:T(8,128)(2,1)}), bf16[1536,1152]{0,1:T(8,128)(2,1)}) %all-gather.19.cloned.1.call-update) | async-done | bytes 3538960 | tf_op jit(solution)/shard_map/all_gather | solution.py:16
  558.9 29.6 %convert_reduce_fusion = (f32[2304]{0:T(1024)}, bf16[1536,2304]{1,0:T(8,128)(2,1)}, f32[1536,2304]{1,0:T(8,128)}) fusion(f32[1536,2304]{1,0:T(8,128)} %fusion.61, f32[2304]{0:T(1024)} %convert_element_type.151, bf16[1536,1152]{0,1:T(8,128)(2,1)} %all-gather.19.cloned.1.call-done, bf16[1152,2304]{1,0:T(8,128)(2,1)} %all-gather.21.cloned.1.call-done), kind=kOutput, calls=%fused_computation.14 | convolution fusion | flops 8235120640 | bytes 44255232 | tf_op jit(solution)/shard_map/dot_general | solution.py:151
  601.5 85.7 %reduce-scatter.19.cloned.1.call-done = f32[1536,576]{0,1:T(8,128)} async-done(((f32[1536,1152]{0,1:T(8,128)}), f32[1536,576]{0,1:T(8,128)}) %reduce-scatter.19.cloned.1.call-update) | async-done | bytes 3538960 | tf_op jit(solution)/shard_map/reduce_scatter | solution.py:20
  710.9 15.3 fusion.55
  727.1 34.4 %all-gather.27.cloned.1.call-done = bf16[1536,1152]{0,1:T(8,128)(2,1)} async-done(((bf16[1536,576]{0,1:T(8,128)(2,1)}), bf16[1536,1152]{0,1:T(8,128)(2,1)}) %all-gather.27.cloned.1.call-update) | async-done | bytes 3538960 | tf_op jit(solution)/shard_map/all_gather | solution.py:16
  886.0 54.0 %reduce-scatter.21.cloned.1.call-done = f32[1536,576]{0,1:T(8,128)} async-done(((f32[1536,1152]{0,1:T(8,128)}), f32[1536,576]{0,1:T(8,128)}) %reduce-scatter.21.cloned.1.call-update) | async-done | bytes 3538960 | tf_op jit(solution)/shard_map/reduce_scatter | solution.py:20
  986.7 14.1 fusion.65
  1002.9 15.3 fusion.54
  1107.0 62.4 %all-reduce.1 = (f32[2,576]{1,0:T(2,128)}, f32[576]{0:T(1024)}, f32[2304]{0:T(1024)}, f32[576]{0:T(1024)}, f32[6,576]{1,0:T(8,128)}) all-reduce(f32[2,576]{1,0:T(2,128)S(1)} %pad_maximum_fusion.2, f32[576]{0:T(1024)S(1)} %copy-done.42, f32[2304]{0:T(1024)S(1)} %copy-done.45, ...), channel_id=1, replica_groups=mesh['dp'=16,'mp'=2] {'dp'}, use_global_device_ids=true, to_apply=%region_37.38 | all-reduce | flops 8064 | bytes 64512 | tf_op jit(solution)/shard_map/psum | solution.py:289
  1171.1 82.7 %reduce-scatter.27.cloned.1.call-done = f32[2304,72]{0,1:T(8,128)} async-done(((f32[2304,1152]{0,1:T(8,128)}), f32[2304,72]{0,1:T(8,128)}) %reduce-scatter.27.cloned.1.call-update) | async-done | bytes 663568 | tf_op jit(solution)/shard_map/reduce_scatter | solution.py:286
  1253.8 69.9 %reduce-scatter.33.cloned.1.call-done = f32[576,72]{0,1:T(8,128)} async-done(((f32[576,1152]{0,1:T(8,128)}), f32[576,72]{0,1:T(8,128)}) %reduce-scatter.33.cloned.1.call-update) | async-done | bytes 165904
  1323.7 111.2 %reduce-scatter.23.cloned.1.call-done = f32[72,3,576]{2,0,1:T(8,128)} async-done(((f32[1152,3,576]{2,0,1:T(8,128)}), f32[72,3,576]{2,0,1:T(8,128)}) %reduce-scatter.23.cloned.1.call-update) | async-done | bytes 497680 | tf_op jit(solution)/shard_map/reduce_scatter | solution.py:283
  1434.8 190.2 %reduce-scatter.29.cloned.1.call-done = f32[72,6,576]{2,0,1:T(8,128)} async-done(((f32[1152,6,576]{2,0,1:T(8,128)}), f32[72,6,576]{2,0,1:T(8,128)}) %reduce-scatter.29.cloned.1.call-update) | async-done | bytes 995344 | tf_op jit(solution)/shard_map/reduce_scatter | solution.py:287
  (291 shorter events, 478.5 us)
Async XLA Ops:
  7.2 83.5 %all-gather.11.cloned.1.call-start = ((), (), s32[]{:S(2)}) async-start(), calls=%async_computation.10 | async-start | bytes 9400320 | tf_op jit(solution)/shard_map/all_gather | solution.py:96
  7.9 135.0 %all-gather.15.cloned.1.call-start = ((), (), s32[]{:S(2)}) async-start(), calls=%async_computation.12 | async-start | bytes 4700160 | tf_op jit(solution)/shard_map/all_gather | solution.py:92
  8.7 184.3 %all-gather.13.cloned.1.call-start = ((), (), s32[]{:S(2)}) async-start(), calls=%async_computation.11 | async-start | bytes 5308416 | tf_op jit(solution)/shard_map/all_gather | solution.py:16
  17.4 73.4 %copy-start.19 = (f32[1152,8]{0,1:T(8,128)}, f32[1152,8]{0,1:T(8,128)S(1)}, u32[]{:S(2)}) copy-start(f32[1152,8]{0,1:T(8,128)S(1)} %reshape.262) | copy-start | bytes 110596
  116.7 122.5 %all-gather.17.cloned.1.call-start = ((), (), s32[]{:S(2)}) async-start(), calls=%async_computation.13 | async-start | bytes 1566720 | tf_op jit(solution)/shard_map/all_gather | solution.py:93
  117.2 253.6 %reduce-scatter.15.cloned.1.call-start = ((), (), s32[]{:S(2)}) async-start(), calls=%async_computation.14 | async-start | bytes 10616832 | tf_op jit(solution)/shard_map/reduce_scatter | solution.py:20
  117.8 695.0 %copy-start.29 = (pred[8,192]{1,0:T(8,128)(4,1)}, pred[8,192]{1,0:T(8,128)(4,1)S(1)}, u32[]{:S(2)}) copy-start(pred[8,192]{1,0:T(8,128)(4,1)S(1)} %iota_compare_fusion) | copy-start | bytes 4612
  117.9 95.9 %copy-start.37 = (f32[8,72]{1,0:T(8,128)}, f32[8,72]{1,0:T(8,128)S(1)}, u32[]{:S(2)}) copy-start(f32[8,72]{1,0:T(8,128)S(1)} %add.200) | copy-start | bytes 6916
  117.9 105.7 %copy-start.43 = (f32[8,72]{1,0:T(8,128)}, f32[8,72]{1,0:T(8,128)S(1)}, u32[]{:S(2)}) copy-start(f32[8,72]{1,0:T(8,128)S(1)} %add.197) | copy-start | bytes 6916
  255.9 144.4 %all-gather.23.cloned.1.call-start = ((), (), s32[]{:S(2)}) async-start(), calls=%async_computation.17 | async-start | bytes 5640192 | tf_op jit(solution)/shard_map/all_gather | solution.py:95
  256.5 194.0 %all-gather.25.cloned.1.call-start = ((), (), s32[]{:S(2)}) async-start(), calls=%async_computation.19 | async-start | bytes 5308416 | tf_op jit(solution)/shard_map/all_gather | solution.py:16
  347.3 162.0 %all-gather.21.cloned.1.call-start = ((), (), s32[]{:S(2)}) async-start(), calls=%async_computation.16 | async-start | bytes 5640192 | tf_op jit(solution)/shard_map/all_gather | solution.py:94
  348.1 210.8 %all-gather.19.cloned.1.call-start = ((), (), s32[]{:S(2)}) async-start(), calls=%async_computation.15 | async-start | bytes 5308416 | tf_op jit(solution)/shard_map/all_gather | solution.py:16
  392.6 310.1 %copy-start.6 = (f32[1536,576]{0,1:T(8,128)}, f32[1536,576]{0,1:T(8,128)S(1)}, u32[]{:S(2)}) copy-start(f32[1536,576]{0,1:T(8,128)S(1)} %get-tuple-element.103) | copy-start | bytes 10616836
  392.7 294.5 %reduce-scatter.19.cloned.1.call-start = ((), (), s32[]{:S(2)}) async-start(), calls=%async_computation.20 | async-start | bytes 10616832 | tf_op jit(solution)/shard_map/reduce_scatter | solution.py:20
  601.4 160.1 %all-gather.27.cloned.1.call-start = ((), (), s32[]{:S(2)}) async-start(), calls=%async_computation.21 | async-start | bytes 5308416 | tf_op jit(solution)/shard_map/all_gather | solution.py:16
  710.9 155.7 %reduce-scatter.17.cloned.1.call-start = ((), (), s32[]{:S(2)}) async-start(), calls=%async_computation.18 | async-start | bytes 10616832 | tf_op jit(solution)/shard_map/reduce_scatter | solution.py:20
  726.3 213.7 %reduce-scatter.21.cloned.1.call-start = ((), (), s32[]{:S(2)}) async-start(), calls=%async_computation.22 | async-start | bytes 10616832 | tf_op jit(solution)/shard_map/reduce_scatter | solution.py:20
  854.2 315.2 %reduce-scatter.31.cloned.1.call-start = ((), (), s32[]{:S(2)}) async-start(), calls=%async_computation.27 | async-start | bytes 884736
  986.7 184.4 %reduce-scatter.25.cloned.1.call-start = ((), (), s32[]{:S(2)}) async-start(), calls=%async_computation.24 | async-start | bytes 11280384 | tf_op jit(solution)/shard_map/reduce_scatter | solution.py:285
  1000.9 252.9 %reduce-scatter.27.cloned.1.call-start = ((), (), s32[]{:S(2)}) async-start(), calls=%async_computation.25 | async-start | bytes 11280384 | tf_op jit(solution)/shard_map/reduce_scatter | solution.py:286
  1018.2 305.4 %reduce-scatter.33.cloned.1.call-start = ((), (), s32[]{:S(2)}) async-start(), calls=%async_computation.28 | async-start | bytes 3133440
  1026.1 408.7 %reduce-scatter.23.cloned.1.call-start = ((), (), s32[]{:S(2)}) async-start(), calls=%async_computation.23 | async-start | bytes 9400320 | tf_op jit(solution)/shard_map/reduce_scatter | solution.py:283
  1039.5 585.6 %reduce-scatter.29.cloned.1.call-start = ((), (), s32[]{:S(2)}) async-start(), calls=%async_computation.26 | async-start | bytes 18800640 | tf_op jit(solution)/shard_map/reduce_scatter | solution.py:287
  (56 other events, 627.2 us)
Sparse Core Ops, SparseCore 0:
  10.2 80.4 all-gather.10
  92.9 49.9 all-gather.14
  145.1 47.8 all-gather.12
  195.0 39.3 all-gather.16
  256.0 85.5 reduce-scatter.14
  343.9 56.3 all-gather.22
  402.5 47.9 all-gather.24
  452.9 56.3 all-gather.20
  510.9 47.9 all-gather.18
  601.6 85.5 reduce-scatter.18
  711.0 50.4 all-gather.26
  763.7 85.5 reduce-scatter.16
  854.3 85.6 reduce-scatter.20
  986.8 16.4 reduce-scatter.30
  1008.2 120.4 reduce-scatter.24
  1133.8 119.9 reduce-scatter.26
  1258.6 64.9 reduce-scatter.32
  1328.8 105.9 reduce-scatter.22
  1439.6 185.4 reduce-scatter.28
where the time goes:
time: 1640 us; the launch traced here: 1630 us
  waiting for transfers between devices  883 us (54%)
  local copies, waits for them, and re-layouts  251 us (15%)
  matrix products  240 us (15%)
  blocking collectives  132 us (8%)
  other arithmetic  110 us (7%)
    reduce_scatter x1, waiting for transfers between devices, local(): lax.psum_scatter(gradient_adaptive_weight, 'dp', scatter_dimension=0, til...  190 us
    all_gather x4, waiting for transfers between devices, features(): return lax.all_gather(values, 'mp', axis=1, tiled=True)  178 us
    reduce_scatter x4, waiting for transfers between devices, partials(): return lax.psum_scatter(values, 'mp', scatter_dimension=1, tiled=True)  140 us
    reduce_scatter x1, waiting for transfers between devices, local(): lax.psum_scatter(grad_w_qkv, 'dp', scatter_dimension=0, tiled=True)  111 us
    reduce_scatter x1, waiting for transfers between devices, local(): lax.psum_scatter(grad_w_two, 'dp', scatter_dimension=1, tiled=True)  82.7 us
    unnamed x21, waiting for transfers between devices  73.2 us
    psum x1, blocking collectives, local(): lax.psum((gradient_query_value_bias, grad_b_out, grad_b_one, grad_b_two,...  62.4 us
    gather x4, local copies, waits for them, and re-layouts, pick_rows(): table_rows[slot_rows]  56 us
  transfers between devices with their start and end apart: 19, of which 14 were waited for; matrix products, arithmetic and copies ran while one was open for 29% of the time, Pallas kernels for 0%

commit v1 on v0

v1 whole, which is shorter than its diff:
```python
from functools import partial
import math

import jax
import jax.numpy as jnp
from jax import lax
from jax.experimental import pallas as pl
from jax.experimental.pallas import tpu as pltpu
from jax.sharding import PartitionSpec as P

HD = 72
EPS = 1e-06
BF = jnp.bfloat16
F32 = jnp.float32
NN = ((1,), (0,))
NT = ((1,), (1,))
TN = ((0,), (0,))


def dot(left, right, dims, kind=F32):
    return lax.dot_general(left, right, (dims, ((), ())), preferred_element_type=kind)


def exact_dot(left, right, dims):
    return lax.dot_general(
        left,
        right,
        (dims, ((), ())),
        precision=lax.Precision.HIGHEST,
        preferred_element_type=F32,
    )


class Steps:
    def __init__(self):
        self.seen = ()

    def __call__(self, *values):
        out = lax.optimization_barrier((*values, *self.seen))[: len(values)]
        self.seen = out
        return out[0] if len(values) == 1 else out


def attend_kernel(heads, counts, qkv_ref, out_ref):
    count = counts[pl.program_id(0)]
    keep, own = out_ref.shape
    inv_root = 1.0 / math.sqrt(HD)
    valid = lax.broadcasted_iota(jnp.int32, (keep, keep), 1) < count
    for h in range(heads):
        a = HD * h
        q, k = qkv_ref[:, a : a + HD], qkv_ref[:, own + a : own + a + HD]
        v = qkv_ref[:, 2 * own + a : 2 * own + a + HD]
        scores = jnp.where(valid, dot(q, k, NT) * inv_root, -1e30)
        power = jnp.exp(scores - jnp.max(scores, axis=1, keepdims=True))
        probability = power / jnp.sum(power, axis=1, keepdims=True)
        out_ref[:, a : a + HD] = dot(probability.astype(BF), v, NN).astype(BF)


def attend_back_kernel(heads, counts, qkv_ref, g_ref, out_ref):
    count = counts[pl.program_id(0)]
    keep, own = g_ref.shape
    inv_root = 1.0 / math.sqrt(HD)
    valid = lax.broadcasted_iota(jnp.int32, (keep, keep), 0) < count
    for h in range(heads):
        a = HD * h
        q, k = qkv_ref[:, a : a + HD], qkv_ref[:, own + a : own + a + HD]
        v, g = qkv_ref[:, 2 * own + a : 2 * own + a + HD], g_ref[:, a : a + HD]
        scores = jnp.where(valid, dot(k, q, NT) * inv_root, -1e30)
        power = jnp.exp(scores - jnp.max(scores, axis=0, keepdims=True))
        probability = power / jnp.sum(power, axis=0, keepdims=True)
        grad_prob = dot(v, g, NT)
        delta = jnp.sum(grad_prob * probability, axis=0, keepdims=True)
        grad_scores = (probability * (grad_prob - delta)).astype(BF)
        out_ref[:, a : a + HD] = (dot(grad_scores, k, TN) * inv_root).astype(BF)
        out_ref[:, own + a : own + a + HD] = (dot(grad_scores, q, NN) * inv_root).astype(BF)
        out_ref[:, 2 * own + a : 2 * own + a + HD] = dot(probability.astype(BF), g, NN).astype(
            BF
        )


def attend(counts, qkv, keep):
    rows, own = qkv.shape[0], qkv.shape[1] // 3

    def block(n):
        return pl.BlockSpec((keep, n), lambda i, c: (i, 0))

    return pl.pallas_call(
        partial(attend_kernel, own // HD),
        out_shape=jax.ShapeDtypeStruct((rows, own), BF),
        grid_spec=pltpu.PrefetchScalarGridSpec(
            num_scalar_prefetch=1,
            grid=(rows // keep,),
            in_specs=[block(3 * own)],
            out_specs=block(own),
        ),
        compiler_params=pltpu.CompilerParams(vmem_limit_bytes=40 * 2**20),
    )(counts, qkv)


def attend_back(counts, qkv, g, keep):
    rows, own = g.shape

    def block(n):
        return pl.BlockSpec((keep, n), lambda i, c: (i, 0))

    return pl.pallas_call(
        partial(attend_back_kernel, own // HD),
        out_shape=jax.ShapeDtypeStruct((rows, 3 * own), BF),
        grid_spec=pltpu.PrefetchScalarGridSpec(
            num_scalar_prefetch=1,
            grid=(rows // keep,),
            in_specs=[block(3 * own), block(own)],
            out_specs=block(3 * own),
        ),
        compiler_params=pltpu.CompilerParams(vmem_limit_bytes=40 * 2**20),
    )(counts, qkv, g)


def local(
    inputs,
    condition,
    cotangent,
    kept_rows,
    kept_counts,
    group_tokens,
    w_qkv,
    b_qv,
    w_out,
    b_out,
    w_one,
    b_one,
    w_two,
    b_two,
    w_ada,
    b_ada,
):
    nd, nm = lax.axis_size("dp"), lax.axis_size("mp")
    d, m = lax.axis_index("dp"), lax.axis_index("mp")
    lat_dev, own, seq = inputs.shape
    keep = kept_rows.shape[1]
    full = own * nm
    blk, nb = full // nd, nd // nm
    mine = lat_dev // nm
    rows = mine * keep
    ff = w_one.shape[1]
    half = full // 2
    far_bits = [b for b in reversed(range(2, nd.bit_length() - 1))]
    bits = far_bits + [1, 0]
    zb = 2 ** len(far_bits)
    shifts = range(nm)

    def over_dp(v, bit):
        return lax.ppermute(v, "dp", [(i, i ^ (1 << bit)) for i in range(nd)])

    def over_mp(v, s):
        return v if s == 0 else lax.ppermute(v, "mp", [(i, i ^ s) for i in range(nm)])

    def rel(place):
        out = jnp.zeros_like(place)
        for k, bit in enumerate(bits):
            out = out | (((place >> k) & 1) << bit)
        return out

    def block_of(place):
        near = place // zb
        return ((place % zb) << 2) | ((d & 3) ^ (((near & 1) << 1) | (near >> 1)))

    def spread(s, kind):
        place = lax.broadcasted_iota(jnp.int32, (own, full), 1)
        feature = lax.broadcasted_iota(jnp.int32, (own, full), 0)
        source = block_of(place // blk)
        wanted = (m ^ s) * nb + feature // blk
        return ((source == wanted) & (place % blk == feature % blk)).astype(kind)

    spreads = [spread(s, BF) for s in shifts]
    place_hot = (
        (d ^ rel(lax.broadcasted_iota(jnp.int32, (nd, nd), 0)))
        == lax.broadcasted_iota(jnp.int32, (nd, nd), 1)
    )
    far_groups = [[low + 4 * k for k in range(zb)] for low in range(4)]
    step = Steps()

    def group_of(v, s):
        return lax.dynamic_slice_in_dim(v, (m ^ s) * mine, mine, 0)

    def regroup(parts):
        stacked = jnp.stack(parts)
        return jnp.concatenate(
            [lax.dynamic_index_in_dim(stacked, m ^ g, 0, keepdims=False) for g in shifts]
        )

    def send_rows(v):
        return [over_mp(group_of(v, s), s).reshape(rows, own) for s in shifts]

    def to_rows(got):
        return sum(dot(g, p, NN) for g, p in zip(got, spreads))

    def from_rows(v):
        parts = [dot(v, p, NT, BF).reshape(mine, keep, own) for p in spreads]
        return [over_mp(part, s) for s, part in enumerate(parts)]

    def far_gather(v):
        return lax.all_gather(v, "dp", axis=0, tiled=True, axis_index_groups=far_groups)

    cond_halves = [over_mp(condition, s) for s in shifts]
    bias_vec = jnp.concatenate([b_qv.reshape(-1), b_one, b_out, b_two])
    bias_all = [over_mp(bias_vec, s) for s in shifts]
    w_a = jnp.concatenate([w_qkv.reshape(blk, 3 * own), w_out.T], axis=1)
    a_z = far_gather(w_a)
    one_z = far_gather(w_one)
    digits = jnp.stack([(group_tokens >> (8 * k)) & 255 for k in range(4)], axis=1)
    pad = -(blk + 4) % 8
    valid = jnp.arange(keep)[None, :] < kept_counts[:, None]
    hot = (
        (kept_rows[:, :, None] == jnp.arange(seq)[None, None, :]) & valid[:, :, None]
    ).astype(BF)

    def pick(source):
        return lax.dot_general(
            hot, source, (((2,), (2,)), ((0,), (0,))), preferred_element_type=BF
        )

    w_a = step(w_a)
    picked = pick(step(inputs))
    picked = step(picked)
    kept_got = send_rows(picked)
    cond_halves = [cond_halves[0], *[step(v) for v in cond_halves[1:]]]
    cond_halves = jnp.stack(cond_halves)
    cond_full = jnp.concatenate(
        [lax.dynamic_index_in_dim(cond_halves, m ^ g, 0, keepdims=False) for g in shifts], axis=1
    )
    cond_send = jnp.concatenate(
        [
            jnp.swapaxes(cond_full.reshape(lat_dev, nd, blk), 0, 1),
            jnp.broadcast_to(digits.astype(BF)[None], (nd, lat_dev, 4)),
            jnp.zeros((nd, lat_dev, pad), BF),
        ],
        axis=2,
    )
    cond_got = lax.all_to_all(cond_send, "dp", 0, 0)
    w_two_t = w_two.T
    w_ada_flat = w_ada.reshape(blk, 6 * own)
    two_z = far_gather(w_two_t)
    w_two_t, w_ada_flat, cond_got = step(w_two_t, w_ada_flat, cond_got)
    cond_got = dot(place_hot.astype(BF), cond_got.reshape(nd, -1), NN).reshape(
        nd, lat_dev, blk + 4 + pad
    )
    token_total = sum(
        jnp.sum(cond_got[:, :, blk + k]) * float(256**k) for k in range(4)
    )
    silu_low = jax.nn.silu(cond_got[:, :, :blk].reshape(nd * lat_dev, blk)).astype(BF)
    part = dot(silu_low, w_ada_flat, NN).reshape(nd, lat_dev, 6 * own)
    part = step(part)

    def part_send(part, bit):
        return over_dp(part[part.shape[0] // 2 :], bit)

    def part_add(part, got):
        return part[: part.shape[0] // 2] + got

    got = part_send(part, 0)
    part = part_add(part, step(got))
    got = part_send(part, 1)

    def core_pair(v):
        return (v, over_dp(v, 0))

    def near_join(a, b):
        return jnp.concatenate([a, b], 0)

    def join(pair, start, stop):
        return jnp.concatenate([v[:, :, start:stop] for v in pair], 0).reshape(full, stop - start)

    def later(vs):
        return [vs[0], *[step(v) for v in vs[1:]]]

    a_z = step(a_z).reshape(zb, blk, 4 * own)
    a_xs = [over_mp(a_z, s) for s in shifts]
    a_y = over_dp(a_z, 1)
    kept_got = later(kept_got)
    kept_slot = step(to_rows(kept_got)).reshape(mine, keep, full)
    part = part_add(part, step(got))
    for bit in reversed(far_bits):
        got = part_send(part, bit)
        part = part_add(part, step(got))
    modulation = part.reshape(lat_dev, 6, own) + b_ada.astype(F32)
    modulation = step(modulation)
    mod_got = [over_mp(group_of(modulation, s), s).reshape(mine * 6, own) for s in shifts]
    a_xs = later(a_xs)
    a_y = step(a_y)
    a_xys = [over_mp(a_y, s) for s in shifts]
    one_z = step(one_z).reshape(zb, blk, ff)
    one_y = over_dp(one_z, 1)
    a_pairs = {0: core_pair(step(near_join(a_z, a_y)))}
    mod_got = later(mod_got)
    mod_rows = sum(
        exact_dot(v, p.astype(F32), NN) for v, p in zip(mod_got, spreads)
    ).reshape(mine, 6, full)
    shift_one, scale_one, gate_one, shift_two, scale_two, gate_two = [
        mod_rows[:, k, None, :] for k in range(6)
    ]
    bias_qv = [v[: 2 * own].reshape(2, own).astype(F32) for v in bias_all]
    bias_one = [v[2 * own : 2 * own + ff].astype(F32) for v in bias_all]
    bias_wide = sum(
        dot(v[2 * own + ff :].reshape(2, own), p, NN) for v, p in zip(bias_all, spreads)
    )
    row_scale = lat_dev * nd * group_tokens.astype(F32) / token_total
    own_scale = group_of(row_scale, 0)[:, None, None]
    own_counts = group_of(kept_counts, 0)

    def cubes(v):
        return v.reshape(mine, keep, -1)

    def flat(v):
        return v.reshape(rows, -1)

    def column_sums(v):
        return dot(jnp.ones((8, rows), BF), v, NN)[0]

    def normalize(v):
        center = jnp.mean(v, axis=-1, keepdims=True)
        var = jnp.mean(v * v, axis=-1, keepdims=True) - center * center
        scaled = lax.rsqrt(var + EPS)
        return (v - center) * scaled, scaled

    def norm_back(g, normed, scaled):
        a = jnp.mean(g, axis=-1, keepdims=True)
        b = jnp.mean(g * normed, axis=-1, keepdims=True)
        return (g - a - normed * b) * scaled

    normed_one, scaled_one = normalize(kept_slot)
    first_low = flat((normed_one * (1.0 + scale_one) + shift_one).astype(BF))
    first_low = step(first_low)
    w_qkvs, wo_t, qkvs, mixtures = [], [], [], []
    attended = bias_wide[0]
    for s in shifts:
        pair = (a_pairs[s][0], step(a_pairs[s][1]))
        w_qkvs.append(join(pair, 0, 3 * own))
        wo_t.append(join(pair, 3 * own, 4 * own))
        bias = jnp.concatenate([bias_qv[s][0], jnp.zeros((own,), F32), bias_qv[s][1]])
        qkv = step((dot(first_low, w_qkvs[s], NN) + bias).astype(BF))
        qkvs.append(qkv)
        mixture = step(attend(own_counts, qkv, keep))
        mixtures.append(mixture)
        attended = step(attended + dot(mixture, wo_t[s], NT))
        if s == 0:
            a_xys = later(a_xys)
            one_y = step(one_y)
            one_xs = [over_mp(one_z, t) for t in shifts]
            two_z = step(two_z).reshape(zb, blk, ff)
            two_y = over_dp(two_z, 1)
            for t in shifts[1:]:
                a_pairs[t] = core_pair(step(near_join(a_xs[t], a_xys[t])))
            g_one = {0: core_pair(step(near_join(one_z, one_y)))}
    one_xs = later(one_xs)
    two_y = step(two_y)
    two_xs = [over_mp(two_z, s) for s in shifts]
    one_xys = [one_y, *[over_dp(v, 1) for v in one_xs[1:]]]
    g_two = {0: core_pair(step(near_join(two_z, two_y)))}
    attended = cubes(attended)
    residual = kept_slot + gate_one * attended
    normed_two, scaled_two = normalize(residual)
    second_low = flat((normed_two * (1.0 + scale_two) + shift_two).astype(BF))
    second_low = step(second_low)
    branch = bias_wide[1]
    w1, w2t, acts, slopes = [], [], [], []
    root = math.sqrt(2.0 / math.pi)
    for s in shifts:
        w1.append(join((g_one[s][0], step(g_one[s][1])), 0, ff))
        hidden = dot(second_low, w1[s], NN) + bias_one[s]
        square = hidden * hidden
        bend = jnp.tanh(root * hidden * (1.0 + 0.044715 * square))
        act = (0.5 * hidden * (1.0 + bend)).astype(BF)
        slope = 0.5 * (1.0 + bend) + 0.5 * root * hidden * (1.0 - bend * bend) * (
            1.0 + 3.0 * 0.044715 * square
        )
        act, slope = step(act, slope)
        acts.append(act)
        slopes.append(slope)
        if s == 0:
            two_xs = later(two_xs)
            one_xys = later(one_xys)
            two_xys = [over_mp(two_y, t) for t in shifts]
            for t in shifts[1:]:
                g_one[t] = core_pair(step(near_join(one_xs[t], one_xys[t])))
            mixture_all = jnp.concatenate(mixtures, axis=1)
            cot_picked = step(pick(cotangent))
        if s:
            for t in shifts[1:]:
                two_xys[t] = step(two_xys[t]) if s == 1 else two_xys[t]
            if s == 1:
                cot_got = send_rows(cot_picked)
            g_two[s] = core_pair(step(near_join(two_xs[s], two_xys[s])))
        w2t.append(join((g_two[s][0], step(g_two[s][1])), 0, ff))
        branch = step(branch + dot(act, w2t[s], NT))
    branch = cubes(branch)
    result = residual + gate_two * branch
    cot_got = later(cot_got)
    fresh_got = from_rows(flat(result).astype(BF))

    def add(a, b):
        return (a.astype(F32) + b.astype(F32)).astype(BF)

    def keep_sum(low_side, v, got):
        kept = (dot(low_side, v, TN) + got.astype(F32)).astype(BF)
        return kept.reshape(2 * zb, blk, -1)

    def y_send(v):
        return over_dp(v[zb:], 1)

    def y_add(v, got):
        return add(v[:zb], got)

    def x_send(vs):
        return {s: over_mp(v, s) for s, v in vs.items() if s}

    def x_add(vs, got):
        total = vs[0].astype(F32)
        for v in got:
            total = total + v.astype(F32)
        return total.astype(BF)

    cot_rows = to_rows(cot_got).reshape(mine, keep, full)
    grad_result = cot_rows * own_scale
    grad_branch = flat((gate_two * grad_result).astype(BF))
    order = list(reversed(shifts))

    def far_scatter(v):
        v = v.reshape(zb * blk, -1)
        v = lax.psum_scatter(
            v, "dp", scatter_dimension=0, tiled=True, axis_index_groups=far_groups
        )
        return v.astype(F32)

    low, high, grad_branch = step(grad_branch[:, :half], grad_branch[:, half:], grad_branch)
    two_sent, two_got, two_kept, two_y_got, two_y, two_x_got = {}, {}, {}, {}, {}, {}
    grad_hiddens = [None] * nm
    for s in order:
        two_sent[s] = step(dot(high, acts[s], TN, BF))
        two_got[s] = over_dp(two_sent[s], 0)
    for s in order:
        grad_hiddens[s] = step((dot(step(grad_branch), w2t[s], NN) * slopes[s]).astype(BF))
        two_kept[s] = step(keep_sum(low, acts[s], step(two_got[s])))
        two_y_got[s] = y_send(two_kept[s])
    low, high = step(second_low[:, :half], second_low[:, half:])
    one_sent, one_got, one_kept = {}, {}, {}
    for s in order:
        one_sent[s] = step(dot(high, grad_hiddens[s], TN, BF))
        one_got[s] = over_dp(one_sent[s], 0)
    fresh_got = later(fresh_got)
    last = order[0]
    grad_second = step(
        sum(dot(v, w, NT) for v, w in zip(lax.optimization_barrier(grad_hiddens), w1))
    )
    one_x_got = {}
    for s in order:
        one_kept[s] = step(keep_sum(low, grad_hiddens[s], step(one_got[s])))
        if s:
            one_x_got[s] = (over_mp(one_kept[s][zb:], s), over_mp(one_kept[s][:zb], s))
    grad_second = cubes(step(grad_second))
    grad_shift_two = jnp.sum(grad_second, axis=1)
    grad_scale_two = jnp.sum(grad_second * normed_two, axis=1)
    grad_residual = grad_result + norm_back(
        grad_second * (1.0 + scale_two), normed_two, scaled_two
    )
    grad_attended = flat((gate_one * grad_residual).astype(BF))
    low, high, grad_attended = step(
        grad_attended[:, :half], grad_attended[:, half:], grad_attended
    )
    out_sent = step(dot(high, mixture_all, TN, BF))
    out_got = over_dp(out_sent, 0)
    grad_mixtures = step(*[dot(step(grad_attended), w, NN, BF) for w in wo_t])
    out_kept = step(keep_sum(low, mixture_all, step(out_got)))
    for s in order:
        two_y[s] = step(y_add(two_kept[s], step(two_y_got[s])))
    one_high = step(x_add([one_kept[0][zb:]], [step(v[0]) for v in one_x_got.values()]))
    one_y_got = over_dp(one_high, 1)
    two_x_got = x_send(two_y)
    grad_qkvs = [None] * nm
    first_half, second_half = step(first_low[:, :half], first_low[:, half:])
    qkv_sent, qkv_got, qkv_kept, qkv_y_got, qkv_y = {}, {}, {}, {}, {}
    for s in order:
        grad_qkvs[s] = step(attend_back(step(own_counts), qkvs[s], grad_mixtures[s], keep))
        if s == last:
            out_y_got = y_send(out_kept)
        qkv_sent[s] = step(dot(second_half, grad_qkvs[s], TN, BF))
        qkv_got[s] = over_dp(qkv_sent[s], 0)
    one_low = step(x_add([one_kept[0][:zb]], [step(v[1]) for v in one_x_got.values()]))
    for s in order:
        qkv_kept[s] = step(keep_sum(first_half, grad_qkvs[s], step(qkv_got[s])))
        qkv_y_got[s] = y_send(qkv_kept[s])
    grad_first = step(
        sum(dot(a, w, NT) for a, w in zip(lax.optimization_barrier(grad_qkvs), w_qkvs))
    )
    two_x = step(x_add(two_y, [step(v) for v in two_x_got.values()]))
    sum_two = far_scatter(two_x)
    out_y = step(y_add(out_kept, step(out_y_got)))
    out_x_got = [over_mp(out_y[:, :, s * own : (s + 1) * own], s) for s in shifts[1:]]
    one_y = step(add(one_low, step(one_y_got)))
    sum_one = far_scatter(one_y)
    grad_first = cubes(step(grad_first))
    grad_shift_one = jnp.sum(grad_first, axis=1)
    grad_scale_one = jnp.sum(grad_first * normed_one, axis=1)
    grad_kept = grad_residual + norm_back(
        grad_first * (1.0 + scale_one), normed_one, scaled_one
    )
    grad_low = step(flat(grad_kept).astype(BF))
    grad_got = from_rows(grad_low)
    grad_gate_two = jnp.sum(grad_result * branch, axis=1)
    grad_gate_one = jnp.sum(grad_residual * attended, axis=1)
    for s in order:
        qkv_y[s] = step(y_add(qkv_kept[s], step(qkv_y_got[s])))
        if s:
            qkv_x_got = x_send({s: qkv_y[s]}) if s == last else {**qkv_x_got, **x_send({s: qkv_y[s]})}
    out_x = x_add([out_y[:, :, :own]], out_x_got)
    qkv_x = x_add(qkv_y, [step(v) for v in qkv_x_got.values()])
    a_x = jnp.concatenate([qkv_x, out_x], axis=2)
    for bit in far_bits:
        n = a_x.shape[0] // 2
        mine_bit = (d >> bit) & 1
        sent = lax.dynamic_slice_in_dim(a_x, (1 - mine_bit) * n, n, 0)
        kept = lax.dynamic_slice_in_dim(a_x, mine_bit * n, n, 0)
        a_x = kept.astype(F32) + over_dp(sent, bit).astype(F32)
        if n > 1:
            a_x = a_x.astype(BF)
    sum_a = a_x[0].astype(F32)
    sum_qkv, sum_out = sum_a[:, : 3 * own].reshape(blk, 3, own), sum_a[:, 3 * own :]

    grad_mod = jnp.stack(
        [
            grad_shift_one,
            grad_scale_one,
            grad_gate_one,
            grad_shift_two,
            grad_scale_two,
            grad_gate_two,
        ],
        axis=1,
    ).astype(BF)
    grad_mod = grad_mod.reshape(mine * 6, full)
    grad_mod = regroup(
        [
            over_mp(dot(grad_mod, p, NT, BF).reshape(mine, 6 * own), s)
            for s, p in enumerate(spreads)
        ]
    )
    grad_mod_all = grad_mod
    for bit in bits:
        grad_mod_all = jnp.concatenate([grad_mod_all, over_dp(grad_mod_all, bit)], 0)
    sum_ada = dot(silu_low, grad_mod_all, TN).reshape(blk, 6, own)
    grad_b_ada = jnp.sum(grad_mod_all.astype(F32), axis=0).reshape(6, own)
    grad_silu = dot(grad_mod_all, w_ada_flat, NT).reshape(nd, lat_dev * blk)
    grad_silu = exact_dot(place_hot.astype(F32), grad_silu, TN).reshape(nd, lat_dev, blk)
    grad_silu = lax.all_to_all(grad_silu, "dp", 0, 0)
    grad_silu = jnp.swapaxes(grad_silu, 0, 1).reshape(lat_dev, nm, own)
    grad_silu = sum(
        over_mp(lax.dynamic_index_in_dim(grad_silu, m ^ s, 1, keepdims=False), s) for s in shifts
    )
    cond_grad = jax.vjp(jax.nn.silu, condition.astype(F32))[1](grad_silu)[0]

    wide = jnp.stack([column_sums(grad_attended), column_sums(grad_branch)])
    bias_own = 0.0
    for s in shifts:
        narrow = exact_dot(wide, spreads[s].astype(F32), NT)
        piece = jnp.concatenate(
            [
                column_sums(grad_qkvs[s][:, :own]),
                column_sums(grad_qkvs[s][:, 2 * own :]),
                column_sums(grad_hiddens[s]),
                narrow.reshape(-1),
            ]
        )
        bias_own = bias_own + over_mp(piece, s)
    for bit in bits:
        bias_own = bias_own + over_dp(bias_own, bit)
    out_b_qv = bias_own[: 2 * own].reshape(2, own)
    out_b_one = bias_own[2 * own : 2 * own + ff]
    out_b_out = bias_own[2 * own + ff : 3 * own + ff]
    out_b_two = bias_own[3 * own + ff :]

    def put(got):
        return lax.dot_general(
            regroup(got), hot, (((1,), (1,)), ((0,), (0,))), preferred_element_type=F32
        )

    taken = jnp.sum(hot.astype(F32), axis=1)[:, None, :] > 0.5
    output = jnp.where(taken, put(fresh_got), inputs.astype(F32)).astype(BF)
    input_grad = jnp.where(
        taken, put(grad_got), cotangent.astype(F32) * row_scale[:, None, None]
    )
    return (
        output,
        input_grad,
        cond_grad,
        sum_qkv,
        out_b_qv,
        sum_out.T,
        out_b_out,
        sum_one,
        out_b_one,
        sum_two.T,
        out_b_two,
        sum_ada,
        grad_b_ada,
    )


def solution(mesh):
    placed = (
        P("dp", "mp", None),
        P("dp", "mp"),
        P("dp", "mp", None),
        P("dp", None),
        P("dp"),
        P("dp"),
        P("dp", None, "mp"),
        P(None, "mp"),
        P("mp", "dp"),
        P("mp"),
        P("dp", "mp"),
        P("mp"),
        P("mp", "dp"),
        P("mp"),
        P("dp", None, "mp"),
        P(None, "mp"),
    )
    return jax.shard_map(
        local,
        mesh=mesh,
        in_specs=placed,
        out_specs=(
            P("dp", "mp", None),
            P("dp", "mp", None),
            P("dp", "mp"),
            P("dp", None, "mp"),
            P(None, "mp"),
            P("mp", "dp"),
            P("mp"),
            P("dp", "mp"),
            P("mp"),
            P("mp", "dp"),
            P("mp"),
            P("dp", None, "mp"),
            P(None, "mp"),
        ),
        check_vma=False,
    )
```

time: 1640 us -> 752 us (0.46)
  waiting for transfers between devices: 883 us -> 198 us
  local copies, waits for them, and re-layouts: 251 us -> 99.5 us
  blocking collectives: 132 us -> 0 us
  starting transfers between devices: 1.32 us -> 55.4 us
  Pallas kernels: 0 us -> 51.2 us
  matrix products: 240 us -> 218 us
    reduce_scatter x8 -> x2, waiting for transfers between devices: 524 us -> 0.01 us  [far_scatter(): lax.psum_scatter(v, 'dp', scatter_dimension=0, tiled=True, axis_index_gro...]
    all_gather x9 -> x3, waiting for transfers between devices: 286 us -> 4.7 us  [far_gather(): lax.all_gather(v, 'dp', axis=0, tiled=True, axis_index_groups=far_groups)]
    ppermute x0 -> x57, waiting for transfers between devices: none -> 186 us  [the longest x37 143 us: over_dp(): return lax.ppermute(v, 'dp', [(i, i ^ 1 << bit) for i in range(nd)])]
    psum x6 -> x0, blocking collectives: 127 us -> none  [the longest x1 62.4 us: local(): lax.psum((gradient_query_value_bias, grad_b_out, grad_b_one, grad_b_two,...]
    unnamed x21 -> x5, waiting for transfers between devices: 73.2 us -> 0.08 us
    gather x4 -> x0, local copies, waits for them, and re-layouts: 56 us -> none  [pick_rows(): table_rows[slot_rows]]
    pallas_call x0 -> x4, Pallas kernels: none -> 51.2 us  [the longest x2 27.1 us: attend_back(): pl.pallas_call(partial(attend_back_kernel, own // HD), out_shape=jax.Shap...]
    mul x12 -> x2, local copies, waits for them, and re-layouts: 45.5 us -> 0.15 us  [local(): grad_result = cot_rows * own_scale]
  transfers between devices with their start and end apart: 19 -> 64, of which waited for: 14 -> 27; matrix products, arithmetic and copies ran while one was open for 29% -> 50% of each run, Pallas kernels for 0% -> 7%
where the time goes in v1:
time: 752 us; the launch traced here: 742 us
  matrix products  218 us (29%)
  waiting for transfers between devices  198 us (26%)
  other arithmetic  102 us (14%)
  local copies, waits for them, and re-layouts  99.5 us (13%)
  starting transfers between devices  55.4 us (7%)
  Pallas kernels  51.2 us (7%)
  between operations  18.7 us (2%)
    dot_general x54, matrix products, dot(): lax.dot_general(left, right, (dims, ((), ())), preferred_element_type=kind)  197 us
    ppermute x37, waiting for transfers between devices, over_dp(): return lax.ppermute(v, 'dp', [(i, i ^ 1 << bit) for i in range(nd)])  143 us
    ppermute x20, waiting for transfers between devices, over_mp(): lax.ppermute(v, 'mp', [(i, i ^ s) for i in range(nm)])  42.7 us
    pallas_call x2, Pallas kernels, attend_back(): pl.pallas_call(partial(attend_back_kernel, own // HD), out_shape=jax.Shap...  27.1 us
    pallas_call x2, Pallas kernels, attend(): pl.pallas_call(partial(attend_kernel, own // HD), out_shape=jax.ShapeDtyp...  24 us
    ppermute x20, starting transfers between devices, over_mp(): lax.ppermute(v, 'mp', [(i, i ^ s) for i in range(nm)])  23.8 us
    unnamed x309, local copies, waits for them, and re-layouts  22.8 us
    ppermute x37, starting transfers between devices, over_dp(): return lax.ppermute(v, 'dp', [(i, i ^ 1 << bit) for i in range(nd)])  21.1 us
  transfers between devices with their start and end apart: 64, of which 27 were waited for; matrix products, arithmetic and copies ran while one was open for 50% of the time, Pallas kernels for 7%

profile of v1, /device:TPU:0, one launch (start us, length us, event | category | flops | bytes accessed | tf_op | source)
XLA Modules:
  0.0 742.0 jit_solution(665882856906675603)
XLA Ops:
  20.5 6.5 all-to-all-start
  66.1 12.1 %collective-permute-done.5 = f32[1,8,3456]{2,1,0:T(8,128)S(1)} collective-permute-done((f32[1,8,3456]{2,1,0:T(8,128)S(1)}, f32[1,8,3456]{2,1,0:T(8,128)S(1)}, u32[]{:S(2)}, u32[]{:S(2)}) %collective-permute-start.5) | collective-permute-done | bytes 110624 | tf_op jit(solution)/shard_map/ppermute | solution.py:153
  135.8 11.8 %shard_map.255 = bf16[768,576]{1,0:T(8,128)(2,1)S(1)} custom-call(s32[4]{0:T(128)S(1)} %dynamic_slice.76.counts, bf16[768,1728]{1,0:T(8,128)(2,1)S(1)} %add_convert_fusion.1.qkv_ref), custom_call_target="tpu_custom_call" | custom-call | tf_op jit(solution)/shard_map/pallas_call | solution.py:87
  151.4 6.6 collective-permute-done.12
  186.5 12.3 %shard_map.256 = bf16[768,576]{1,0:T(8,128)(2,1)S(1)} custom-call(s32[4]{0:T(128)S(1)} %dynamic_slice.76.counts, bf16[768,1728]{1,0:T(8,128)(2,1)S(1)} %add_convert_fusion.qkv_ref), custom_call_target="tpu_custom_call" | custom-call | tf_op jit(solution)/shard_map/pallas_call | solution.py:87
  217.1 9.7 %multiply_add_fusion.1 = (f32[768,2304]{1,0:T(8,128)}, bf16[768,2304]{1,0:T(8,128)(2,1)S(1)}) fusion(f32[2304]{0:T(1024)S(1)} %copy-done.130, bf16[768,1152]{1,0:T(8,128)(2,1)S(1)} %fusion.10, bf16[1152,2304]{1,0:T(8,128)(2,1)S(1)} %bitcast.296), kind=kOutput, calls=%fused_computation.6 | convolution fusion | flops 4110483456 | bytes 17703936 | tf_op jit(solution)/shard_map/dot_general | solution.py:21
  242.4 6.7 convolution_add_fusion.7
  251.3 10.2 %multiply_add_fusion = (f32[768,2304]{1,0:T(8,128)}, bf16[768,2304]{1,0:T(8,128)(2,1)}) fusion(f32[2304]{0:T(1024)S(1)} %slice_convert_fusion, bf16[768,1152]{1,0:T(8,128)(2,1)S(1)} %fusion.10, bf16[1152,2304]{1,0:T(8,128)(2,1)S(1)} %bitcast.298), kind=kOutput, calls=%fused_computation.2 | convolution fusion | flops 4110483456 | bytes 17703936 | tf_op jit(solution)/shard_map/dot_general | solution.py:21
  261.6 10.6 %collective-permute-done.21 = bf16[4,72,2304]{2,1,0:T(8,128)(2,1)} collective-permute-done((bf16[4,72,2304]{2,1,0:T(8,128)(2,1)}, bf16[4,72,2304]{2,1,0:T(8,128)(2,1)}, u32[]{:S(2)}, u32[]{:S(2)}) %collective-permute-start.21) | collective-permute-done | bytes 1327136 | tf_op jit(solution)/shard_map/ppermute | solution.py:156
  294.9 7.0 convolution_add_fusion.6
  301.9 9.3 %collective-permute-done.24 = bf16[4,192,576]{2,1,0:T(8,128)(2,1)S(1)} collective-permute-done((bf16[4,192,576]{2,1,0:T(8,128)(2,1)S(1)}, bf16[4,192,576]{2,1,0:T(8,128)(2,1)S(1)}, u32[]{:S(2)}, u32[]{:S(2)}) %collective-permute-start.24) | collective-permute-done | bytes 884768 | tf_op jit(solution)/shard_map/ppermute | solution.py:156
  325.7 7.1 multiply_convert_fusion.1
  348.9 8.8 %multiply_convert_fusion = bf16[768,2304]{1,0:T(8,128)(2,1)S(1)} fusion(f32[768,2304]{1,0:T(8,128)} %get-tuple-element.176, bf16[768,1152]{1,0:T(8,128)(2,1)S(1)} %get-tuple-element.200, bf16[1152,2304]{1,0:T(8,128)(2,1)} %bitcast.301), kind=kOutput, calls=%fused_computation | convolution fusion | flops 4080402432 | bytes 17694720 | tf_op jit(solution)/shard_map/dot_general | solution.py:21
  371.2 9.1 %fusion.161 = f32[768,1152]{1,0:T(8,128)} fusion(bf16[768,2304]{1,0:T(8,128)(2,1)S(1)} %multiply_convert_fusion, bf16[1152,2304]{1,0:T(8,128)(2,1)} %bitcast.297), kind=kOutput, calls=%fused_computation.357 | convolution fusion | flops 4076863488 | bytes 12386304 | tf_op jit(solution)/shard_map/dot_general | solution.py:21
  380.4 8.9 %convolution_add_fusion.5 = f32[768,1152]{1,0:T(8,128)S(1)} fusion(f32[768,1152]{1,0:T(8,128)} %fusion.161, bf16[768,2304]{1,0:T(8,128)(2,1)S(1)} %multiply_convert_fusion.1, bf16[1152,2304]{1,0:T(8,128)(2,1)} %bitcast.299), kind=kOutput, calls=%fused_computation.47 | convolution fusion | flops 4077748224 | bytes 15925248 | tf_op jit(solution)/shard_map/dot_general | solution.py:21
  438.4 10.7 %collective-permute-done.30 = bf16[4,72,2304]{2,1,0:T(8,128)(2,1)} collective-permute-done((bf16[4,72,2304]{2,1,0:T(8,128)(2,1)}, bf16[4,72,2304]{2,1,0:T(8,128)(2,1)}, u32[]{:S(2)}, u32[]{:S(2)}) %collective-permute-start.30) | collective-permute-done | bytes 1327136 | tf_op jit(solution)/shard_map/ppermute | solution.py:153
  458.2 13.4 %shard_map.257 = bf16[768,1728]{1,0:T(8,128)(2,1)S(1)} custom-call(s32[4]{0:T(128)S(1)} %copy-done.15, bf16[768,1728]{1,0:T(8,128)(2,1)S(1)} %copy-done.3, bf16[768,576]{1,0:T(8,128)(2,1)S(1)} %copy.106.g_ref), custom_call_target="tpu_custom_call" | custom-call | tf_op jit(solution)/shard_map/pallas_call | solution.py:106
  478.1 13.7 %shard_map.258 = bf16[768,1728]{1,0:T(8,128)(2,1)S(1)} custom-call(s32[4]{0:T(128)S(1)} %copy-done.15, bf16[768,1728]{1,0:T(8,128)(2,1)S(1)} %copy-done.1, bf16[768,576]{1,0:T(8,128)(2,1)S(1)} %copy-done.9), custom_call_target="tpu_custom_call" | custom-call | tf_op jit(solution)/shard_map/pallas_call | solution.py:106
  503.5 5.9 fusion.165
  511.1 5.7 convolution_add_fusion.4
  538.6 24.4 %collective-permute-done.37 = bf16[4,72,1152]{2,1,0:T(8,128)(2,1)} collective-permute-done((bf16[4,72,1152]{2,1,0:T(8,128)(2,1)}, bf16[4,72,1152]{2,1,0:T(8,128)(2,1)}, u32[]{:S(2)}, u32[]{:S(2)}) %collective-permute-start.37) | collective-permute-done | bytes 663584 | tf_op jit(solution)/shard_map/ppermute | solution.py:153
  611.4 39.6 %collective-permute-done.43 = bf16[32,3456]{1,0:T(8,128)(2,1)S(1)} collective-permute-done((bf16[32,3456]{1,0:T(8,128)(2,1)S(1)}, bf16[32,3456]{1,0:T(8,128)(2,1)S(1)}, u32[]{:S(2)}, u32[]{:S(2)}) %collective-permute-start.43) | collective-permute-done | bytes 221216 | tf_op jit(solution)/shard_map/ppermute | solution.py:153
  681.3 9.9 %collective-permute-done.48 = bf16[4,72,1728]{2,1,0:T(8,128)(2,1)} collective-permute-done((bf16[4,72,1728]{2,1,0:T(8,128)(2,1)}, bf16[4,72,1728]{2,1,0:T(8,128)(2,1)}, u32[]{:S(2)}, u32[]{:S(2)}) %collective-permute-start.48) | collective-permute-done | bytes 995360 | tf_op jit(solution)/shard_map/ppermute | solution.py:156
  700.0 24.4 %collective-permute-done.50 = bf16[2,72,2304]{2,1,0:T(8,128)(2,1)S(1)} collective-permute-done((bf16[2,72,2304]{2,1,0:T(8,128)(2,1)S(1)}, bf16[2,72,2304]{2,1,0:T(8,128)(2,1)S(1)}, u32[]{:S(2)}, u32[]{:S(2)}) %collective-permute-start.50) | collective-permute-done | bytes 663584 | tf_op jit(solution)/shard_map/ppermute | solution.py:153
  (667 shorter events, 438.8 us)
Async XLA Ops:
  7.2 40.4 %all-gather.4.cloned.1.call-start = ((), (), s32[]{:S(2)}) async-start(), calls=%async_computation.4 | async-start | bytes 1658880 | tf_op jit(solution)/shard_map/all_gather | solution.py:203
  27.0 65.7 %all-gather.6.cloned.1.call-start = ((), (), s32[]{:S(2)}) async-start(), calls=%async_computation.5 | async-start | bytes 1658880 | tf_op jit(solution)/shard_map/all_gather | solution.py:203
  56.2 106.4 %all-gather.8.cloned.1.call-start = ((), (), s32[]{:S(2)}) async-start(), calls=%async_computation.6 | async-start | bytes 1658880 | tf_op jit(solution)/shard_map/all_gather | solution.py:203
  92.6 34.9 %collective-permute-start.10 = (bf16[8,72,2304]{2,1,0:T(8,128)(2,1)}, bf16[8,72,2304]{2,1,0:T(8,128)(2,1)}, u32[]{:S(2)}, u32[]{:S(2)}) collective-permute-start(bf16[8,72,2304]{2,1,0:T(8,128)(2,1)} %pad_maximum_fusion.6), channel_id=1, source_target_pairs={{0,2},{2,0},{4,6},{6,4},{8,10},{10,8},{12,14},{14,12},{16,18},{18,... | collective-permute-start | bytes 7962632 | tf_op jit(solution)/shard_map/ppermute | solution.py:153
  92.7 632.1 %reduce-scatter.5.cloned.1.call-start = ((), (), s32[]{:S(2)}) async-start(), calls=%async_computation.8 | async-start | bytes 1658880 | tf_op jit(solution)/shard_map/reduce_scatter | solution.py:430
  167.3 46.1 %collective-permute-start.16 = (bf16[8,72,2304]{2,1,0:T(8,128)(2,1)}, bf16[8,72,2304]{2,1,0:T(8,128)(2,1)}, u32[]{:S(2)}, u32[]{:S(2)}) collective-permute-start(bf16[8,72,2304]{2,1,0:T(8,128)(2,1)} %pad_maximum_fusion.8), channel_id=1, source_target_pairs={{0,2},{2,0},{4,6},{6,4},{8,10},{10,8},{12,14},{14,12},{16,18},{18,... | collective-permute-start | bytes 7962632 | tf_op jit(solution)/shard_map/ppermute | solution.py:153
  169.8 32.3 %collective-permute-start.15 = (bf16[4,72,2304]{2,1,0:T(8,128)(2,1)}, bf16[4,72,2304]{2,1,0:T(8,128)(2,1)}, u32[]{:S(2)}, u32[]{:S(2)}) collective-permute-start(bf16[4,72,2304]{2,1,0:T(8,128)(2,1)} %bitcast.323), channel_id=1, source_target_pairs={{0,1},{1,0},{2,3},{3,2},{4,5},{5,4},{6,7},{7,6},{8,9},{9,8},{10,11... | collective-permute-start | bytes 3981320 | tf_op jit(solution)/shard_map/ppermute | solution.py:156
  175.7 32.4 %collective-permute-start.14 = (bf16[4,72,2304]{2,1,0:T(8,128)(2,1)}, bf16[4,72,2304]{2,1,0:T(8,128)(2,1)}, u32[]{:S(2)}, u32[]{:S(2)}) collective-permute-start(bf16[4,72,2304]{2,1,0:T(8,128)(2,1)} %bitcast.26), channel_id=1, source_target_pairs={{0,4},{2,6},{4,0},{6,2},{8,12},{10,14},{12,8},{14,10},{16,20},{18,... | collective-permute-start | bytes 3981320 | tf_op jit(solution)/shard_map/ppermute | solution.py:153
  176.4 53.1 %collective-permute-start.19 = (bf16[4,72,2304]{2,1,0:T(8,128)(2,1)}, bf16[4,72,2304]{2,1,0:T(8,128)(2,1)}, u32[]{:S(2)}, u32[]{:S(2)}) collective-permute-start(bf16[4,72,2304]{2,1,0:T(8,128)(2,1)} %bitcast.26), channel_id=1, source_target_pairs={{0,1},{1,0},{2,3},{3,2},{4,5},{5,4},{6,7},{7,6},{8,9},{9,8},{10,11... | collective-permute-start | bytes 3981320 | tf_op jit(solution)/shard_map/ppermute | solution.py:156
  202.1 33.2 %collective-permute-start.18 = (bf16[4,72,2304]{2,1,0:T(8,128)(2,1)}, bf16[4,72,2304]{2,1,0:T(8,128)(2,1)}, u32[]{:S(2)}, u32[]{:S(2)}) collective-permute-start(bf16[4,72,2304]{2,1,0:T(8,128)(2,1)} %collective-permute-done.15), channel_id=1, source_target_pairs={{0,4},{2,6},{4,0},{6,2},{8,12},{10,14},{12,8},{14,10},{16,20},{18,... | collective-permute-start | bytes 3981320 | tf_op jit(solution)/shard_map/ppermute | solution.py:153
  325.2 32.5 %collective-permute-start.25 = (bf16[576,2304]{1,0:T(8,128)(2,1)}, bf16[576,2304]{1,0:T(8,128)(2,1)}, u32[]{:S(2)}, u32[]{:S(2)}) collective-permute-start(bf16[576,2304]{1,0:T(8,128)(2,1)} %fusion.157), channel_id=1, source_target_pairs={{0,2},{2,0},{4,6},{6,4},{8,10},{10,8},{12,14},{14,12},{16,18},{18,... | collective-permute-start | bytes 7962632 | tf_op jit(solution)/shard_map/ppermute | solution.py:153
  337.0 34.2 %collective-permute-start.23 = (bf16[4,192,576]{2,1,0:T(8,128)(2,1)}, bf16[4,192,576]{2,1,0:T(8,128)(2,1)S(1)}, u32[]{:S(2)}, u32[]{:S(2)}) collective-permute-start(bf16[4,192,576]{2,1,0:T(8,128)(2,1)} %fusion.23), channel_id=1, source_target_pairs={{0,1},{1,0},{2,3},{3,2},{4,5},{5,4},{6,7},{7,6},{8,9},{9,8},{10,11... | collective-permute-start | bytes 2654216 | tf_op jit(solution)/shard_map/ppermute | solution.py:156
  389.3 46.3 %collective-permute-start.31 = (bf16[4,72,2304]{2,1,0:T(8,128)(2,1)}, bf16[4,72,2304]{2,1,0:T(8,128)(2,1)}, u32[]{:S(2)}, u32[]{:S(2)}) collective-permute-start(bf16[4,72,2304]{2,1,0:T(8,128)(2,1)} %slice.315), channel_id=1, source_target_pairs={{0,4},{2,6},{4,0},{6,2},{8,12},{10,14},{12,8},{14,10},{16,20},{18,... | collective-permute-start | bytes 3981320 | tf_op jit(solution)/shard_map/ppermute | solution.py:153
  389.6 59.5 %collective-permute-start.30 = (bf16[4,72,2304]{2,1,0:T(8,128)(2,1)}, bf16[4,72,2304]{2,1,0:T(8,128)(2,1)}, u32[]{:S(2)}, u32[]{:S(2)}) collective-permute-start(bf16[4,72,2304]{2,1,0:T(8,128)(2,1)} %slice.313), channel_id=1, source_target_pairs={{0,4},{2,6},{4,0},{6,2},{8,12},{10,14},{12,8},{14,10},{16,20},{18,... | collective-permute-start | bytes 3981320 | tf_op jit(solution)/shard_map/ppermute | solution.py:153
  429.9 87.8 %collective-permute-start.35 = (bf16[4,72,2304]{2,1,0:T(8,128)(2,1)}, bf16[4,72,2304]{2,1,0:T(8,128)(2,1)}, u32[]{:S(2)}, u32[]{:S(2)}) collective-permute-start(bf16[4,72,2304]{2,1,0:T(8,128)(2,1)} %get-tuple-element.344), channel_id=1, source_target_pairs={{0,1},{1,0},{2,3},{3,2},{4,5},{5,4},{6,7},{7,6},{8,9},{9,8},{10,11... | collective-permute-start | bytes 3981320 | tf_op jit(solution)/shard_map/ppermute | solution.py:156
  499.7 35.3 %collective-permute-start.38 = (bf16[4,72,2304]{2,1,0:T(8,128)(2,1)}, bf16[4,72,2304]{2,1,0:T(8,128)(2,1)}, u32[]{:S(2)}, u32[]{:S(2)}) collective-permute-start(bf16[4,72,2304]{2,1,0:T(8,128)(2,1)} %add_convert_fusion.14), channel_id=1, source_target_pairs={{0,1},{1,0},{2,3},{3,2},{4,5},{5,4},{6,7},{7,6},{8,9},{9,8},{10,11... | collective-permute-start | bytes 3981320 | tf_op jit(solution)/shard_map/ppermute | solution.py:156
  517.7 47.5 %collective-permute-start.36 = (bf16[4,72,2304]{2,1,0:T(8,128)(2,1)}, bf16[4,72,2304]{2,1,0:T(8,128)(2,1)}, u32[]{:S(2)}, u32[]{:S(2)}) collective-permute-start(bf16[4,72,2304]{2,1,0:T(8,128)(2,1)} %add_convert_fusion.12), channel_id=1, source_target_pairs={{0,4},{2,6},{4,0},{6,2},{8,12},{10,14},{12,8},{14,10},{16,20},{18,... | collective-permute-start | bytes 3981320 | tf_op jit(solution)/shard_map/ppermute | solution.py:153
  521.1 42.0 %collective-permute-start.37 = (bf16[4,72,1152]{2,1,0:T(8,128)(2,1)}, bf16[4,72,1152]{2,1,0:T(8,128)(2,1)}, u32[]{:S(2)}, u32[]{:S(2)}) collective-permute-start(bf16[4,72,1152]{2,1,0:T(8,128)(2,1)} %slice.321), channel_id=1, source_target_pairs={{0,4},{2,6},{4,0},{6,2},{8,12},{10,14},{12,8},{14,10},{16,20},{18,... | collective-permute-start | bytes 1990664 | tf_op jit(solution)/shard_map/ppermute | solution.py:153
  579.2 147.5 %reduce-scatter.3.cloned.1.call-start = ((), (), s32[]{:S(2)}) async-start(), calls=%async_computation.7 | async-start | bytes 1658880 | tf_op jit(solution)/shard_map/reduce_scatter | solution.py:430
  595.4 63.5 %collective-permute-start.49 = (bf16[4,72,576]{2,1,0:T(8,128)(2,1)}, bf16[4,72,576]{2,1,0:T(8,128)(2,1)}, u32[]{:S(2)}, u32[]{:S(2)}) collective-permute-start(bf16[4,72,576]{2,1,0:T(8,128)(2,1)} %slice.327), channel_id=1, source_target_pairs={{0,1},{1,0},{2,3},{3,2},{4,5},{5,4},{6,7},{7,6},{8,9},{9,8},{10,11... | collective-permute-start | bytes 995336 | tf_op jit(solution)/shard_map/ppermute | solution.py:156
  601.1 61.9 %collective-permute-start.47 = (bf16[4,72,1728]{2,1,0:T(8,128)(2,1)}, bf16[4,72,1728]{2,1,0:T(8,128)(2,1)}, u32[]{:S(2)}, u32[]{:S(2)}) collective-permute-start(bf16[4,72,1728]{2,1,0:T(8,128)(2,1)} %slice.325), channel_id=1, source_target_pairs={{0,4},{2,6},{4,0},{6,2},{8,12},{10,14},{12,8},{14,10},{16,20},{18,... | collective-permute-start | bytes 2985992 | tf_op jit(solution)/shard_map/ppermute | solution.py:153
  602.9 76.9 %collective-permute-start.46 = (bf16[4,72,1728]{2,1,0:T(8,128)(2,1)}, bf16[4,72,1728]{2,1,0:T(8,128)(2,1)S(1)}, u32[]{:S(2)}, u32[]{:S(2)}) collective-permute-start(bf16[4,72,1728]{2,1,0:T(8,128)(2,1)} %slice.323), channel_id=1, source_target_pairs={{0,4},{2,6},{4,0},{6,2},{8,12},{10,14},{12,8},{14,10},{16,20},{18,... | collective-permute-start | bytes 2985992 | tf_op jit(solution)/shard_map/ppermute | solution.py:153
  607.1 43.9 %collective-permute-start.43 = (bf16[32,3456]{1,0:T(8,128)(2,1)S(1)}, bf16[32,3456]{1,0:T(8,128)(2,1)S(1)}, u32[]{:S(2)}, u32[]{:S(2)}) collective-permute-start(bf16[32,3456]{1,0:T(8,128)(2,1)S(1)} %pad_maximum_fusion.20), channel_id=1, source_target_pairs={{0,4},{2,6},{4,0},{6,2},{8,12},{10,14},{12,8},{14,10},{16,20},{18,... | collective-permute-start | bytes 663560 | tf_op jit(solution)/shard_map/ppermute | solution.py:153
  610.1 65.0 %collective-permute-start.39 = (bf16[4,192,576]{2,1,0:T(8,128)(2,1)}, bf16[4,192,576]{2,1,0:T(8,128)(2,1)}, u32[]{:S(2)}, u32[]{:S(2)}) collective-permute-start(bf16[4,192,576]{2,1,0:T(8,128)(2,1)} %bitcast.48), channel_id=1, source_target_pairs={{0,1},{1,0},{2,3},{3,2},{4,5},{5,4},{6,7},{7,6},{8,9},{9,8},{10,11... | collective-permute-start | bytes 2654216 | tf_op jit(solution)/shard_map/ppermute | solution.py:156
  (187 other events, 2977.9 us)
Sparse Core Ops, SparseCore 0:
  13.4 34.0 all-gather.3
  56.3 36.3 all-gather.5
  94.2 32.8 all-gather.7
  579.3 33.7 reduce-scatter.4
  615.3 30.4 reduce-scatter.2

commit v2 on v1

--- a/solution.py
+++ b/solution.py
@@ -78,8 +78,8 @@
         )
 
 
-def attend(counts, qkv, keep):
-    rows, own = qkv.shape[0], qkv.shape[1] // 3
+def attend(counts, qkv, own, keep):
+    rows = qkv.shape[0]
 
     def block(n):
         return pl.BlockSpec((keep, n), lambda i, c: (i, 0))
@@ -90,7 +90,7 @@
         grid_spec=pltpu.PrefetchScalarGridSpec(
             num_scalar_prefetch=1,
             grid=(rows // keep,),
-            in_specs=[block(3 * own)],
+            in_specs=[block(qkv.shape[1])],
             out_specs=block(own),
         ),
         compiler_params=pltpu.CompilerParams(vmem_limit_bytes=40 * 2**20),
@@ -109,7 +109,7 @@
         grid_spec=pltpu.PrefetchScalarGridSpec(
             num_scalar_prefetch=1,
             grid=(rows // keep,),
-            in_specs=[block(3 * own), block(own)],
+            in_specs=[block(qkv.shape[1]), block(own)],
             out_specs=block(3 * own),
         ),
         compiler_params=pltpu.CompilerParams(vmem_limit_bytes=40 * 2**20),
@@ -149,11 +149,15 @@
     zb = 2 ** len(far_bits)
     shifts = range(nm)
 
+    step = Steps()
+
     def over_dp(v, bit):
-        return lax.ppermute(v, "dp", [(i, i ^ (1 << bit)) for i in range(nd)])
+        return lax.ppermute(step(v), "dp", [(i, i ^ (1 << bit)) for i in range(nd)])
 
     def over_mp(v, s):
-        return v if s == 0 else lax.ppermute(v, "mp", [(i, i ^ s) for i in range(nm)])
+        if s == 0:
+            return v
+        return lax.ppermute(step(v), "mp", [(i, i ^ s) for i in range(nm)])
 
     def rel(place):
         out = jnp.zeros_like(place)
@@ -178,7 +182,6 @@
         == lax.broadcasted_iota(jnp.int32, (nd, nd), 1)
     )
     far_groups = [[low + 4 * k for k in range(zb)] for low in range(4)]
-    step = Steps()
 
     def group_of(v, s):
         return lax.dynamic_slice_in_dim(v, (m ^ s) * mine, mine, 0)
@@ -202,9 +205,15 @@
     def far_gather(v):
         return lax.all_gather(v, "dp", axis=0, tiled=True, axis_index_groups=far_groups)
 
-    cond_halves = [over_mp(condition, s) for s in shifts]
+    def later(vs):
+        return [vs[0], *[step(v) for v in vs[1:]]]
+
     bias_vec = jnp.concatenate([b_qv.reshape(-1), b_one, b_out, b_two])
-    bias_all = [over_mp(bias_vec, s) for s in shifts]
+    bias_size = bias_vec.shape[0]
+    bias_rows = -(-bias_size // own)
+    bias_vec = jnp.pad(bias_vec, (0, bias_rows * own - bias_size)).reshape(bias_rows, own)
+    small = jnp.concatenate([condition, bias_vec], axis=0)
+    smalls = [over_mp(small, s) for s in shifts]
     w_a = jnp.concatenate([w_qkv.reshape(blk, 3 * own), w_out.T], axis=1)
     a_z = far_gather(w_a)
     one_z = far_gather(w_one)
@@ -220,22 +229,24 @@
             hot, source, (((2,), (2,)), ((0,), (0,))), preferred_element_type=BF
         )
 
-    w_a = step(w_a)
-    picked = pick(step(inputs))
-    picked = step(picked)
+    w_a, small = step(w_a, small)
+    picked = step(pick(step(inputs)))
     kept_got = send_rows(picked)
-    cond_halves = [cond_halves[0], *[step(v) for v in cond_halves[1:]]]
-    cond_halves = jnp.stack(cond_halves)
+    smalls = later(smalls)
+    cond_halves = jnp.stack([v[:lat_dev] for v in smalls])
+    bias_all = [v[lat_dev:].reshape(-1) for v in smalls]
     cond_full = jnp.concatenate(
         [lax.dynamic_index_in_dim(cond_halves, m ^ g, 0, keepdims=False) for g in shifts], axis=1
     )
-    cond_send = jnp.concatenate(
-        [
-            jnp.swapaxes(cond_full.reshape(lat_dev, nd, blk), 0, 1),
-            jnp.broadcast_to(digits.astype(BF)[None], (nd, lat_dev, 4)),
-            jnp.zeros((nd, lat_dev, pad), BF),
-        ],
-        axis=2,
+    cond_send = step(
+        jnp.concatenate(
+            [
+                jnp.swapaxes(cond_full.reshape(lat_dev, nd, blk), 0, 1),
+                jnp.broadcast_to(digits.astype(BF)[None], (nd, lat_dev, 4)),
+                jnp.zeros((nd, lat_dev, pad), BF),
+            ],
+            axis=2,
+        )
     )
     cond_got = lax.all_to_all(cond_send, "dp", 0, 0)
     w_two_t = w_two.T
@@ -258,6 +269,12 @@
     def part_add(part, got):
         return part[: part.shape[0] // 2] + got
 
+    def far_mask(place):
+        return sum(((place >> k) & 1) << bit for k, bit in enumerate(far_bits))
+
+    def over_far(v, place):
+        return lax.ppermute(step(v), "dp", [(i, i ^ far_mask(place)) for i in range(nd)])
+
     got = part_send(part, 0)
     part = part_add(part, step(got))
     got = part_send(part, 1)
@@ -265,44 +282,49 @@
     def core_pair(v):
         return (v, over_dp(v, 0))
 
-    def near_join(a, b):
-        return jnp.concatenate([a, b], 0)
-
-    def join(pair, start, stop):
-        return jnp.concatenate([v[:, :, start:stop] for v in pair], 0).reshape(full, stop - start)
-
-    def later(vs):
-        return [vs[0], *[step(v) for v in vs[1:]]]
-
-    a_z = step(a_z).reshape(zb, blk, 4 * own)
+    def join(first, second):
+        return jnp.stack([first[0], second[0], first[1], second[1]]).reshape(full, -1)
+
+    a_z = step(a_z)
     a_xs = [over_mp(a_z, s) for s in shifts]
     a_y = over_dp(a_z, 1)
     kept_got = later(kept_got)
     kept_slot = step(to_rows(kept_got)).reshape(mine, keep, full)
-    part = part_add(part, step(got))
-    for bit in reversed(far_bits):
-        got = part_send(part, bit)
-        part = part_add(part, step(got))
-    modulation = part.reshape(lat_dev, 6, own) + b_ada.astype(F32)
+    part = step(part_add(part, step(got)))
+    part_gots = [over_far(part[p], p) for p in range(1, zb)]
+    a_zc = core_pair(a_z)
+    modulation = part[0] + b_ada.astype(F32).reshape(6 * own)
+    for v in part_gots:
+        modulation = modulation + step(v)
     modulation = step(modulation)
-    mod_got = [over_mp(group_of(modulation, s), s).reshape(mine * 6, own) for s in shifts]
+
+    def mod_group(s):
+        own_part = group_of(modulation, s)
+        return jnp.stack([own_part[:, k * own : (k + 1) * own] for k in range(6)]).reshape(
+            6 * mine, own
+        )
+
+    mod_got = [over_mp(mod_group(s), s) for s in shifts]
+    cot_picked = step(pick(step(cotangent)))
+    cot_parts = step(*[group_of(cot_picked, s).reshape(rows, own) for s in shifts])
+    cot_parts = cot_parts if nm > 1 else [cot_parts]
+    mod_got = later(mod_got)
     a_xs = later(a_xs)
     a_y = step(a_y)
     a_xys = [over_mp(a_y, s) for s in shifts]
-    one_z = step(one_z).reshape(zb, blk, ff)
+    one_z = step(one_z)
     one_y = over_dp(one_z, 1)
-    a_pairs = {0: core_pair(step(near_join(a_z, a_y)))}
-    mod_got = later(mod_got)
+    a_yc = core_pair(a_y)
     mod_rows = sum(
         exact_dot(v, p.astype(F32), NN) for v, p in zip(mod_got, spreads)
-    ).reshape(mine, 6, full)
+    ).reshape(6, mine, full)
     shift_one, scale_one, gate_one, shift_two, scale_two, gate_two = [
-        mod_rows[:, k, None, :] for k in range(6)
+        mod_rows[k, :, None, :] for k in range(6)
     ]
     bias_qv = [v[: 2 * own].reshape(2, own).astype(F32) for v in bias_all]
     bias_one = [v[2 * own : 2 * own + ff].astype(F32) for v in bias_all]
     bias_wide = sum(
-        dot(v[2 * own + ff :].reshape(2, own), p, NN) for v, p in zip(bias_all, spreads)
+        dot(v[2 * own + ff : bias_size].reshape(2, own), p, NN) for v, p in zip(bias_all, spreads)
     )
     row_scale = lat_dev * nd * group_tokens.astype(F32) / token_total
     own_scale = group_of(row_scale, 0)[:, None, None]
@@ -331,42 +353,47 @@
     normed_one, scaled_one = normalize(kept_slot)
     first_low = flat((normed_one * (1.0 + scale_one) + shift_one).astype(BF))
     first_low = step(first_low)
-    w_qkvs, wo_t, qkvs, mixtures = [], [], [], []
+    w_as, qkvs, mixtures, wo_t = [], [], [], []
     attended = bias_wide[0]
+    a_pairs = {0: (a_zc, a_yc)}
     for s in shifts:
-        pair = (a_pairs[s][0], step(a_pairs[s][1]))
-        w_qkvs.append(join(pair, 0, 3 * own))
-        wo_t.append(join(pair, 3 * own, 4 * own))
-        bias = jnp.concatenate([bias_qv[s][0], jnp.zeros((own,), F32), bias_qv[s][1]])
-        qkv = step((dot(first_low, w_qkvs[s], NN) + bias).astype(BF))
+        first, second = a_pairs[s]
+        w_as.append(join((first[0], step(first[1])), (second[0], step(second[1]))))
+        bias = jnp.concatenate(
+            [bias_qv[s][0], jnp.zeros((own,), F32), bias_qv[s][1], jnp.zeros((own,), F32)]
+        )
+        qkv = step((dot(first_low, w_as[s], NN) + bias).astype(BF))
         qkvs.append(qkv)
-        mixture = step(attend(own_counts, qkv, keep))
+        mixture = step(attend(own_counts, qkv, own, keep))
         mixtures.append(mixture)
-        attended = step(attended + dot(mixture, wo_t[s], NT))
         if s == 0:
             a_xys = later(a_xys)
             one_y = step(one_y)
             one_xs = [over_mp(one_z, t) for t in shifts]
-            two_z = step(two_z).reshape(zb, blk, ff)
+            two_z = step(two_z)
             two_y = over_dp(two_z, 1)
             for t in shifts[1:]:
-                a_pairs[t] = core_pair(step(near_join(a_xs[t], a_xys[t])))
-            g_one = {0: core_pair(step(near_join(one_z, one_y)))}
+                a_pairs[t] = (core_pair(a_xs[t]), core_pair(a_xys[t]))
+        wo_t.append(w_as[s][:, 3 * own :])
+        attended = step(attended + dot(mixture, wo_t[s], NT))
+    one_zc, one_yc = core_pair(one_z), core_pair(one_y)
     one_xs = later(one_xs)
     two_y = step(two_y)
     two_xs = [over_mp(two_z, s) for s in shifts]
     one_xys = [one_y, *[over_dp(v, 1) for v in one_xs[1:]]]
-    g_two = {0: core_pair(step(near_join(two_z, two_y)))}
+    g_one = {0: (one_zc, one_yc)}
     attended = cubes(attended)
     residual = kept_slot + gate_one * attended
     normed_two, scaled_two = normalize(residual)
     second_low = flat((normed_two * (1.0 + scale_two) + shift_two).astype(BF))
     second_low = step(second_low)
+    g_two = {0: (core_pair(two_z), core_pair(two_y))}
     branch = bias_wide[1]
     w1, w2t, acts, slopes = [], [], [], []
     root = math.sqrt(2.0 / math.pi)
     for s in shifts:
-        w1.append(join((g_one[s][0], step(g_one[s][1])), 0, ff))
+        first, second = g_one[s]
+        w1.append(join((first[0], step(first[1])), (second[0], step(second[1]))))
         hidden = dot(second_low, w1[s], NN) + bias_one[s]
         square = hidden * hidden
         bend = jnp.tanh(root * hidden * (1.0 + 0.044715 * square))
@@ -380,36 +407,46 @@
         if s == 0:
             two_xs = later(two_xs)
             one_xys = later(one_xys)
-            two_xys = [over_mp(two_y, t) for t in shifts]
+            cols = ff // 384 * 128
+            two_xys = [None]
             for t in shifts[1:]:
-                g_one[t] = core_pair(step(near_join(one_xs[t], one_xys[t])))
+                two_xys.append(
+                    (over_mp(two_y[:, :cols], t), over_dp(two_xs[t][:, cols:], 1))
+                )
+            for t in shifts[1:]:
+                g_one[t] = (core_pair(one_xs[t]), core_pair(one_xys[t]))
             mixture_all = jnp.concatenate(mixtures, axis=1)
-            cot_picked = step(pick(cotangent))
+            cot_got = [over_mp(v, t) for t, v in enumerate(cot_parts)]
+        if s == 1:
+            for t in shifts[1:]:
+                ends = [core_pair(step(v)) for v in two_xys[t]]
+                g_two[t] = (core_pair(two_xs[t]), ends)
+            cot_got = later(cot_got)
+        first, second = g_two[s]
         if s:
-            for t in shifts[1:]:
-                two_xys[t] = step(two_xys[t]) if s == 1 else two_xys[t]
-            if s == 1:
-                cot_got = send_rows(cot_picked)
-            g_two[s] = core_pair(step(near_join(two_xs[s], two_xys[s])))
-        w2t.append(join((g_two[s][0], step(g_two[s][1])), 0, ff))
+            second = [(v[0], step(v[1])) for v in second]
+            second = [jnp.concatenate([v[k] for v in second], axis=1) for k in range(2)]
+        else:
+            second = (second[0], step(second[1]))
+        w2t.append(join((first[0], step(first[1])), second))
         branch = step(branch + dot(act, w2t[s], NT))
     branch = cubes(branch)
     result = residual + gate_two * branch
-    cot_got = later(cot_got)
-    fresh_got = from_rows(flat(result).astype(BF))
+    result_low = flat(result).astype(BF)
 
     def add(a, b):
         return (a.astype(F32) + b.astype(F32)).astype(BF)
 
+    near = zb * blk
+
     def keep_sum(low_side, v, got):
-        kept = (dot(low_side, v, TN) + got.astype(F32)).astype(BF)
-        return kept.reshape(2 * zb, blk, -1)
+        return (dot(low_side, v, TN) + got.astype(F32)).astype(BF)
 
     def y_send(v):
-        return over_dp(v[zb:], 1)
+        return over_dp(v[near:], 1)
 
     def y_add(v, got):
-        return add(v[:zb], got)
+        return add(v[:near], got)
 
     def x_send(vs):
         return {s: over_mp(v, s) for s, v in vs.items() if s}
@@ -430,33 +467,33 @@
         v = lax.psum_scatter(
             v, "dp", scatter_dimension=0, tiled=True, axis_index_groups=far_groups
         )
-        return v.astype(F32)
+        return v
 
     low, high, grad_branch = step(grad_branch[:, :half], grad_branch[:, half:], grad_branch)
-    two_sent, two_got, two_kept, two_y_got, two_y, two_x_got = {}, {}, {}, {}, {}, {}
+    two_got, two_kept, two_y_got, two_y, two_x_got = {}, {}, {}, {}, {}
     grad_hiddens = [None] * nm
+    last = order[0]
     for s in order:
-        two_sent[s] = step(dot(high, acts[s], TN, BF))
-        two_got[s] = over_dp(two_sent[s], 0)
+        two_got[s] = over_dp(step(dot(high, acts[s], TN, BF)), 0)
     for s in order:
         grad_hiddens[s] = step((dot(step(grad_branch), w2t[s], NN) * slopes[s]).astype(BF))
         two_kept[s] = step(keep_sum(low, acts[s], step(two_got[s])))
         two_y_got[s] = y_send(two_kept[s])
     low, high = step(second_low[:, :half], second_low[:, half:])
-    one_sent, one_got, one_kept = {}, {}, {}
+    one_got, one_kept, one_x_got = {}, {}, {}
     for s in order:
-        one_sent[s] = step(dot(high, grad_hiddens[s], TN, BF))
-        one_got[s] = over_dp(one_sent[s], 0)
-    fresh_got = later(fresh_got)
-    last = order[0]
-    grad_second = step(
-        sum(dot(v, w, NT) for v, w in zip(lax.optimization_barrier(grad_hiddens), w1))
-    )
-    one_x_got = {}
+        one_got[s] = over_dp(step(dot(high, grad_hiddens[s], TN, BF)), 0)
     for s in order:
         one_kept[s] = step(keep_sum(low, grad_hiddens[s], step(one_got[s])))
         if s:
-            one_x_got[s] = (over_mp(one_kept[s][zb:], s), over_mp(one_kept[s][:zb], s))
+            one_x_got[s] = (over_mp(one_kept[s][near:], s), over_mp(one_kept[s][:near], s))
+    grad_second = None
+    for s in shifts:
+        piece = dot(step(grad_hiddens[s]), w1[s], NT)
+        grad_second = step(piece if grad_second is None else grad_second + piece)
+    for s in order[:-1]:
+        two_y[s] = step(y_add(two_kept[s], step(two_y_got[s])))
+        two_x_got[s] = over_mp(two_y[s], s)
     grad_second = cubes(step(grad_second))
     grad_shift_two = jnp.sum(grad_second, axis=1)
     grad_scale_two = jnp.sum(grad_second * normed_two, axis=1)
@@ -467,65 +504,51 @@
     low, high, grad_attended = step(
         grad_attended[:, :half], grad_attended[:, half:], grad_attended
     )
-    out_sent = step(dot(high, mixture_all, TN, BF))
-    out_got = over_dp(out_sent, 0)
-    grad_mixtures = step(*[dot(step(grad_attended), w, NN, BF) for w in wo_t])
+    out_got = over_dp(step(dot(high, mixture_all, TN, BF)), 0)
+    grad_mixtures = [step(dot(step(grad_attended), w, NN, BF)) for w in wo_t]
+    two_y[0] = step(y_add(two_kept[0], step(two_y_got[0])))
+    one_high = step(x_add([one_kept[0][near:]], [step(v[0]) for v in one_x_got.values()]))
+    one_y_got = over_dp(one_high, 1)
     out_kept = step(keep_sum(low, mixture_all, step(out_got)))
-    for s in order:
-        two_y[s] = step(y_add(two_kept[s], step(two_y_got[s])))
-    one_high = step(x_add([one_kept[0][zb:]], [step(v[0]) for v in one_x_got.values()]))
-    one_y_got = over_dp(one_high, 1)
-    two_x_got = x_send(two_y)
-    grad_qkvs = [None] * nm
+    out_y_got = y_send(out_kept)
+    grad_qkvs, qkv_got, qk_kept, v_kept, qk_y_got, qk_y = [None] * nm, {}, {}, {}, {}, {}
     first_half, second_half = step(first_low[:, :half], first_low[:, half:])
-    qkv_sent, qkv_got, qkv_kept, qkv_y_got, qkv_y = {}, {}, {}, {}, {}
     for s in order:
         grad_qkvs[s] = step(attend_back(step(own_counts), qkvs[s], grad_mixtures[s], keep))
         if s == last:
-            out_y_got = y_send(out_kept)
-        qkv_sent[s] = step(dot(second_half, grad_qkvs[s], TN, BF))
-        qkv_got[s] = over_dp(qkv_sent[s], 0)
-    one_low = step(x_add([one_kept[0][:zb]], [step(v[1]) for v in one_x_got.values()]))
-    for s in order:
-        qkv_kept[s] = step(keep_sum(first_half, grad_qkvs[s], step(qkv_got[s])))
-        qkv_y_got[s] = y_send(qkv_kept[s])
-    grad_first = step(
-        sum(dot(a, w, NT) for a, w in zip(lax.optimization_barrier(grad_qkvs), w_qkvs))
-    )
+            one_x_got = {t: step(v[1]) for t, v in one_x_got.items()}
+            one_low = step(x_add([one_kept[0][:near]], one_x_got.values()))
+        else:
+            one_y_got = step(one_y_got) if s == 0 else one_y_got
+        qkv_got[s] = over_dp(step(dot(second_half, grad_qkvs[s], TN, BF)), 0)
     two_x = step(x_add(two_y, [step(v) for v in two_x_got.values()]))
     sum_two = far_scatter(two_x)
+    one_y = step(add(one_low, one_y_got))
+    fresh_got = from_rows(result_low)
+    sum_one = far_scatter(one_y)
+    v_x_got = {}
+    for s in order:
+        kept = step(keep_sum(first_half, grad_qkvs[s], step(qkv_got[s])))
+        qk_kept[s], v_kept[s] = kept[:, : 2 * own], kept[:, 2 * own :]
+        qk_y_got[s] = y_send(qk_kept[s])
+        if s:
+            v_x_got[s] = over_mp(v_kept[s], s)
     out_y = step(y_add(out_kept, step(out_y_got)))
-    out_x_got = [over_mp(out_y[:, :, s * own : (s + 1) * own], s) for s in shifts[1:]]
-    one_y = step(add(one_low, step(one_y_got)))
-    sum_one = far_scatter(one_y)
+    out_x_got = [over_mp(out_y[:, s * own : (s + 1) * own], s) for s in shifts[1:]]
+    w_qkvs = [w[:, : 3 * own] for w in w_as]
+    grad_first = step(dot(step(grad_qkvs[0]), w_qkvs[0], NT))
+    fresh_got = later(fresh_got)
+    qk_y[last] = step(y_add(qk_kept[last], step(qk_y_got[last])))
+    qk_x_got = {last: over_mp(qk_y[last], last)} if last else {}
+    for s in shifts[1:]:
+        grad_first = step(grad_first + dot(step(grad_qkvs[s]), w_qkvs[s], NT))
+    v_x = step(x_add(v_kept, [step(v) for v in v_x_got.values()]))
+    v_y_got = y_send(v_x)
     grad_first = cubes(step(grad_first))
     grad_shift_one = jnp.sum(grad_first, axis=1)
     grad_scale_one = jnp.sum(grad_first * normed_one, axis=1)
-    grad_kept = grad_residual + norm_back(
-        grad_first * (1.0 + scale_one), normed_one, scaled_one
-    )
-    grad_low = step(flat(grad_kept).astype(BF))
-    grad_got = from_rows(grad_low)
     grad_gate_two = jnp.sum(grad_result * branch, axis=1)
     grad_gate_one = jnp.sum(grad_residual * attended, axis=1)
-    for s in order:
-        qkv_y[s] = step(y_add(qkv_kept[s], step(qkv_y_got[s])))
-        if s:
-            qkv_x_got = x_send({s: qkv_y[s]}) if s == last else {**qkv_x_got, **x_send({s: qkv_y[s]})}
-    out_x = x_add([out_y[:, :, :own]], out_x_got)
-    qkv_x = x_add(qkv_y, [step(v) for v in qkv_x_got.values()])
-    a_x = jnp.concatenate([qkv_x, out_x], axis=2)
-    for bit in far_bits:
-        n = a_x.shape[0] // 2
-        mine_bit = (d >> bit) & 1
-        sent = lax.dynamic_slice_in_dim(a_x, (1 - mine_bit) * n, n, 0)
-        kept = lax.dynamic_slice_in_dim(a_x, mine_bit * n, n, 0)
-        a_x = kept.astype(F32) + over_dp(sent, bit).astype(F32)
-        if n > 1:
-            a_x = a_x.astype(BF)
-    sum_a = a_x[0].astype(F32)
-    sum_qkv, sum_out = sum_a[:, : 3 * own].reshape(blk, 3, own), sum_a[:, 3 * own :]
-
     grad_mod = jnp.stack(
         [
             grad_shift_one,
@@ -537,31 +560,60 @@
         ],
         axis=1,
     ).astype(BF)
-    grad_mod = grad_mod.reshape(mine * 6, full)
-    grad_mod = regroup(
-        [
-            over_mp(dot(grad_mod, p, NT, BF).reshape(mine, 6 * own), s)
-            for s, p in enumerate(spreads)
-        ]
-    )
-    grad_mod_all = grad_mod
-    for bit in bits:
-        grad_mod_all = jnp.concatenate([grad_mod_all, over_dp(grad_mod_all, bit)], 0)
-    sum_ada = dot(silu_low, grad_mod_all, TN).reshape(blk, 6, own)
-    grad_b_ada = jnp.sum(grad_mod_all.astype(F32), axis=0).reshape(6, own)
+    grad_mod = step(grad_mod.reshape(mine * 6, full))
+    if last:
+        qk_x_got[last] = step(qk_x_got[last])
+    out_x_got = [step(v) for v in out_x_got]
+    mod_back = [
+        over_mp(dot(grad_mod, p, NT, BF).reshape(mine, 6 * own), s)
+        for s, p in enumerate(spreads)
+    ]
+    for s in order[1:]:
+        qk_y[s] = step(y_add(qk_kept[s], step(qk_y_got[s])))
+        if s:
+            qk_x_got[s] = over_mp(qk_y[s], s)
+    mod_back = step(regroup(later(mod_back)))
+    mod_gots = [over_far(mod_back, p) for p in range(1, zb)]
+    out_x = x_add([out_y[:, :own]], out_x_got)
+    qk_x = step(x_add(qk_y, [step(v) for v in qk_x_got.values()]))
+    v_y = y_add(v_x, step(v_y_got))
+    a_x = step(jnp.concatenate([qk_x, v_y, out_x], axis=1)).reshape(zb, blk, 4 * own)
+    far_at = d >> 2
+    far_kept = lax.dynamic_index_in_dim(a_x, far_at, 0, keepdims=False)
+    far_sent = [
+        lax.dynamic_index_in_dim(a_x, far_at ^ k, 0, keepdims=False) for k in range(1, zb)
+    ]
+    mod_gots = [step(v) for v in mod_gots]
+    grad_mod_all = step(jnp.concatenate([mod_back, *mod_gots], 0))
+    mod_got = over_dp(grad_mod_all, 1)
+    far_got = [
+        lax.ppermute(step(v), "dp", [(i, i ^ ((k + 1) << 2)) for i in range(nd)])
+        for k, v in enumerate(far_sent)
+    ]
+    grad_kept = grad_residual + norm_back(
+        step(grad_first) * (1.0 + scale_one), normed_one, scaled_one
+    )
+    grad_low = step(flat(grad_kept).astype(BF))
+    grad_mod_all = step(jnp.concatenate([grad_mod_all, step(mod_got)], 0))
+    mod_got = over_dp(grad_mod_all, 0)
+    grad_got = from_rows(grad_low)
+    grad_mod_all = step(jnp.concatenate([grad_mod_all, step(mod_got)], 0))
     grad_silu = dot(grad_mod_all, w_ada_flat, NT).reshape(nd, lat_dev * blk)
     grad_silu = exact_dot(place_hot.astype(F32), grad_silu, TN).reshape(nd, lat_dev, blk)
-    grad_silu = lax.all_to_all(grad_silu, "dp", 0, 0)
+    grad_silu = lax.all_to_all(step(grad_silu), "dp", 0, 0)
+    grad_attended, grad_branch, *held = step(
+        grad_attended, grad_branch, *grad_qkvs, *grad_hiddens
+    )
+    grad_qkvs, grad_hiddens = held[:nm], held[nm:]
+    bias_wide_sums = step(jnp.stack([column_sums(grad_attended), column_sums(grad_branch)]))
+    grad_silu = step(grad_silu)
     grad_silu = jnp.swapaxes(grad_silu, 0, 1).reshape(lat_dev, nm, own)
-    grad_silu = sum(
+    silu_got = [
         over_mp(lax.dynamic_index_in_dim(grad_silu, m ^ s, 1, keepdims=False), s) for s in shifts
-    )
-    cond_grad = jax.vjp(jax.nn.silu, condition.astype(F32))[1](grad_silu)[0]
-
-    wide = jnp.stack([column_sums(grad_attended), column_sums(grad_branch)])
+    ]
     bias_own = 0.0
     for s in shifts:
-        narrow = exact_dot(wide, spreads[s].astype(F32), NT)
+        narrow = exact_dot(bias_wide_sums, spreads[s].astype(F32), NT)
         piece = jnp.concatenate(
             [
                 column_sums(grad_qkvs[s][:, :own]),
@@ -570,24 +622,44 @@
                 narrow.reshape(-1),
             ]
         )
-        bias_own = bias_own + over_mp(piece, s)
-    for bit in bits:
-        bias_own = bias_own + over_dp(bias_own, bit)
+        bias_own = bias_own + step(over_mp(piece, s))
+    bias_gots = [over_far(bias_own, p) for p in range(1, zb)]
+    taken = jnp.sum(hot.astype(F32), axis=1)[:, None, :] > 0.5
+
+    def put(got):
+        return lax.dot_general(
+            regroup(got), hot, (((1,), (1,)), ((0,), (0,))), preferred_element_type=F32
+        )
+
+    sum_ada = dot(silu_low, grad_mod_all, TN).reshape(blk, 6, own)
+    grad_b_ada = jnp.sum(grad_mod_all.astype(F32), axis=0).reshape(6, own)
+    sum_ada, grad_b_ada = step(sum_ada, grad_b_ada)
+    for v in bias_gots:
+        bias_own = bias_own + step(v)
+    bias_got = over_dp(bias_own, 1)
+    output = jnp.where(taken, put(fresh_got), inputs.astype(F32)).astype(BF)
+    output = step(output)
+    bias_own = step(bias_own + bias_got)
+    bias_got = over_dp(bias_own, 0)
+    sum_two, sum_one = step(sum_two, sum_one)
+    sum_two, sum_one = sum_two.astype(F32), sum_one.astype(F32)
+    total = far_kept.astype(F32)
+    for v in far_got:
+        total = total + v.astype(F32)
+    total = step(total)
+    input_grad = jnp.where(
+        taken, put(later(grad_got)), cotangent.astype(F32) * row_scale[:, None, None]
+    )
+    input_grad = step(input_grad)
+    bias_own = bias_own + bias_got
+    cond_grad = jax.vjp(jax.nn.silu, condition.astype(F32))[1](sum(silu_got))[0]
+    sum_qkv, sum_out = total[:, : 3 * own].reshape(blk, 3, own), total[:, 3 * own :]
+
     out_b_qv = bias_own[: 2 * own].reshape(2, own)
     out_b_one = bias_own[2 * own : 2 * own + ff]
     out_b_out = bias_own[2 * own + ff : 3 * own + ff]
     out_b_two = bias_own[3 * own + ff :]
 
-    def put(got):
-        return lax.dot_general(
-            regroup(got), hot, (((1,), (1,)), ((0,), (0,))), preferred_element_type=F32
-        )
-
-    taken = jnp.sum(hot.astype(F32), axis=1)[:, None, :] > 0.5
-    output = jnp.where(taken, put(fresh_got), inputs.astype(F32)).astype(BF)
-    input_grad = jnp.where(
-        taken, put(grad_got), cotangent.astype(F32) * row_scale[:, None, None]
-    )
     return (
         output,
         input_grad,

time: 752 us -> 607 us (0.81)
  waiting for transfers between devices: 198 us -> 83.7 us
  local copies, waits for them, and re-layouts: 99.5 us -> 58.6 us
  starting transfers between devices: 55.4 us -> 69 us
    ppermute x57 -> x70, waiting for transfers between devices: 186 us -> 75.4 us  [the longest x20 29.6 us: over_mp(): return lax.ppermute(step(v), 'mp', [(i, i ^ s) for i in range(nm)])]
    concatenate x17 -> x4, other arithmetic: 26.3 us -> 1.71 us  [the longest x1 0.91 us: local(): grad_mod_all = step(jnp.concatenate([mod_back, *mod_gots], 0))]
    another operation x1 -> x10, other arithmetic: 0.03 us -> 20.7 us  [the longest x8 20.6 us: join(): jnp.stack([first[0], second[0], first[1], second[1]]).reshape(full, -1)]
    slice x17 -> x14, local copies, waits for them, and re-layouts: 26.8 us -> 9.88 us  [the longest x6 4.24 us: y_send(): return over_dp(v[near:], 1)]
    ppermute x57 -> x70, starting transfers between devices: 44.9 us -> 58.7 us  [the longest x20 22.9 us: over_mp(): return lax.ppermute(step(v), 'mp', [(i, i ^ s) for i in range(nm)])]
    unnamed x309 -> x254, local copies, waits for them, and re-layouts: 22.8 us -> 12.3 us
  transfers between devices with their start and end apart: 64 -> 77, of which waited for: 27 -> 23; matrix products, arithmetic and copies ran while one was open for 50% -> 56% of each run, Pallas kernels for 7% -> 9%
where the time goes in v2:
time: 607 us; the launch traced here: 602 us
  matrix products  220 us (36%)
  other arithmetic  101 us (17%)
  waiting for transfers between devices  83.7 us (14%)
  starting transfers between devices  69 us (11%)
  local copies, waits for them, and re-layouts  58.6 us (10%)
  Pallas kernels  51.2 us (8%)
  between operations  19.1 us (3%)
    dot_general x54, matrix products, dot(): lax.dot_general(left, right, (dims, ((), ())), preferred_element_type=kind)  200 us
    ppermute x20, waiting for transfers between devices, over_mp(): return lax.ppermute(step(v), 'mp', [(i, i ^ s) for i in range(nm)])  29.6 us
    pallas_call x2, Pallas kernels, attend_back(): pl.pallas_call(partial(attend_back_kernel, own // HD), out_shape=jax.Shap...  26.9 us
    ppermute x38, waiting for transfers between devices, over_dp(): return lax.ppermute(step(v), 'dp', [(i, i ^ 1 << bit) for i in range(nd)])  24.9 us
    pallas_call x2, Pallas kernels, attend(): pl.pallas_call(partial(attend_kernel, own // HD), out_shape=jax.ShapeDtyp...  24.3 us
    ppermute x20, starting transfers between devices, over_mp(): return lax.ppermute(step(v), 'mp', [(i, i ^ s) for i in range(nm)])  22.9 us
    another operation x8, other arithmetic, join(): jnp.stack([first[0], second[0], first[1], second[1]]).reshape(full, -1)  20.6 us
    ppermute x38, starting transfers between devices, over_dp(): return lax.ppermute(step(v), 'dp', [(i, i ^ 1 << bit) for i in range(nd)])  18.1 us
  transfers between devices with their start and end apart: 77, of which 23 were waited for; matrix products, arithmetic and copies ran while one was open for 56% of the time, Pallas kernels for 9%

profile of v2, /device:TPU:0, one launch (start us, length us, event | category | flops | bytes accessed | tf_op | source)
XLA Modules:
  0.0 602.2 jit_solution(5211592973974564483)
XLA Ops:
  24.9 6.4 %all-to-all-start = ((bf16[16,8,80]{2,1,0:T(8,128)(2,1)}), bf16[16,8,80]{2,1,0:T(8,128)(2,1)S(1)}, u32[]{:S(2)}, u32[]{:S(2)}) async-start(bf16[16,8,80]{2,1,0:T(8,128)(2,1)} %copy.92), calls=%async_computation | async-start | bytes 65536 | tf_op jit(solution)/shard_map/all_to_all | solution.py:251
  32.2 6.3 %all-to-all-done = bf16[16,8,80]{2,1,0:T(8,128)(2,1)S(1)} async-done(((bf16[16,8,80]{2,1,0:T(8,128)(2,1)}), bf16[16,8,80]{2,1,0:T(8,128)(2,1)S(1)}, u32[]{:S(2)}, u32[]{:S(2)}) %all-to-all-start) | async-done | bytes 20512 | tf_op jit(solution)/shard_map/all_to_all | solution.py:251
  47.0 5.8 convolution_add_fusion.1
  62.0 7.1 %collective-permute-done.4 = f32[8,3456]{1,0:T(8,128)S(1)} collective-permute-done((f32[8,3456]{1,0:T(8,128)S(1)}, f32[8,3456]{1,0:T(8,128)S(1)}, u32[]{:S(2)}, u32[]{:S(2)}) %collective-permute-start.4) | collective-permute-done | bytes 110624 | tf_op jit(solution)/shard_map/ppermute | solution.py:276
  79.2 12.0 %collective-permute-done.7 = f32[24,576]{1,0:T(8,128)S(1)} collective-permute-done((f32[24,576]{1,0:T(8,128)S(1)}, f32[24,576]{1,0:T(8,128)S(1)}, u32[]{:S(2)}, u32[]{:S(2)}) %collective-permute-start.7) | collective-permute-done | bytes 55328 | tf_op jit(solution)/shard_map/ppermute | solution.py:160
  111.6 12.0 %shard_map.255 = bf16[768,576]{1,0:T(8,128)(2,1)S(1)} custom-call(s32[4]{0:T(128)S(1)} %dynamic_slice.79.counts, bf16[768,2304]{1,0:T(8,128)(2,1)S(1)} %add_convert_fusion.1.qkv_ref), custom_call_target="tpu_custom_call" | custom-call | tf_op jit(solution)/shard_map/pallas_call | solution.py:87
  146.7 12.3 %shard_map.256 = bf16[768,576]{1,0:T(8,128)(2,1)S(1)} custom-call(s32[4]{0:T(128)S(1)} %dynamic_slice.79.counts, bf16[768,2304]{1,0:T(8,128)(2,1)S(1)} %add_convert_fusion.qkv_ref), custom_call_target="tpu_custom_call" | custom-call | tf_op jit(solution)/shard_map/pallas_call | solution.py:87
  181.4 10.3 %multiply_add_fusion.1 = (f32[768,2304]{1,0:T(8,128)}, bf16[768,2304]{1,0:T(8,128)(2,1)}) fusion(f32[2304]{0:T(1024)S(1)} %convert_element_type.299, bf16[768,1152]{1,0:T(8,128)(2,1)S(1)} %fusion.15, bf16[1152,2304]{1,0:T(8,128)(2,1)S(1)} %bitcast.357), kind=kOutput, calls=%fused_computation.6 | convolution fusion | flops 4110483456 | bytes 17703936 | tf_op jit(solution)/shard_map/dot_general | solution.py:21
  191.7 6.9 %collective-permute-done.23 = bf16[288,2304]{1,0:T(8,128)(2,1)S(1)} collective-permute-done((bf16[288,2304]{1,0:T(8,128)(2,1)}, bf16[288,2304]{1,0:T(8,128)(2,1)S(1)}, u32[]{:S(2)}, u32[]{:S(2)}) %collective-permute-start.23) | collective-permute-done | bytes 1327136 | tf_op jit(solution)/shard_map/ppermute | solution.py:160
  213.4 10.2 %convolution_add_fusion.6 = f32[768,1152]{1,0:T(8,128)} fusion(bf16[768,2304]{1,0:T(8,128)(2,1)} %get-tuple-element.315, bf16[1152,2304]{1,0:T(8,128)(2,1)} %bitcast.363, f32[1152]{0:T(1024)S(1)} %get-tuple-element.555), kind=kOutput, calls=%fused_computation.51 | convolution fusion | flops 4077748224 | bytes 12390912 | tf_op jit(solution)/shard_map/dot_general | solution.py:21
  228.7 9.9 %multiply_add_fusion = (f32[768,2304]{1,0:T(8,128)}, bf16[768,2304]{1,0:T(8,128)(2,1)S(1)}) fusion(f32[2304]{0:T(1024)S(1)} %reshape.440, bf16[768,1152]{1,0:T(8,128)(2,1)S(1)} %copy-done.44, bf16[1152,2304]{1,0:T(8,128)(2,1)S(1)} %bitcast.361), kind=kOutput, calls=%fused_computation.2 | convolution fusion | flops 4110483456 | bytes 17703936 | tf_op jit(solution)/shard_map/dot_general | solution.py:21
  250.3 8.0 %convolution_add_fusion.5 = f32[768,1152]{1,0:T(8,128)} fusion(f32[768,1152]{1,0:T(8,128)} %convolution_add_fusion.6, bf16[768,2304]{1,0:T(8,128)(2,1)S(1)} %get-tuple-element.329, bf16[1152,2304]{1,0:T(8,128)(2,1)S(1)} %bitcast.367), kind=kOutput, calls=%fused_computation.50 | convolution fusion | flops 4077748224 | bytes 15925248 | tf_op jit(solution)/shard_map/dot_general | solution.py:21
  268.0 7.2 %multiply_convert_fusion.1 = bf16[768,2304]{1,0:T(8,128)(2,1)S(1)} fusion(f32[768,2304]{1,0:T(8,128)} %get-tuple-element.330, bf16[768,1152]{1,0:T(8,128)(2,1)S(1)} %get-tuple-element.459, bf16[1152,2304]{1,0:T(8,128)(2,1)S(1)} %bitcast.368), kind=kOutput, calls=%fused_computation.1 | convolution fusion | flops 4080402432 | bytes 17694720 | tf_op jit(solution)/shard_map/dot_general | solution.py:21
  275.2 6.4 %add_convert_fusion.5 = bf16[576,2304]{1,0:T(8,128)(2,1)S(1)} fusion(bf16[576,2304]{1,0:T(8,128)(2,1)} %collective-permute-done.33, bf16[768,576]{1,0:T(8,128)(2,1)S(1)} %get-tuple-element.341, bf16[768,2304]{1,0:T(8,128)(2,1)} %copy-done.53), kind=kOutput, calls=%fused_computation.31 | convolution fusion | flops 2042413056 | bytes 9732096 | tf_op jit(solution)/shard_map/dot_general | solution.py:21
  281.7 7.5 %multiply_convert_fusion = bf16[768,2304]{1,0:T(8,128)(2,1)S(1)} fusion(f32[768,2304]{1,0:T(8,128)} %get-tuple-element.316, bf16[768,1152]{1,0:T(8,128)(2,1)S(1)} %get-tuple-element.459, bf16[1152,2304]{1,0:T(8,128)(2,1)S(1)} %bitcast.366), kind=kOutput, calls=%fused_computation | convolution fusion | flops 4080402432 | bytes 17694720 | tf_op jit(solution)/shard_map/dot_general | solution.py:21
  289.2 6.4 %add_convert_fusion.4 = bf16[576,2304]{1,0:T(8,128)(2,1)S(1)} fusion(bf16[576,2304]{1,0:T(8,128)(2,1)} %collective-permute-done.32, bf16[768,576]{1,0:T(8,128)(2,1)S(1)} %get-tuple-element.341, bf16[768,2304]{1,0:T(8,128)(2,1)} %get-tuple-element.315), kind=kOutput, calls=%fused_computation.30 | convolution fusion | flops 2042413056 | bytes 9732096 | tf_op jit(solution)/shard_map/dot_general | solution.py:21
  315.5 6.8 %fusion.171 = f32[768,1152]{1,0:T(8,128)} fusion(bf16[768,2304]{1,0:T(8,128)(2,1)S(1)} %multiply_convert_fusion, bf16[1152,2304]{1,0:T(8,128)(2,1)S(1)} %bitcast.360), kind=kOutput, calls=%fused_computation.381 | convolution fusion | flops 4076863488 | bytes 12386304 | tf_op jit(solution)/shard_map/dot_general | solution.py:21
  322.3 8.4 %convolution_add_fusion.4 = f32[768,1152]{1,0:T(8,128)S(1)} fusion(f32[768,1152]{1,0:T(8,128)} %fusion.171, bf16[768,2304]{1,0:T(8,128)(2,1)S(1)} %multiply_convert_fusion.1, bf16[1152,2304]{1,0:T(8,128)(2,1)} %bitcast.362), kind=kOutput, calls=%fused_computation.49 | convolution fusion | flops 4077748224 | bytes 15925248 | tf_op jit(solution)/shard_map/dot_general | solution.py:21
  374.2 13.5 %shard_map.257 = bf16[768,1728]{1,0:T(8,128)(2,1)S(1)} custom-call(s32[4]{0:T(128)S(1)} %copy-done.10, bf16[768,2304]{1,0:T(8,128)(2,1)S(1)} %copy-done.3, bf16[768,576]{1,0:T(8,128)(2,1)S(1)} %copy.97.g_ref), custom_call_target="tpu_custom_call" | custom-call | tf_op jit(solution)/shard_map/pallas_call | solution.py:106
  393.5 13.5 %shard_map.258 = bf16[768,1728]{1,0:T(8,128)(2,1)S(1)} custom-call(s32[4]{0:T(128)S(1)} %copy-done.10, bf16[768,2304]{1,0:T(8,128)(2,1)S(1)} %copy-done.1, bf16[768,576]{1,0:T(8,128)(2,1)S(1)} %copy-done.6), custom_call_target="tpu_custom_call" | custom-call | tf_op jit(solution)/shard_map/pallas_call | solution.py:106
  445.5 5.7 fusion.4
  459.7 7.5 %fusion.6 = f32[768,1152]{1,0:T(8,128)S(1)} fusion(f32[768,1152]{1,0:T(8,128)} %fusion.4, bf16[768,1728]{1,0:T(8,128)(2,1)S(1)} %copy-done.5, bf16[1152,2304]{1,0:T(8,128)(2,1)} %bitcast.350), kind=kOutput, calls=%fused_computation.48 | convolution fusion | flops 3058532352 | bytes 13860864 | tf_op jit(solution)/shard_map/dot_general | solution.py:21
  518.6 5.8 add_convert_fusion.8
  530.5 6.2 %collective-permute-done.65 = bf16[72,2304]{1,0:T(8,128)(2,1)S(1)} collective-permute-done((bf16[72,2304]{1,0:T(8,128)(2,1)S(1)}, bf16[72,2304]{1,0:T(8,128)(2,1)S(1)}, u32[]{:S(2)}, u32[]{:S(2)}) %collective-permute-start.65) | collective-permute-done | bytes 331808 | tf_op jit(solution)/shard_map/ppermute | solution.py:590
  (632 shorter events, 381.4 us)
Async XLA Ops:
  7.2 39.8 %all-gather.4.cloned.1.call-start = ((), (), s32[]{:S(2)}) async-start(), calls=%async_computation.4 | async-start | bytes 1658880 | tf_op jit(solution)/shard_map/all_gather | solution.py:206
  10.3 80.9 %all-gather.6.cloned.1.call-start = ((), (), s32[]{:S(2)}) async-start(), calls=%async_computation.5 | async-start | bytes 1658880 | tf_op jit(solution)/shard_map/all_gather | solution.py:206
  11.1 121.1 %all-gather.8.cloned.1.call-start = ((), (), s32[]{:S(2)}) async-start(), calls=%async_computation.6 | async-start | bytes 1658880 | tf_op jit(solution)/shard_map/all_gather | solution.py:206
  31.3 550.2 %reduce-scatter.5.cloned.1.call-start = ((), (), s32[]{:S(2)}) async-start(), calls=%async_computation.8 | async-start | bytes 1658880 | tf_op jit(solution)/shard_map/reduce_scatter | solution.py:467
  69.2 32.1 %collective-permute-start.10 = (bf16[288,2304]{1,0:T(8,128)(2,1)}, bf16[288,2304]{1,0:T(8,128)(2,1)}, u32[]{:S(2)}, u32[]{:S(2)}) collective-permute-start(bf16[288,2304]{1,0:T(8,128)(2,1)} %all-gather.4.cloned.1.call-done), channel_id=1, source_target_pairs={{0,2},{2,0},{4,6},{6,4},{8,10},{10,8},{12,14},{14,12},{16,18},{18,... | collective-permute-start | bytes 3981320 | tf_op jit(solution)/shard_map/ppermute | solution.py:155
  99.0 31.9 %collective-permute-start.12 = (bf16[288,2304]{1,0:T(8,128)(2,1)}, bf16[288,2304]{1,0:T(8,128)(2,1)}, u32[]{:S(2)}, u32[]{:S(2)}) collective-permute-start(bf16[288,2304]{1,0:T(8,128)(2,1)} %collective-permute-done.8), channel_id=1, source_target_pairs={{0,1},{1,0},{2,3},{3,2},{4,5},{5,4},{6,7},{7,6},{8,9},{9,8},{10,11... | collective-permute-start | bytes 3981320 | tf_op jit(solution)/shard_map/ppermute | solution.py:160
  100.7 31.6 %collective-permute-start.13 = (bf16[288,2304]{1,0:T(8,128)(2,1)}, bf16[288,2304]{1,0:T(8,128)(2,1)}, u32[]{:S(2)}, u32[]{:S(2)}) collective-permute-start(bf16[288,2304]{1,0:T(8,128)(2,1)} %all-gather.6.cloned.1.call-done), channel_id=1, source_target_pairs={{0,4},{2,6},{4,0},{6,2},{8,12},{10,14},{12,8},{14,10},{16,20},{18,... | collective-permute-start | bytes 3981320 | tf_op jit(solution)/shard_map/ppermute | solution.py:155
  133.9 33.4 %collective-permute-start.16 = (bf16[288,2304]{1,0:T(8,128)(2,1)}, bf16[288,2304]{1,0:T(8,128)(2,1)}, u32[]{:S(2)}, u32[]{:S(2)}) collective-permute-start(bf16[288,2304]{1,0:T(8,128)(2,1)} %all-gather.6.cloned.1.call-done), channel_id=1, source_target_pairs={{0,1},{1,0},{2,3},{3,2},{4,5},{5,4},{6,7},{7,6},{8,9},{9,8},{10,11... | collective-permute-start | bytes 3981320 | tf_op jit(solution)/shard_map/ppermute | solution.py:160
  134.4 32.9 %collective-permute-start.17 = (bf16[288,2304]{1,0:T(8,128)(2,1)}, bf16[288,2304]{1,0:T(8,128)(2,1)}, u32[]{:S(2)}, u32[]{:S(2)}) collective-permute-start(bf16[288,2304]{1,0:T(8,128)(2,1)} %all-gather.8.cloned.1.call-done), channel_id=1, source_target_pairs={{0,4},{2,6},{4,0},{6,2},{8,12},{10,14},{12,8},{14,10},{16,20},{18,... | collective-permute-start | bytes 3981320 | tf_op jit(solution)/shard_map/ppermute | solution.py:155
  167.3 31.3 %collective-permute-start.23 = (bf16[288,2304]{1,0:T(8,128)(2,1)}, bf16[288,2304]{1,0:T(8,128)(2,1)S(1)}, u32[]{:S(2)}, u32[]{:S(2)}) collective-permute-start(bf16[288,2304]{1,0:T(8,128)(2,1)} %all-gather.8.cloned.1.call-done), channel_id=1, source_target_pairs={{0,1},{1,0},{2,3},{3,2},{4,5},{5,4},{6,7},{7,6},{8,9},{9,8},{10,11... | collective-permute-start | bytes 3981320 | tf_op jit(solution)/shard_map/ppermute | solution.py:160
  174.6 31.1 %collective-permute-start.22 = (bf16[288,2304]{1,0:T(8,128)(2,1)}, bf16[288,2304]{1,0:T(8,128)(2,1)}, u32[]{:S(2)}, u32[]{:S(2)}) collective-permute-start(bf16[288,2304]{1,0:T(8,128)(2,1)} %collective-permute-done.16), channel_id=1, source_target_pairs={{0,4},{2,6},{4,0},{6,2},{8,12},{10,14},{12,8},{14,10},{16,20},{18,... | collective-permute-start | bytes 3981320 | tf_op jit(solution)/shard_map/ppermute | solution.py:155
  206.2 32.4 %collective-permute-start.26 = (bf16[288,768]{1,0:T(8,128)(2,1)}, bf16[288,768]{1,0:T(8,128)(2,1)}, u32[]{:S(2)}, u32[]{:S(2)}) collective-permute-start(bf16[288,768]{1,0:T(8,128)(2,1)} %slice.355), channel_id=1, source_target_pairs={{0,1},{1,0},{2,3},{3,2},{4,5},{5,4},{6,7},{7,6},{8,9},{9,8},{10,11... | collective-permute-start | bytes 1327112 | tf_op jit(solution)/shard_map/ppermute | solution.py:160
  206.7 32.0 %collective-permute-start.27 = (bf16[288,1536]{1,0:T(8,128)(2,1)}, bf16[288,1536]{1,0:T(8,128)(2,1)}, u32[]{:S(2)}, u32[]{:S(2)}) collective-permute-start(bf16[288,1536]{1,0:T(8,128)(2,1)} %slice.354), channel_id=1, source_target_pairs={{0,4},{2,6},{4,0},{6,2},{8,12},{10,14},{12,8},{14,10},{16,20},{18,... | collective-permute-start | bytes 2654216 | tf_op jit(solution)/shard_map/ppermute | solution.py:155
  303.9 32.0 %collective-permute-start.37 = (bf16[288,2304]{1,0:T(8,128)(2,1)S(1)}, bf16[288,2304]{1,0:T(8,128)(2,1)}, u32[]{:S(2)}, u32[]{:S(2)}) collective-permute-start(bf16[288,2304]{1,0:T(8,128)(2,1)S(1)} %slice.365), channel_id=1, source_target_pairs={{0,4},{2,6},{4,0},{6,2},{8,12},{10,14},{12,8},{14,10},{16,20},{18,... | collective-permute-start | bytes 3981320 | tf_op jit(solution)/shard_map/ppermute | solution.py:155
  304.5 59.6 %collective-permute-start.40 = (bf16[288,2304]{1,0:T(8,128)(2,1)}, bf16[288,2304]{1,0:T(8,128)(2,1)}, u32[]{:S(2)}, u32[]{:S(2)}) collective-permute-start(bf16[288,2304]{1,0:T(8,128)(2,1)} %slice.366), channel_id=1, source_target_pairs={{0,4},{2,6},{4,0},{6,2},{8,12},{10,14},{12,8},{14,10},{16,20},{18,... | collective-permute-start | bytes 3981320 | tf_op jit(solution)/shard_map/ppermute | solution.py:155
  310.0 57.4 %collective-permute-start.39 = (bf16[288,2304]{1,0:T(8,128)(2,1)}, bf16[288,2304]{1,0:T(8,128)(2,1)}, u32[]{:S(2)}, u32[]{:S(2)}) collective-permute-start(bf16[288,2304]{1,0:T(8,128)(2,1)} %get-tuple-element.362), channel_id=1, source_target_pairs={{0,1},{1,0},{2,3},{3,2},{4,5},{5,4},{6,7},{7,6},{8,9},{9,8},{10,11... | collective-permute-start | bytes 3981320 | tf_op jit(solution)/shard_map/ppermute | solution.py:160
  350.5 37.2 %collective-permute-start.36 = (bf16[288,2304]{1,0:T(8,128)(2,1)}, bf16[288,2304]{1,0:T(8,128)(2,1)}, u32[]{:S(2)}, u32[]{:S(2)}) collective-permute-start(bf16[288,2304]{1,0:T(8,128)(2,1)} %get-tuple-element.363), channel_id=1, source_target_pairs={{0,1},{1,0},{2,3},{3,2},{4,5},{5,4},{6,7},{7,6},{8,9},{9,8},{10,11... | collective-permute-start | bytes 3981320 | tf_op jit(solution)/shard_map/ppermute | solution.py:160
  357.2 54.3 %collective-permute-start.42 = (bf16[288,2304]{1,0:T(8,128)(2,1)}, bf16[288,2304]{1,0:T(8,128)(2,1)}, u32[]{:S(2)}, u32[]{:S(2)}) collective-permute-start(bf16[288,2304]{1,0:T(8,128)(2,1)} %add_convert_fusion.15), channel_id=1, source_target_pairs={{0,1},{1,0},{2,3},{3,2},{4,5},{5,4},{6,7},{7,6},{8,9},{9,8},{10,11... | collective-permute-start | bytes 3981320 | tf_op jit(solution)/shard_map/ppermute | solution.py:160
  369.0 41.1 %collective-permute-start.41 = (bf16[288,2304]{1,0:T(8,128)(2,1)S(1)}, bf16[288,2304]{1,0:T(8,128)(2,1)S(1)}, u32[]{:S(2)}, u32[]{:S(2)}) collective-permute-start(bf16[288,2304]{1,0:T(8,128)(2,1)S(1)} %add_convert_fusion.13), channel_id=1, source_target_pairs={{0,4},{2,6},{4,0},{6,2},{8,12},{10,14},{12,8},{14,10},{16,20},{18,... | collective-permute-start | bytes 3981320 | tf_op jit(solution)/shard_map/ppermute | solution.py:155
  414.7 166.8 %reduce-scatter.3.cloned.1.call-start = ((), (), s32[]{:S(2)}) async-start(), calls=%async_computation.7 | async-start | bytes 1658880 | tf_op jit(solution)/shard_map/reduce_scatter | solution.py:467
  432.8 34.5 %collective-permute-start.48 = (bf16[576,576]{1,0:T(8,128)(2,1)S(1)}, bf16[576,576]{1,0:T(8,128)(2,1)}, u32[]{:S(2)}, u32[]{:S(2)}) collective-permute-start(bf16[576,576]{1,0:T(8,128)(2,1)S(1)} %slice.379), channel_id=1, source_target_pairs={{0,1},{1,0},{2,3},{3,2},{4,5},{5,4},{6,7},{7,6},{8,9},{9,8},{10,11... | collective-permute-start | bytes 1990664 | tf_op jit(solution)/shard_map/ppermute | solution.py:160
  456.5 32.5 %collective-permute-start.50 = (bf16[288,1152]{1,0:T(8,128)(2,1)}, bf16[288,1152]{1,0:T(8,128)(2,1)}, u32[]{:S(2)}, u32[]{:S(2)}) collective-permute-start(bf16[288,1152]{1,0:T(8,128)(2,1)} %add_convert_fusion.19), channel_id=1, source_target_pairs={{0,1},{1,0},{2,3},{3,2},{4,5},{5,4},{6,7},{7,6},{8,9},{9,8},{10,11... | collective-permute-start | bytes 1990664 | tf_op jit(solution)/shard_map/ppermute | solution.py:160
  458.6 32.0 %collective-permute-start.52 = (bf16[288,1152]{1,0:T(8,128)(2,1)}, bf16[288,1152]{1,0:T(8,128)(2,1)}, u32[]{:S(2)}, u32[]{:S(2)}) collective-permute-start(bf16[288,1152]{1,0:T(8,128)(2,1)} %slice.381), channel_id=1, source_target_pairs={{0,4},{2,6},{4,0},{6,2},{8,12},{10,14},{12,8},{14,10},{16,20},{18,... | collective-permute-start | bytes 1990664 | tf_op jit(solution)/shard_map/ppermute | solution.py:155
  529.9 59.2 %collective-permute-start.63 = (bf16[4,192,576]{2,1,0:T(8,128)(2,1)}, bf16[4,192,576]{2,1,0:T(8,128)(2,1)}, u32[]{:S(2)}, u32[]{:S(2)}) collective-permute-start(bf16[4,192,576]{2,1,0:T(8,128)(2,1)} %bitcast.96), channel_id=1, source_target_pairs={{0,1},{1,0},{2,3},{3,2},{4,5},{5,4},{6,7},{7,6},{8,9},{9,8},{10,11... | collective-permute-start | bytes 2654216 | tf_op jit(solution)/shard_map/ppermute | solution.py:160
  (174 other events, 2655.8 us)
Sparse Core Ops, SparseCore 0:
  10.5 36.4 all-gather.3
  48.5 40.6 all-gather.5
  90.8 31.3 all-gather.7
  414.9 29.5 reduce-scatter.4
  446.6 30.4 reduce-scatter.2

commit v3 on v2

--- a/solution.py
+++ b/solution.py
@@ -293,6 +293,11 @@
     part = step(part_add(part, step(got)))
     part_gots = [over_far(part[p], p) for p in range(1, zb)]
     a_zc = core_pair(a_z)
+    cot_picked = step(pick(step(cotangent)))
+    cot_parts = step(*[group_of(cot_picked, s).reshape(rows, own) for s in shifts])
+    cot_parts = cot_parts if nm > 1 else [cot_parts]
+    a_xs = later(a_xs)
+    a_y = step(a_y)
     modulation = part[0] + b_ada.astype(F32).reshape(6 * own)
     for v in part_gots:
         modulation = modulation + step(v)
@@ -305,16 +310,11 @@
         )
 
     mod_got = [over_mp(mod_group(s), s) for s in shifts]
-    cot_picked = step(pick(step(cotangent)))
-    cot_parts = step(*[group_of(cot_picked, s).reshape(rows, own) for s in shifts])
-    cot_parts = cot_parts if nm > 1 else [cot_parts]
-    mod_got = later(mod_got)
-    a_xs = later(a_xs)
-    a_y = step(a_y)
     a_xys = [over_mp(a_y, s) for s in shifts]
     one_z = step(one_z)
     one_y = over_dp(one_z, 1)
     a_yc = core_pair(a_y)
+    mod_got = later(mod_got)
     mod_rows = sum(
         exact_dot(v, p.astype(F32), NN) for v, p in zip(mod_got, spreads)
     ).reshape(6, mine, full)
@@ -421,11 +421,12 @@
             for t in shifts[1:]:
                 ends = [core_pair(step(v)) for v in two_xys[t]]
                 g_two[t] = (core_pair(two_xs[t]), ends)
-            cot_got = later(cot_got)
         first, second = g_two[s]
         if s:
             second = [(v[0], step(v[1])) for v in second]
             second = [jnp.concatenate([v[k] for v in second], axis=1) for k in range(2)]
+            if s == 1:
+                cot_got = later(cot_got)
         else:
             second = (second[0], step(second[1]))
         w2t.append(join((first[0], step(first[1])), second))
@@ -491,9 +492,6 @@
     for s in shifts:
         piece = dot(step(grad_hiddens[s]), w1[s], NT)
         grad_second = step(piece if grad_second is None else grad_second + piece)
-    for s in order[:-1]:
-        two_y[s] = step(y_add(two_kept[s], step(two_y_got[s])))
-        two_x_got[s] = over_mp(two_y[s], s)
     grad_second = cubes(step(grad_second))
     grad_shift_two = jnp.sum(grad_second, axis=1)
     grad_scale_two = jnp.sum(grad_second * normed_two, axis=1)
@@ -506,6 +504,9 @@
     )
     out_got = over_dp(step(dot(high, mixture_all, TN, BF)), 0)
     grad_mixtures = [step(dot(step(grad_attended), w, NN, BF)) for w in wo_t]
+    for s in order[:-1]:
+        two_y[s] = step(y_add(two_kept[s], step(two_y_got[s])))
+        two_x_got[s] = over_mp(two_y[s], s)
     two_y[0] = step(y_add(two_kept[0], step(two_y_got[0])))
     one_high = step(x_add([one_kept[0][near:]], [step(v[0]) for v in one_x_got.values()]))
     one_y_got = over_dp(one_high, 1)
@@ -533,15 +534,14 @@
         qk_y_got[s] = y_send(qk_kept[s])
         if s:
             v_x_got[s] = over_mp(v_kept[s], s)
+    w_qkvs = [w[:, : 3 * own] for w in w_as]
+    grad_first = step(dot(step(grad_qkvs[0]), w_qkvs[0], NT))
+    for s in shifts[1:]:
+        grad_first = step(grad_first + dot(step(grad_qkvs[s]), w_qkvs[s], NT))
     out_y = step(y_add(out_kept, step(out_y_got)))
     out_x_got = [over_mp(out_y[:, s * own : (s + 1) * own], s) for s in shifts[1:]]
-    w_qkvs = [w[:, : 3 * own] for w in w_as]
-    grad_first = step(dot(step(grad_qkvs[0]), w_qkvs[0], NT))
-    fresh_got = later(fresh_got)
     qk_y[last] = step(y_add(qk_kept[last], step(qk_y_got[last])))
     qk_x_got = {last: over_mp(qk_y[last], last)} if last else {}
-    for s in shifts[1:]:
-        grad_first = step(grad_first + dot(step(grad_qkvs[s]), w_qkvs[s], NT))
     v_x = step(x_add(v_kept, [step(v) for v in v_x_got.values()]))
     v_y_got = y_send(v_x)
     grad_first = cubes(step(grad_first))
@@ -560,14 +560,15 @@
         ],
         axis=1,
     ).astype(BF)
+    fresh_got = later(fresh_got)
     grad_mod = step(grad_mod.reshape(mine * 6, full))
-    if last:
-        qk_x_got[last] = step(qk_x_got[last])
-    out_x_got = [step(v) for v in out_x_got]
     mod_back = [
         over_mp(dot(grad_mod, p, NT, BF).reshape(mine, 6 * own), s)
         for s, p in enumerate(spreads)
     ]
+    if last:
+        qk_x_got[last] = step(qk_x_got[last])
+    out_x_got = [step(v) for v in out_x_got]
     for s in order[1:]:
         qk_y[s] = step(y_add(qk_kept[s], step(qk_y_got[s])))
         if s:
@@ -623,6 +624,7 @@
             ]
         )
         bias_own = bias_own + step(over_mp(piece, s))
+    far_got = [step(v) for v in far_got]
     bias_gots = [over_far(bias_own, p) for p in range(1, zb)]
     taken = jnp.sum(hot.astype(F32), axis=1)[:, None, :] > 0.5
 
@@ -634,6 +636,10 @@
     sum_ada = dot(silu_low, grad_mod_all, TN).reshape(blk, 6, own)
     grad_b_ada = jnp.sum(grad_mod_all.astype(F32), axis=0).reshape(6, own)
     sum_ada, grad_b_ada = step(sum_ada, grad_b_ada)
+    input_grad = jnp.where(
+        taken, put(later(grad_got)), cotangent.astype(F32) * row_scale[:, None, None]
+    )
+    input_grad = step(input_grad)
     for v in bias_gots:
         bias_own = bias_own + step(v)
     bias_got = over_dp(bias_own, 1)
@@ -647,10 +653,6 @@
     for v in far_got:
         total = total + v.astype(F32)
     total = step(total)
-    input_grad = jnp.where(
-        taken, put(later(grad_got)), cotangent.astype(F32) * row_scale[:, None, None]
-    )
-    input_grad = step(input_grad)
     bias_own = bias_own + bias_got
     cond_grad = jax.vjp(jax.nn.silu, condition.astype(F32))[1](sum(silu_got))[0]
     sum_qkv, sum_out = total[:, : 3 * own].reshape(blk, 3, own), total[:, 3 * own :]

time: 607 us -> 598 us (0.985)
  waiting for transfers between devices: 83.7 us -> 63.9 us
  local copies, waits for them, and re-layouts: 58.6 us -> 67.5 us
    ppermute x9, waiting for transfers between devices: 14.7 us -> 0.02 us  [over_far(): lax.ppermute(step(v), 'dp', [(i, i ^ far_mask(place)) for i in range(nd)])]
    ppermute x3, waiting for transfers between devices: 6.19 us -> 0.01 us  [local(): lax.ppermute(step(v), 'dp', [(i, i ^ k + 1 << 2) for i in range(nd)])]
    unnamed x254 -> x262, local copies, waits for them, and re-layouts: 12.3 us -> 18.4 us
  transfers between devices with their start and end apart: 77 -> 77, of which waited for: 23 -> 14; matrix products, arithmetic and copies ran while one was open for 56% -> 59% of each run, Pallas kernels for 9% -> 9%
where the time goes in v3:
time: 598 us; the launch traced here: 593 us
  matrix products  218 us (36%)
  other arithmetic  106 us (18%)
  local copies, waits for them, and re-layouts  67.5 us (11%)
  starting transfers between devices  67 us (11%)
  waiting for transfers between devices  63.9 us (11%)
  Pallas kernels  51.2 us (9%)
  between operations  19 us (3%)
    dot_general x54, matrix products, dot(): lax.dot_general(left, right, (dims, ((), ())), preferred_element_type=kind)  201 us
    ppermute x20, waiting for transfers between devices, over_mp(): return lax.ppermute(step(v), 'mp', [(i, i ^ s) for i in range(nm)])  28.5 us
    pallas_call x2, Pallas kernels, attend_back(): pl.pallas_call(partial(attend_back_kernel, own // HD), out_shape=jax.Shap...  26.9 us
    ppermute x38, waiting for transfers between devices, over_dp(): return lax.ppermute(step(v), 'dp', [(i, i ^ 1 << bit) for i in range(nd)])  24.8 us
    pallas_call x2, Pallas kernels, attend(): pl.pallas_call(partial(attend_kernel, own // HD), out_shape=jax.ShapeDtyp...  24.3 us
    another operation x8, other arithmetic, join(): jnp.stack([first[0], second[0], first[1], second[1]]).reshape(full, -1)  23 us
    ppermute x20, starting transfers between devices, over_mp(): return lax.ppermute(step(v), 'mp', [(i, i ^ s) for i in range(nm)])  20 us
    ppermute x38, starting transfers between devices, over_dp(): return lax.ppermute(step(v), 'dp', [(i, i ^ 1 << bit) for i in range(nd)])  19 us
  transfers between devices with their start and end apart: 77, of which 14 were waited for; matrix products, arithmetic and copies ran while one was open for 59% of the time, Pallas kernels for 9%

profile of v3, /device:TPU:0, one launch (start us, length us, event | category | flops | bytes accessed | tf_op | source)
XLA Modules:
  0.0 593.3 jit_solution(7977584606592875769)
XLA Ops:
  24.8 6.4 %all-to-all-start = ((bf16[16,8,80]{2,1,0:T(8,128)(2,1)}), bf16[16,8,80]{2,1,0:T(8,128)(2,1)S(1)}, u32[]{:S(2)}, u32[]{:S(2)}) async-start(bf16[16,8,80]{2,1,0:T(8,128)(2,1)} %copy.92), calls=%async_computation | async-start | bytes 65536 | tf_op jit(solution)/shard_map/all_to_all | solution.py:251
  33.1 5.3 all-to-all-done
  50.9 5.6 convolution_add_fusion.1
  68.2 10.8 %collective-permute-done.6 = bf16[288,2304]{1,0:T(8,128)(2,1)S(1)} collective-permute-done((bf16[288,2304]{1,0:T(8,128)(2,1)}, bf16[288,2304]{1,0:T(8,128)(2,1)S(1)}, u32[]{:S(2)}, u32[]{:S(2)}) %collective-permute-start.6) | collective-permute-done | bytes 1327136 | tf_op jit(solution)/shard_map/ppermute | solution.py:160
  79.0 9.3 %collective-permute-done.5 = bf16[288,2304]{1,0:T(8,128)(2,1)} collective-permute-done((bf16[288,2304]{1,0:T(8,128)(2,1)}, bf16[288,2304]{1,0:T(8,128)(2,1)}, u32[]{:S(2)}, u32[]{:S(2)}) %collective-permute-start.5) | collective-permute-done | bytes 1327136 | tf_op jit(solution)/shard_map/ppermute | solution.py:155
  112.3 12.0 %shard_map.255 = bf16[768,576]{1,0:T(8,128)(2,1)S(1)} custom-call(s32[4]{0:T(128)S(1)} %dynamic_slice.79.counts, bf16[768,2304]{1,0:T(8,128)(2,1)S(1)} %add_convert_fusion.1.qkv_ref), custom_call_target="tpu_custom_call" | custom-call | tf_op jit(solution)/shard_map/pallas_call | solution.py:87
  142.9 12.3 %shard_map.256 = bf16[768,576]{1,0:T(8,128)(2,1)S(1)} custom-call(s32[4]{0:T(128)S(1)} %dynamic_slice.79.counts, bf16[768,2304]{1,0:T(8,128)(2,1)S(1)} %add_convert_fusion.qkv_ref), custom_call_target="tpu_custom_call" | custom-call | tf_op jit(solution)/shard_map/pallas_call | solution.py:87
  174.9 10.3 %multiply_add_fusion.1 = (f32[768,2304]{1,0:T(8,128)}, bf16[768,2304]{1,0:T(8,128)(2,1)}) fusion(f32[2304]{0:T(1024)S(1)} %convert_element_type.299, bf16[768,1152]{1,0:T(8,128)(2,1)S(1)} %fusion.15, bf16[1152,2304]{1,0:T(8,128)(2,1)S(1)} %bitcast.359), kind=kOutput, calls=%fused_computation.6 | convolution fusion | flops 4110483456 | bytes 17703936 | tf_op jit(solution)/shard_map/dot_general | solution.py:21
  185.3 8.7 %collective-permute-done.23 = bf16[288,2304]{1,0:T(8,128)(2,1)S(1)} collective-permute-done((bf16[288,2304]{1,0:T(8,128)(2,1)}, bf16[288,2304]{1,0:T(8,128)(2,1)S(1)}, u32[]{:S(2)}, u32[]{:S(2)}) %collective-permute-start.23) | collective-permute-done | bytes 1327136 | tf_op jit(solution)/shard_map/ppermute | solution.py:160
  207.9 10.2 %convolution_add_fusion.6 = f32[768,1152]{1,0:T(8,128)} fusion(bf16[768,2304]{1,0:T(8,128)(2,1)} %get-tuple-element.317, bf16[1152,2304]{1,0:T(8,128)(2,1)} %bitcast.365, f32[1152]{0:T(1024)S(1)} %get-tuple-element.559), kind=kOutput, calls=%fused_computation.51 | convolution fusion | flops 4077748224 | bytes 12390912 | tf_op jit(solution)/shard_map/dot_general | solution.py:21
  221.9 10.4 %multiply_add_fusion = (f32[768,2304]{1,0:T(8,128)}, bf16[768,2304]{1,0:T(8,128)(2,1)}) fusion(f32[2304]{0:T(1024)S(1)} %reshape.440, bf16[768,1152]{1,0:T(8,128)(2,1)S(1)} %copy-done.44, bf16[1152,2304]{1,0:T(8,128)(2,1)S(1)} %bitcast.363), kind=kOutput, calls=%fused_computation.2 | convolution fusion | flops 4110483456 | bytes 17703936 | tf_op jit(solution)/shard_map/dot_general | solution.py:21
  248.7 8.1 %convolution_add_fusion.5 = f32[768,1152]{1,0:T(8,128)} fusion(f32[768,1152]{1,0:T(8,128)} %convolution_add_fusion.6, bf16[768,2304]{1,0:T(8,128)(2,1)S(1)} %copy-done.55, bf16[1152,2304]{1,0:T(8,128)(2,1)S(1)} %bitcast.369), kind=kOutput, calls=%fused_computation.50 | convolution fusion | flops 4077748224 | bytes 15925248 | tf_op jit(solution)/shard_map/dot_general | solution.py:21
  264.9 8.7 %multiply_convert_fusion.1 = bf16[768,2304]{1,0:T(8,128)(2,1)S(1)} fusion(f32[768,2304]{1,0:T(8,128)} %get-tuple-element.332, bf16[768,1152]{1,0:T(8,128)(2,1)S(1)} %get-tuple-element.460, bf16[1152,2304]{1,0:T(8,128)(2,1)} %bitcast.370), kind=kOutput, calls=%fused_computation.1 | convolution fusion | flops 4080402432 | bytes 17694720 | tf_op jit(solution)/shard_map/dot_general | solution.py:21
  273.6 5.3 add_convert_fusion.5
  280.3 7.5 %multiply_convert_fusion = bf16[768,2304]{1,0:T(8,128)(2,1)S(1)} fusion(f32[768,2304]{1,0:T(8,128)} %get-tuple-element.318, bf16[768,1152]{1,0:T(8,128)(2,1)S(1)} %get-tuple-element.460, bf16[1152,2304]{1,0:T(8,128)(2,1)S(1)} %bitcast.368), kind=kOutput, calls=%fused_computation | convolution fusion | flops 4080402432 | bytes 17694720 | tf_op jit(solution)/shard_map/dot_general | solution.py:21
  287.8 5.6 add_convert_fusion.4
  312.0 6.8 %fusion.171 = f32[768,1152]{1,0:T(8,128)} fusion(bf16[768,2304]{1,0:T(8,128)(2,1)S(1)} %multiply_convert_fusion, bf16[1152,2304]{1,0:T(8,128)(2,1)S(1)} %bitcast.362), kind=kOutput, calls=%fused_computation.381 | convolution fusion | flops 4076863488 | bytes 12386304 | tf_op jit(solution)/shard_map/dot_general | solution.py:21
  318.9 8.5 %convolution_add_fusion.4 = f32[768,1152]{1,0:T(8,128)S(1)} fusion(f32[768,1152]{1,0:T(8,128)} %fusion.171, bf16[768,2304]{1,0:T(8,128)(2,1)S(1)} %multiply_convert_fusion.1, bf16[1152,2304]{1,0:T(8,128)(2,1)} %bitcast.364), kind=kOutput, calls=%fused_computation.49 | convolution fusion | flops 4077748224 | bytes 15925248 | tf_op jit(solution)/shard_map/dot_general | solution.py:21
  329.3 5.2 fusion.10
  372.0 13.5 %shard_map.257 = bf16[768,1728]{1,0:T(8,128)(2,1)S(1)} custom-call(s32[4]{0:T(128)S(1)} %copy-done.10, bf16[768,2304]{1,0:T(8,128)(2,1)S(1)} %copy-done.3, bf16[768,576]{1,0:T(8,128)(2,1)S(1)} %copy.97.g_ref), custom_call_target="tpu_custom_call" | custom-call | tf_op jit(solution)/shard_map/pallas_call | solution.py:106
  391.3 13.5 %shard_map.258 = bf16[768,1728]{1,0:T(8,128)(2,1)S(1)} custom-call(s32[4]{0:T(128)S(1)} %copy-done.10, bf16[768,2304]{1,0:T(8,128)(2,1)S(1)} %copy-done.1, bf16[768,576]{1,0:T(8,128)(2,1)S(1)} %copy-done.6), custom_call_target="tpu_custom_call" | custom-call | tf_op jit(solution)/shard_map/pallas_call | solution.py:106
  439.2 5.5 fusion.4
  444.8 6.3 %fusion.6 = f32[768,1152]{1,0:T(8,128)S(1)} fusion(f32[768,1152]{1,0:T(8,128)} %fusion.4, bf16[768,1728]{1,0:T(8,128)(2,1)S(1)} %copy-done.5, bf16[1152,2304]{1,0:T(8,128)(2,1)S(1)} %bitcast.352), kind=kOutput, calls=%fused_computation.48 | convolution fusion | flops 3058532352 | bytes 13959168 | tf_op jit(solution)/shard_map/dot_general | solution.py:21
  511.8 5.8 add_convert_fusion.8
  (640 shorter events, 372.6 us)
Async XLA Ops:
  7.2 40.4 %all-gather.4.cloned.1.call-start = ((), (), s32[]{:S(2)}) async-start(), calls=%async_computation.4 | async-start | bytes 1658880 | tf_op jit(solution)/shard_map/all_gather | solution.py:206
  10.3 79.6 %all-gather.6.cloned.1.call-start = ((), (), s32[]{:S(2)}) async-start(), calls=%async_computation.5 | async-start | bytes 1658880 | tf_op jit(solution)/shard_map/all_gather | solution.py:206
  11.1 115.2 %all-gather.8.cloned.1.call-start = ((), (), s32[]{:S(2)}) async-start(), calls=%async_computation.6 | async-start | bytes 1658880 | tf_op jit(solution)/shard_map/all_gather | solution.py:206
  31.2 547.5 %reduce-scatter.5.cloned.1.call-start = ((), (), s32[]{:S(2)}) async-start(), calls=%async_computation.8 | async-start | bytes 1658880 | tf_op jit(solution)/shard_map/reduce_scatter | solution.py:468
  49.2 39.1 %collective-permute-start.5 = (bf16[288,2304]{1,0:T(8,128)(2,1)}, bf16[288,2304]{1,0:T(8,128)(2,1)}, u32[]{:S(2)}, u32[]{:S(2)}) collective-permute-start(bf16[288,2304]{1,0:T(8,128)(2,1)} %all-gather.4.cloned.1.call-done), channel_id=1, source_target_pairs={{0,4},{2,6},{4,0},{6,2},{8,12},{10,14},{12,8},{14,10},{16,20},{18,... | collective-permute-start | bytes 3981320 | tf_op jit(solution)/shard_map/ppermute | solution.py:155
  94.4 31.7 %collective-permute-start.12 = (bf16[288,2304]{1,0:T(8,128)(2,1)}, bf16[288,2304]{1,0:T(8,128)(2,1)}, u32[]{:S(2)}, u32[]{:S(2)}) collective-permute-start(bf16[288,2304]{1,0:T(8,128)(2,1)} %collective-permute-done.5), channel_id=1, source_target_pairs={{0,1},{1,0},{2,3},{3,2},{4,5},{5,4},{6,7},{7,6},{8,9},{9,8},{10,11... | collective-permute-start | bytes 3981320 | tf_op jit(solution)/shard_map/ppermute | solution.py:160
  128.0 34.7 %collective-permute-start.16 = (bf16[288,2304]{1,0:T(8,128)(2,1)}, bf16[288,2304]{1,0:T(8,128)(2,1)}, u32[]{:S(2)}, u32[]{:S(2)}) collective-permute-start(bf16[288,2304]{1,0:T(8,128)(2,1)} %all-gather.6.cloned.1.call-done), channel_id=1, source_target_pairs={{0,1},{1,0},{2,3},{3,2},{4,5},{5,4},{6,7},{7,6},{8,9},{9,8},{10,11... | collective-permute-start | bytes 3981320 | tf_op jit(solution)/shard_map/ppermute | solution.py:160
  129.9 32.8 %collective-permute-start.17 = (bf16[288,2304]{1,0:T(8,128)(2,1)}, bf16[288,2304]{1,0:T(8,128)(2,1)}, u32[]{:S(2)}, u32[]{:S(2)}) collective-permute-start(bf16[288,2304]{1,0:T(8,128)(2,1)} %all-gather.8.cloned.1.call-done), channel_id=1, source_target_pairs={{0,4},{2,6},{4,0},{6,2},{8,12},{10,14},{12,8},{14,10},{16,20},{18,... | collective-permute-start | bytes 3981320 | tf_op jit(solution)/shard_map/ppermute | solution.py:155
  170.9 31.7 %collective-permute-start.20 = (bf16[288,2304]{1,0:T(8,128)(2,1)S(1)}, bf16[288,2304]{1,0:T(8,128)(2,1)S(1)}, u32[]{:S(2)}, u32[]{:S(2)}) collective-permute-start(bf16[288,2304]{1,0:T(8,128)(2,1)S(1)} %copy-done.69), channel_id=1, source_target_pairs={{0,2},{2,0},{4,6},{6,4},{8,10},{10,8},{12,14},{14,12},{16,18},{18,... | collective-permute-start | bytes 3981320 | tf_op jit(solution)/shard_map/ppermute | solution.py:155
  200.3 32.0 %collective-permute-start.26 = (bf16[288,768]{1,0:T(8,128)(2,1)}, bf16[288,768]{1,0:T(8,128)(2,1)}, u32[]{:S(2)}, u32[]{:S(2)}) collective-permute-start(bf16[288,768]{1,0:T(8,128)(2,1)} %slice.355), channel_id=1, source_target_pairs={{0,1},{1,0},{2,3},{3,2},{4,5},{5,4},{6,7},{7,6},{8,9},{9,8},{10,11... | collective-permute-start | bytes 1327112 | tf_op jit(solution)/shard_map/ppermute | solution.py:160
  301.7 51.6 %collective-permute-start.40 = (bf16[288,2304]{1,0:T(8,128)(2,1)}, bf16[288,2304]{1,0:T(8,128)(2,1)}, u32[]{:S(2)}, u32[]{:S(2)}) collective-permute-start(bf16[288,2304]{1,0:T(8,128)(2,1)} %slice.365), channel_id=1, source_target_pairs={{0,4},{2,6},{4,0},{6,2},{8,12},{10,14},{12,8},{14,10},{16,20},{18,... | collective-permute-start | bytes 3981320 | tf_op jit(solution)/shard_map/ppermute | solution.py:155
  303.2 58.7 %collective-permute-start.39 = (bf16[288,2304]{1,0:T(8,128)(2,1)}, bf16[288,2304]{1,0:T(8,128)(2,1)}, u32[]{:S(2)}, u32[]{:S(2)}) collective-permute-start(bf16[288,2304]{1,0:T(8,128)(2,1)} %slice.366), channel_id=1, source_target_pairs={{0,4},{2,6},{4,0},{6,2},{8,12},{10,14},{12,8},{14,10},{16,20},{18,... | collective-permute-start | bytes 3981320 | tf_op jit(solution)/shard_map/ppermute | solution.py:155
  307.8 56.9 %collective-permute-start.38 = (bf16[288,2304]{1,0:T(8,128)(2,1)}, bf16[288,2304]{1,0:T(8,128)(2,1)}, u32[]{:S(2)}, u32[]{:S(2)}) collective-permute-start(bf16[288,2304]{1,0:T(8,128)(2,1)} %get-tuple-element.364), channel_id=1, source_target_pairs={{0,1},{1,0},{2,3},{3,2},{4,5},{5,4},{6,7},{7,6},{8,9},{9,8},{10,11... | collective-permute-start | bytes 3981320 | tf_op jit(solution)/shard_map/ppermute | solution.py:160
  340.1 45.4 %collective-permute-start.36 = (bf16[288,2304]{1,0:T(8,128)(2,1)}, bf16[288,2304]{1,0:T(8,128)(2,1)}, u32[]{:S(2)}, u32[]{:S(2)}) collective-permute-start(bf16[288,2304]{1,0:T(8,128)(2,1)} %get-tuple-element.365), channel_id=1, source_target_pairs={{0,1},{1,0},{2,3},{3,2},{4,5},{5,4},{6,7},{7,6},{8,9},{9,8},{10,11... | collective-permute-start | bytes 3981320 | tf_op jit(solution)/shard_map/ppermute | solution.py:160
  356.6 52.7 %collective-permute-start.42 = (bf16[288,2304]{1,0:T(8,128)(2,1)}, bf16[288,2304]{1,0:T(8,128)(2,1)}, u32[]{:S(2)}, u32[]{:S(2)}) collective-permute-start(bf16[288,2304]{1,0:T(8,128)(2,1)} %add_convert_fusion.15), channel_id=1, source_target_pairs={{0,1},{1,0},{2,3},{3,2},{4,5},{5,4},{6,7},{7,6},{8,9},{9,8},{10,11... | collective-permute-start | bytes 3981320 | tf_op jit(solution)/shard_map/ppermute | solution.py:160
  366.4 41.6 %collective-permute-start.41 = (bf16[288,2304]{1,0:T(8,128)(2,1)S(1)}, bf16[288,2304]{1,0:T(8,128)(2,1)S(1)}, u32[]{:S(2)}, u32[]{:S(2)}) collective-permute-start(bf16[288,2304]{1,0:T(8,128)(2,1)S(1)} %add_convert_fusion.13), channel_id=1, source_target_pairs={{0,4},{2,6},{4,0},{6,2},{8,12},{10,14},{12,8},{14,10},{16,20},{18,... | collective-permute-start | bytes 3981320 | tf_op jit(solution)/shard_map/ppermute | solution.py:155
  412.6 166.1 %reduce-scatter.3.cloned.1.call-start = ((), (), s32[]{:S(2)}) async-start(), calls=%async_computation.7 | async-start | bytes 1658880 | tf_op jit(solution)/shard_map/reduce_scatter | solution.py:468
  422.9 49.4 %collective-permute-start.43 = (bf16[4,192,576]{2,1,0:T(8,128)(2,1)}, bf16[4,192,576]{2,1,0:T(8,128)(2,1)}, u32[]{:S(2)}, u32[]{:S(2)}) collective-permute-start(bf16[4,192,576]{2,1,0:T(8,128)(2,1)} %fusion.28), channel_id=1, source_target_pairs={{0,1},{1,0},{2,3},{3,2},{4,5},{5,4},{6,7},{7,6},{8,9},{9,8},{10,11... | collective-permute-start | bytes 2654216 | tf_op jit(solution)/shard_map/ppermute | solution.py:160
  431.1 32.6 %collective-permute-start.46 = (bf16[576,576]{1,0:T(8,128)(2,1)}, bf16[576,576]{1,0:T(8,128)(2,1)}, u32[]{:S(2)}, u32[]{:S(2)}) collective-permute-start(bf16[576,576]{1,0:T(8,128)(2,1)} %slice.378), channel_id=1, source_target_pairs={{0,1},{1,0},{2,3},{3,2},{4,5},{5,4},{6,7},{7,6},{8,9},{9,8},{10,11... | collective-permute-start | bytes 1990664 | tf_op jit(solution)/shard_map/ppermute | solution.py:160
  438.5 46.4 %collective-permute-start.50 = (bf16[288,1152]{1,0:T(8,128)(2,1)}, bf16[288,1152]{1,0:T(8,128)(2,1)}, u32[]{:S(2)}, u32[]{:S(2)}) collective-permute-start(bf16[288,1152]{1,0:T(8,128)(2,1)} %slice.380), channel_id=1, source_target_pairs={{0,4},{2,6},{4,0},{6,2},{8,12},{10,14},{12,8},{14,10},{16,20},{18,... | collective-permute-start | bytes 1990664 | tf_op jit(solution)/shard_map/ppermute | solution.py:155
  520.4 42.3 %collective-permute-start.62 = (bf16[72,2304]{1,0:T(8,128)(2,1)}, bf16[72,2304]{1,0:T(8,128)(2,1)}, u32[]{:S(2)}, u32[]{:S(2)}) collective-permute-start(bf16[72,2304]{1,0:T(8,128)(2,1)} %get-tuple-element.445), channel_id=1, source_target_pairs={{0,8},{2,10},{4,12},{6,14},{8,0},{10,2},{12,4},{14,6},{16,24},{18,... | collective-permute-start | bytes 995336 | tf_op jit(solution)/shard_map/ppermute | solution.py:591
  520.4 42.3 %collective-permute-start.61 = (bf16[72,2304]{1,0:T(8,128)(2,1)}, bf16[72,2304]{1,0:T(8,128)(2,1)}, u32[]{:S(2)}, u32[]{:S(2)}) collective-permute-start(bf16[72,2304]{1,0:T(8,128)(2,1)} %get-tuple-element.446), channel_id=1, source_target_pairs={{0,16},{2,18},{4,20},{6,22},{8,24},{10,26},{12,28},{14,30},{16,0},... | collective-permute-start | bytes 995336 | tf_op jit(solution)/shard_map/ppermute | solution.py:591
  522.3 40.4 %collective-permute-start.60 = (bf16[72,2304]{1,0:T(8,128)(2,1)}, bf16[72,2304]{1,0:T(8,128)(2,1)}, u32[]{:S(2)}, u32[]{:S(2)}) collective-permute-start(bf16[72,2304]{1,0:T(8,128)(2,1)} %get-tuple-element.447), channel_id=1, source_target_pairs={{0,24},{2,26},{4,28},{6,30},{8,16},{10,18},{12,20},{14,22},{16,8},... | collective-permute-start | bytes 995336 | tf_op jit(solution)/shard_map/ppermute | solution.py:591
  527.5 41.1 %collective-permute-start.64 = (bf16[4,192,576]{2,1,0:T(8,128)(2,1)}, bf16[4,192,576]{2,1,0:T(8,128)(2,1)}, u32[]{:S(2)}, u32[]{:S(2)}) collective-permute-start(bf16[4,192,576]{2,1,0:T(8,128)(2,1)} %bitcast.96), channel_id=1, source_target_pairs={{0,1},{1,0},{2,3},{3,2},{4,5},{5,4},{6,7},{7,6},{8,9},{9,8},{10,11... | collective-permute-start | bytes 2654216 | tf_op jit(solution)/shard_map/ppermute | solution.py:160
  (177 other events, 2896.3 us)
Sparse Core Ops, SparseCore 0:
  10.4 36.4 all-gather.3
  48.5 41.3 all-gather.5
  91.5 31.7 all-gather.7
  412.7 29.1 reduce-scatter.4
  444.1 30.4 reduce-scatter.2

commit v4 on v3

--- a/solution.py
+++ b/solution.py
@@ -542,8 +542,6 @@
     out_x_got = [over_mp(out_y[:, s * own : (s + 1) * own], s) for s in shifts[1:]]
     qk_y[last] = step(y_add(qk_kept[last], step(qk_y_got[last])))
     qk_x_got = {last: over_mp(qk_y[last], last)} if last else {}
-    v_x = step(x_add(v_kept, [step(v) for v in v_x_got.values()]))
-    v_y_got = y_send(v_x)
     grad_first = cubes(step(grad_first))
     grad_shift_one = jnp.sum(grad_first, axis=1)
     grad_scale_one = jnp.sum(grad_first * normed_one, axis=1)
@@ -560,8 +558,10 @@
         ],
         axis=1,
     ).astype(BF)
+    grad_mod = step(grad_mod.reshape(mine * 6, full))
+    v_x = step(x_add(v_kept, [step(v) for v in v_x_got.values()]))
+    v_y_got = y_send(v_x)
     fresh_got = later(fresh_got)
-    grad_mod = step(grad_mod.reshape(mine * 6, full))
     mod_back = [
         over_mp(dot(grad_mod, p, NT, BF).reshape(mine, 6 * own), s)
         for s, p in enumerate(spreads)
@@ -643,7 +643,7 @@
     for v in bias_gots:
         bias_own = bias_own + step(v)
     bias_got = over_dp(bias_own, 1)
-    output = jnp.where(taken, put(fresh_got), inputs.astype(F32)).astype(BF)
+    output = jnp.where(taken, put([step(v) for v in fresh_got]), inputs.astype(F32)).astype(BF)
     output = step(output)
     bias_own = step(bias_own + bias_got)
     bias_got = over_dp(bias_own, 0)

time: 598 us -> 617 us (1.032)
  waiting for transfers between devices: 63.9 us -> 83.5 us
    ppermute x20, waiting for transfers between devices: 28.5 us -> 48.4 us  [over_mp(): return lax.ppermute(step(v), 'mp', [(i, i ^ s) for i in range(nm)])]
    unnamed x262 -> x258, local copies, waits for them, and re-layouts: 18.4 us -> 19.7 us
  transfers between devices with their start and end apart: 77 -> 77, of which waited for: 14 -> 15; matrix products, arithmetic and copies ran while one was open for 59% -> 56% of each run, Pallas kernels for 9% -> 8%
where the time goes in v4:
time: 617 us; the launch traced here: 612 us
  matrix products  215 us (35%)
  other arithmetic  105 us (17%)
  waiting for transfers between devices  83.5 us (14%)
  starting transfers between devices  70 us (11%)
  local copies, waits for them, and re-layouts  67.8 us (11%)
  Pallas kernels  51.2 us (8%)
  between operations  19 us (3%)
    dot_general x54, matrix products, dot(): lax.dot_general(left, right, (dims, ((), ())), preferred_element_type=kind)  199 us
    ppermute x20, waiting for transfers between devices, over_mp(): return lax.ppermute(step(v), 'mp', [(i, i ^ s) for i in range(nm)])  48.4 us
    pallas_call x2, Pallas kernels, attend_back(): pl.pallas_call(partial(attend_back_kernel, own // HD), out_shape=jax.Shap...  26.9 us
    pallas_call x2, Pallas kernels, attend(): pl.pallas_call(partial(attend_kernel, own // HD), out_shape=jax.ShapeDtyp...  24.3 us
    another operation x8, other arithmetic, join(): jnp.stack([first[0], second[0], first[1], second[1]]).reshape(full, -1)  23.1 us
    ppermute x38, waiting for transfers between devices, over_dp(): return lax.ppermute(step(v), 'dp', [(i, i ^ 1 << bit) for i in range(nd)])  21.7 us
    ppermute x20, starting transfers between devices, over_mp(): return lax.ppermute(step(v), 'mp', [(i, i ^ s) for i in range(nm)])  21.5 us
    ppermute x38, starting transfers between devices, over_dp(): return lax.ppermute(step(v), 'dp', [(i, i ^ 1 << bit) for i in range(nd)])  20.3 us
  transfers between devices with their start and end apart: 77, of which 15 were waited for; matrix products, arithmetic and copies ran while one was open for 56% of the time, Pallas kernels for 8%

profile of v4, /device:TPU:0, one launch (start us, length us, event | category | flops | bytes accessed | tf_op | source)
XLA Modules:
  0.0 611.7 jit_solution(6543432268450001633)
XLA Ops:
  24.8 6.4 %all-to-all-start = ((bf16[16,8,80]{2,1,0:T(8,128)(2,1)}), bf16[16,8,80]{2,1,0:T(8,128)(2,1)S(1)}, u32[]{:S(2)}, u32[]{:S(2)}) async-start(bf16[16,8,80]{2,1,0:T(8,128)(2,1)} %copy.92), calls=%async_computation | async-start | bytes 65536 | tf_op jit(solution)/shard_map/all_to_all | solution.py:251
  50.9 5.6 convolution_add_fusion.1
  68.2 10.8 %collective-permute-done.6 = bf16[288,2304]{1,0:T(8,128)(2,1)S(1)} collective-permute-done((bf16[288,2304]{1,0:T(8,128)(2,1)}, bf16[288,2304]{1,0:T(8,128)(2,1)S(1)}, u32[]{:S(2)}, u32[]{:S(2)}) %collective-permute-start.6) | collective-permute-done | bytes 1327136 | tf_op jit(solution)/shard_map/ppermute | solution.py:160
  79.0 9.3 %collective-permute-done.5 = bf16[288,2304]{1,0:T(8,128)(2,1)} collective-permute-done((bf16[288,2304]{1,0:T(8,128)(2,1)}, bf16[288,2304]{1,0:T(8,128)(2,1)}, u32[]{:S(2)}, u32[]{:S(2)}) %collective-permute-start.5) | collective-permute-done | bytes 1327136 | tf_op jit(solution)/shard_map/ppermute | solution.py:155
  112.3 12.0 %shard_map.255 = bf16[768,576]{1,0:T(8,128)(2,1)S(1)} custom-call(s32[4]{0:T(128)S(1)} %dynamic_slice.79.counts, bf16[768,2304]{1,0:T(8,128)(2,1)S(1)} %add_convert_fusion.1.qkv_ref), custom_call_target="tpu_custom_call" | custom-call | tf_op jit(solution)/shard_map/pallas_call | solution.py:87
  142.9 12.3 %shard_map.256 = bf16[768,576]{1,0:T(8,128)(2,1)S(1)} custom-call(s32[4]{0:T(128)S(1)} %dynamic_slice.79.counts, bf16[768,2304]{1,0:T(8,128)(2,1)S(1)} %add_convert_fusion.qkv_ref), custom_call_target="tpu_custom_call" | custom-call | tf_op jit(solution)/shard_map/pallas_call | solution.py:87
  174.9 10.3 %multiply_add_fusion.1 = (f32[768,2304]{1,0:T(8,128)}, bf16[768,2304]{1,0:T(8,128)(2,1)}) fusion(f32[2304]{0:T(1024)S(1)} %convert_element_type.299, bf16[768,1152]{1,0:T(8,128)(2,1)S(1)} %fusion.15, bf16[1152,2304]{1,0:T(8,128)(2,1)S(1)} %bitcast.354), kind=kOutput, calls=%fused_computation.6 | convolution fusion | flops 4110483456 | bytes 17703936 | tf_op jit(solution)/shard_map/dot_general | solution.py:21
  185.2 8.7 %collective-permute-done.23 = bf16[288,2304]{1,0:T(8,128)(2,1)S(1)} collective-permute-done((bf16[288,2304]{1,0:T(8,128)(2,1)}, bf16[288,2304]{1,0:T(8,128)(2,1)S(1)}, u32[]{:S(2)}, u32[]{:S(2)}) %collective-permute-start.23) | collective-permute-done | bytes 1327136 | tf_op jit(solution)/shard_map/ppermute | solution.py:160
  207.9 10.2 %convolution_add_fusion.6 = f32[768,1152]{1,0:T(8,128)} fusion(bf16[768,2304]{1,0:T(8,128)(2,1)} %get-tuple-element.319, bf16[1152,2304]{1,0:T(8,128)(2,1)} %bitcast.360, f32[1152]{0:T(1024)S(1)} %get-tuple-element.563), kind=kOutput, calls=%fused_computation.51 | convolution fusion | flops 4077748224 | bytes 12390912 | tf_op jit(solution)/shard_map/dot_general | solution.py:21
  221.9 10.4 %multiply_add_fusion = (f32[768,2304]{1,0:T(8,128)}, bf16[768,2304]{1,0:T(8,128)(2,1)}) fusion(f32[2304]{0:T(1024)S(1)} %reshape.435, bf16[768,1152]{1,0:T(8,128)(2,1)S(1)} %copy-done.46, bf16[1152,2304]{1,0:T(8,128)(2,1)S(1)} %bitcast.358), kind=kOutput, calls=%fused_computation.2 | convolution fusion | flops 4110483456 | bytes 17703936 | tf_op jit(solution)/shard_map/dot_general | solution.py:21
  248.7 8.1 %convolution_add_fusion.5 = f32[768,1152]{1,0:T(8,128)} fusion(f32[768,1152]{1,0:T(8,128)} %convolution_add_fusion.6, bf16[768,2304]{1,0:T(8,128)(2,1)S(1)} %copy-done.57, bf16[1152,2304]{1,0:T(8,128)(2,1)S(1)} %bitcast.364), kind=kOutput, calls=%fused_computation.50 | convolution fusion | flops 4077748224 | bytes 15925248 | tf_op jit(solution)/shard_map/dot_general | solution.py:21
  266.5 8.7 %multiply_convert_fusion.1 = bf16[768,2304]{1,0:T(8,128)(2,1)S(1)} fusion(f32[768,2304]{1,0:T(8,128)} %get-tuple-element.334, bf16[768,1152]{1,0:T(8,128)(2,1)S(1)} %get-tuple-element.462, bf16[1152,2304]{1,0:T(8,128)(2,1)} %bitcast.365), kind=kOutput, calls=%fused_computation.1 | convolution fusion | flops 4080402432 | bytes 17694720 | tf_op jit(solution)/shard_map/dot_general | solution.py:21
  283.2 7.5 %multiply_convert_fusion = bf16[768,2304]{1,0:T(8,128)(2,1)S(1)} fusion(f32[768,2304]{1,0:T(8,128)} %get-tuple-element.320, bf16[768,1152]{1,0:T(8,128)(2,1)S(1)} %get-tuple-element.462, bf16[1152,2304]{1,0:T(8,128)(2,1)S(1)} %bitcast.363), kind=kOutput, calls=%fused_computation | convolution fusion | flops 4080402432 | bytes 17694720 | tf_op jit(solution)/shard_map/dot_general | solution.py:21
  290.7 5.3 add_convert_fusion.4
  314.8 6.8 %fusion.168 = f32[768,1152]{1,0:T(8,128)} fusion(bf16[768,2304]{1,0:T(8,128)(2,1)S(1)} %multiply_convert_fusion, bf16[1152,2304]{1,0:T(8,128)(2,1)S(1)} %bitcast.357), kind=kOutput, calls=%fused_computation.380 | convolution fusion | flops 4076863488 | bytes 12386304 | tf_op jit(solution)/shard_map/dot_general | solution.py:21
  321.6 8.5 %convolution_add_fusion.4 = f32[768,1152]{1,0:T(8,128)S(1)} fusion(f32[768,1152]{1,0:T(8,128)} %fusion.168, bf16[768,2304]{1,0:T(8,128)(2,1)S(1)} %multiply_convert_fusion.1, bf16[1152,2304]{1,0:T(8,128)(2,1)} %bitcast.359), kind=kOutput, calls=%fused_computation.49 | convolution fusion | flops 4077748224 | bytes 15925248 | tf_op jit(solution)/shard_map/dot_general | solution.py:21
  374.5 13.5 %shard_map.257 = bf16[768,1728]{1,0:T(8,128)(2,1)S(1)} custom-call(s32[4]{0:T(128)S(1)} %copy-done.10, bf16[768,2304]{1,0:T(8,128)(2,1)S(1)} %copy-done.3, bf16[768,576]{1,0:T(8,128)(2,1)S(1)} %copy.97.g_ref), custom_call_target="tpu_custom_call" | custom-call | tf_op jit(solution)/shard_map/pallas_call | solution.py:106
  393.9 13.5 %shard_map.258 = bf16[768,1728]{1,0:T(8,128)(2,1)S(1)} custom-call(s32[4]{0:T(128)S(1)} %copy-done.10, bf16[768,2304]{1,0:T(8,128)(2,1)S(1)} %copy-done.1, bf16[768,576]{1,0:T(8,128)(2,1)S(1)} %copy-done.6), custom_call_target="tpu_custom_call" | custom-call | tf_op jit(solution)/shard_map/pallas_call | solution.py:106
  441.1 5.6 fusion.4
  446.7 7.5 %fusion.6 = f32[768,1152]{1,0:T(8,128)S(1)} fusion(f32[768,1152]{1,0:T(8,128)} %fusion.4, bf16[768,1728]{1,0:T(8,128)(2,1)S(1)} %copy-done.5, bf16[1152,2304]{1,0:T(8,128)(2,1)} %bitcast.347), kind=kOutput, calls=%fused_computation.48 | convolution fusion | flops 3058532352 | bytes 13860864 | tf_op jit(solution)/shard_map/dot_general | solution.py:21
  480.5 7.0 %collective-permute-done.51 = bf16[288,576]{1,0:T(8,128)(2,1)} collective-permute-done((bf16[288,576]{1,0:T(8,128)(2,1)}, bf16[288,576]{1,0:T(8,128)(2,1)}, u32[]{:S(2)}, u32[]{:S(2)}) %collective-permute-start.51) | collective-permute-done | bytes 331808 | tf_op jit(solution)/shard_map/ppermute | solution.py:160
  513.8 5.8 add_convert_fusion.8
  550.6 6.3 %all-to-all-done.1 = f32[16,8,72]{2,1,0:T(8,128)S(1)} async-done(((f32[16,8,72]{2,1,0:T(8,128)}), f32[16,8,72]{2,1,0:T(8,128)S(1)}, u32[]{:S(2)}, u32[]{:S(2)}) %all-to-all-start.1) | async-done | bytes 36896 | tf_op jit(solution)/shard_map/all_to_all | solution.py:604
  569.6 14.6 %collective-permute-done.64 = bf16[4,192,576]{2,1,0:T(8,128)(2,1)S(1)} collective-permute-done((bf16[4,192,576]{2,1,0:T(8,128)(2,1)}, bf16[4,192,576]{2,1,0:T(8,128)(2,1)S(1)}, u32[]{:S(2)}, u32[]{:S(2)}) %collective-permute-start.64) | collective-permute-done | bytes 884768 | tf_op jit(solution)/shard_map/ppermute | solution.py:160
  (635 shorter events, 378.1 us)
Async XLA Ops:
  7.2 40.4 %all-gather.4.cloned.1.call-start = ((), (), s32[]{:S(2)}) async-start(), calls=%async_computation.4 | async-start | bytes 1658880 | tf_op jit(solution)/shard_map/all_gather | solution.py:206
  10.3 79.6 %all-gather.6.cloned.1.call-start = ((), (), s32[]{:S(2)}) async-start(), calls=%async_computation.5 | async-start | bytes 1658880 | tf_op jit(solution)/shard_map/all_gather | solution.py:206
  11.1 115.2 %all-gather.8.cloned.1.call-start = ((), (), s32[]{:S(2)}) async-start(), calls=%async_computation.6 | async-start | bytes 1658880 | tf_op jit(solution)/shard_map/all_gather | solution.py:206
  31.2 565.9 %reduce-scatter.5.cloned.1.call-start = ((), (), s32[]{:S(2)}) async-start(), calls=%async_computation.8 | async-start | bytes 1658880 | tf_op jit(solution)/shard_map/reduce_scatter | solution.py:468
  47.5 31.5 %collective-permute-start.6 = (bf16[288,2304]{1,0:T(8,128)(2,1)}, bf16[288,2304]{1,0:T(8,128)(2,1)S(1)}, u32[]{:S(2)}, u32[]{:S(2)}) collective-permute-start(bf16[288,2304]{1,0:T(8,128)(2,1)} %all-gather.4.cloned.1.call-done), channel_id=1, source_target_pairs={{0,1},{1,0},{2,3},{3,2},{4,5},{5,4},{6,7},{7,6},{8,9},{9,8},{10,11... | collective-permute-start | bytes 3981320 | tf_op jit(solution)/shard_map/ppermute | solution.py:160
  49.2 39.1 %collective-permute-start.5 = (bf16[288,2304]{1,0:T(8,128)(2,1)}, bf16[288,2304]{1,0:T(8,128)(2,1)}, u32[]{:S(2)}, u32[]{:S(2)}) collective-permute-start(bf16[288,2304]{1,0:T(8,128)(2,1)} %all-gather.4.cloned.1.call-done), channel_id=1, source_target_pairs={{0,4},{2,6},{4,0},{6,2},{8,12},{10,14},{12,8},{14,10},{16,20},{18,... | collective-permute-start | bytes 3981320 | tf_op jit(solution)/shard_map/ppermute | solution.py:155
  94.4 31.7 %collective-permute-start.12 = (bf16[288,2304]{1,0:T(8,128)(2,1)}, bf16[288,2304]{1,0:T(8,128)(2,1)}, u32[]{:S(2)}, u32[]{:S(2)}) collective-permute-start(bf16[288,2304]{1,0:T(8,128)(2,1)} %collective-permute-done.5), channel_id=1, source_target_pairs={{0,1},{1,0},{2,3},{3,2},{4,5},{5,4},{6,7},{7,6},{8,9},{9,8},{10,11... | collective-permute-start | bytes 3981320 | tf_op jit(solution)/shard_map/ppermute | solution.py:160
  128.0 34.6 %collective-permute-start.16 = (bf16[288,2304]{1,0:T(8,128)(2,1)}, bf16[288,2304]{1,0:T(8,128)(2,1)}, u32[]{:S(2)}, u32[]{:S(2)}) collective-permute-start(bf16[288,2304]{1,0:T(8,128)(2,1)} %all-gather.6.cloned.1.call-done), channel_id=1, source_target_pairs={{0,1},{1,0},{2,3},{3,2},{4,5},{5,4},{6,7},{7,6},{8,9},{9,8},{10,11... | collective-permute-start | bytes 3981320 | tf_op jit(solution)/shard_map/ppermute | solution.py:160
  129.9 32.8 %collective-permute-start.17 = (bf16[288,2304]{1,0:T(8,128)(2,1)}, bf16[288,2304]{1,0:T(8,128)(2,1)}, u32[]{:S(2)}, u32[]{:S(2)}) collective-permute-start(bf16[288,2304]{1,0:T(8,128)(2,1)} %all-gather.8.cloned.1.call-done), channel_id=1, source_target_pairs={{0,4},{2,6},{4,0},{6,2},{8,12},{10,14},{12,8},{14,10},{16,20},{18,... | collective-permute-start | bytes 3981320 | tf_op jit(solution)/shard_map/ppermute | solution.py:155
  162.6 31.3 %collective-permute-start.23 = (bf16[288,2304]{1,0:T(8,128)(2,1)}, bf16[288,2304]{1,0:T(8,128)(2,1)S(1)}, u32[]{:S(2)}, u32[]{:S(2)}) collective-permute-start(bf16[288,2304]{1,0:T(8,128)(2,1)} %all-gather.8.cloned.1.call-done), channel_id=1, source_target_pairs={{0,1},{1,0},{2,3},{3,2},{4,5},{5,4},{6,7},{7,6},{8,9},{9,8},{10,11... | collective-permute-start | bytes 3981320 | tf_op jit(solution)/shard_map/ppermute | solution.py:160
  170.9 31.7 %collective-permute-start.20 = (bf16[288,2304]{1,0:T(8,128)(2,1)S(1)}, bf16[288,2304]{1,0:T(8,128)(2,1)S(1)}, u32[]{:S(2)}, u32[]{:S(2)}) collective-permute-start(bf16[288,2304]{1,0:T(8,128)(2,1)S(1)} %copy-done.70), channel_id=1, source_target_pairs={{0,2},{2,0},{4,6},{6,4},{8,10},{10,8},{12,14},{14,12},{16,18},{18,... | collective-permute-start | bytes 3981320 | tf_op jit(solution)/shard_map/ppermute | solution.py:155
  200.3 32.0 %collective-permute-start.26 = (bf16[288,768]{1,0:T(8,128)(2,1)}, bf16[288,768]{1,0:T(8,128)(2,1)}, u32[]{:S(2)}, u32[]{:S(2)}) collective-permute-start(bf16[288,768]{1,0:T(8,128)(2,1)} %slice.355), channel_id=1, source_target_pairs={{0,1},{1,0},{2,3},{3,2},{4,5},{5,4},{6,7},{7,6},{8,9},{9,8},{10,11... | collective-permute-start | bytes 1327112 | tf_op jit(solution)/shard_map/ppermute | solution.py:160
  304.3 51.7 %collective-permute-start.39 = (bf16[288,2304]{1,0:T(8,128)(2,1)}, bf16[288,2304]{1,0:T(8,128)(2,1)}, u32[]{:S(2)}, u32[]{:S(2)}) collective-permute-start(bf16[288,2304]{1,0:T(8,128)(2,1)} %slice.363), channel_id=1, source_target_pairs={{0,4},{2,6},{4,0},{6,2},{8,12},{10,14},{12,8},{14,10},{16,20},{18,... | collective-permute-start | bytes 3981320 | tf_op jit(solution)/shard_map/ppermute | solution.py:155
  305.8 58.7 %collective-permute-start.38 = (bf16[288,2304]{1,0:T(8,128)(2,1)}, bf16[288,2304]{1,0:T(8,128)(2,1)}, u32[]{:S(2)}, u32[]{:S(2)}) collective-permute-start(bf16[288,2304]{1,0:T(8,128)(2,1)} %slice.366), channel_id=1, source_target_pairs={{0,4},{2,6},{4,0},{6,2},{8,12},{10,14},{12,8},{14,10},{16,20},{18,... | collective-permute-start | bytes 3981320 | tf_op jit(solution)/shard_map/ppermute | solution.py:155
  310.5 56.7 %collective-permute-start.37 = (bf16[288,2304]{1,0:T(8,128)(2,1)}, bf16[288,2304]{1,0:T(8,128)(2,1)}, u32[]{:S(2)}, u32[]{:S(2)}) collective-permute-start(bf16[288,2304]{1,0:T(8,128)(2,1)} %get-tuple-element.366), channel_id=1, source_target_pairs={{0,1},{1,0},{2,3},{3,2},{4,5},{5,4},{6,7},{7,6},{8,9},{9,8},{10,11... | collective-permute-start | bytes 3981320 | tf_op jit(solution)/shard_map/ppermute | solution.py:160
  342.9 45.2 %collective-permute-start.40 = (bf16[288,2304]{1,0:T(8,128)(2,1)}, bf16[288,2304]{1,0:T(8,128)(2,1)}, u32[]{:S(2)}, u32[]{:S(2)}) collective-permute-start(bf16[288,2304]{1,0:T(8,128)(2,1)} %get-tuple-element.367), channel_id=1, source_target_pairs={{0,1},{1,0},{2,3},{3,2},{4,5},{5,4},{6,7},{7,6},{8,9},{9,8},{10,11... | collective-permute-start | bytes 3981320 | tf_op jit(solution)/shard_map/ppermute | solution.py:160
  359.4 52.6 %collective-permute-start.44 = (bf16[288,2304]{1,0:T(8,128)(2,1)}, bf16[288,2304]{1,0:T(8,128)(2,1)}, u32[]{:S(2)}, u32[]{:S(2)}) collective-permute-start(bf16[288,2304]{1,0:T(8,128)(2,1)} %add_convert_fusion.15), channel_id=1, source_target_pairs={{0,1},{1,0},{2,3},{3,2},{4,5},{5,4},{6,7},{7,6},{8,9},{9,8},{10,11... | collective-permute-start | bytes 3981320 | tf_op jit(solution)/shard_map/ppermute | solution.py:160
  368.9 41.6 %collective-permute-start.41 = (bf16[288,2304]{1,0:T(8,128)(2,1)S(1)}, bf16[288,2304]{1,0:T(8,128)(2,1)S(1)}, u32[]{:S(2)}, u32[]{:S(2)}) collective-permute-start(bf16[288,2304]{1,0:T(8,128)(2,1)S(1)} %add_convert_fusion.13), channel_id=1, source_target_pairs={{0,4},{2,6},{4,0},{6,2},{8,12},{10,14},{12,8},{14,10},{16,20},{18,... | collective-permute-start | bytes 3981320 | tf_op jit(solution)/shard_map/ppermute | solution.py:155
  415.1 181.9 %reduce-scatter.3.cloned.1.call-start = ((), (), s32[]{:S(2)}) async-start(), calls=%async_computation.7 | async-start | bytes 1658880 | tf_op jit(solution)/shard_map/reduce_scatter | solution.py:468
  425.5 47.3 %collective-permute-start.47 = (bf16[4,192,576]{2,1,0:T(8,128)(2,1)}, bf16[4,192,576]{2,1,0:T(8,128)(2,1)}, u32[]{:S(2)}, u32[]{:S(2)}) collective-permute-start(bf16[4,192,576]{2,1,0:T(8,128)(2,1)} %fusion.28), channel_id=1, source_target_pairs={{0,1},{1,0},{2,3},{3,2},{4,5},{5,4},{6,7},{7,6},{8,9},{9,8},{10,11... | collective-permute-start | bytes 2654216 | tf_op jit(solution)/shard_map/ppermute | solution.py:160
  433.7 34.5 %collective-permute-start.48 = (bf16[576,576]{1,0:T(8,128)(2,1)}, bf16[576,576]{1,0:T(8,128)(2,1)}, u32[]{:S(2)}, u32[]{:S(2)}) collective-permute-start(bf16[576,576]{1,0:T(8,128)(2,1)} %slice.378), channel_id=1, source_target_pairs={{0,1},{1,0},{2,3},{3,2},{4,5},{5,4},{6,7},{7,6},{8,9},{9,8},{10,11... | collective-permute-start | bytes 1990664 | tf_op jit(solution)/shard_map/ppermute | solution.py:160
  522.4 40.6 %collective-permute-start.62 = (bf16[72,2304]{1,0:T(8,128)(2,1)}, bf16[72,2304]{1,0:T(8,128)(2,1)}, u32[]{:S(2)}, u32[]{:S(2)}) collective-permute-start(bf16[72,2304]{1,0:T(8,128)(2,1)} %get-tuple-element.447), channel_id=1, source_target_pairs={{0,8},{2,10},{4,12},{6,14},{8,0},{10,2},{12,4},{14,6},{16,24},{18,... | collective-permute-start | bytes 995336 | tf_op jit(solution)/shard_map/ppermute | solution.py:591
  522.4 40.6 %collective-permute-start.61 = (bf16[72,2304]{1,0:T(8,128)(2,1)}, bf16[72,2304]{1,0:T(8,128)(2,1)}, u32[]{:S(2)}, u32[]{:S(2)}) collective-permute-start(bf16[72,2304]{1,0:T(8,128)(2,1)} %get-tuple-element.448), channel_id=1, source_target_pairs={{0,16},{2,18},{4,20},{6,22},{8,24},{10,26},{12,28},{14,30},{16,0},... | collective-permute-start | bytes 995336 | tf_op jit(solution)/shard_map/ppermute | solution.py:591
  524.3 38.7 %collective-permute-start.60 = (bf16[72,2304]{1,0:T(8,128)(2,1)}, bf16[72,2304]{1,0:T(8,128)(2,1)}, u32[]{:S(2)}, u32[]{:S(2)}) collective-permute-start(bf16[72,2304]{1,0:T(8,128)(2,1)} %get-tuple-element.449), channel_id=1, source_target_pairs={{0,24},{2,26},{4,28},{6,30},{8,16},{10,18},{12,20},{14,22},{16,8},... | collective-permute-start | bytes 995336 | tf_op jit(solution)/shard_map/ppermute | solution.py:591
  (175 other events, 2966.9 us)
Sparse Core Ops, SparseCore 0:
  10.4 36.4 all-gather.3
  48.5 41.3 all-gather.5
  91.5 31.7 all-gather.7
  415.3 29.2 reduce-scatter.4
  446.7 30.4 reduce-scatter.2
